TPU v7x, 256 devices: a whole 4x4x8 slice. The times are simulated.
256 devices in a mesh: rows: 64 (over y, z, core), feat: 4 (over x).
Axes of the slice: x: 4, y: 4, z: 8, core: 2. Of those that a mesh axis runs over, the one named last changes fastest.
Arguments:
- embeddings: bfloat16 [131072, 1024], P('rows', 'feat'), may hold values from -8 to 8
- parent_ids: int32 [131072, 1], P('rows'), may hold values from 0 to 63; in each aligned block of 2048 rows (0 to 2047, 2048 to 4095, ...) at most 64 rows name the same one
- child_assignment: int32 [131072], P('rows'), may hold values from 0 to 63
Outputs:
- centroids: bfloat16 [4096, 1024], P('rows', 'feat')
- row_fit: float32 [131072], P('rows')
Inputs may be any that keep to these rules, and one draw needn't show every extreme that they name: `parent_ids`: in the rows of one index of rows, at most 64 rows name any one parent, a bound that some block reaches.
All inputs are finite; a program needn't handle non-finite values.
Results may differ from a plain program's by a relative error of at most 0.011.
Values may be sent and summed in bfloat16 or wider, within the bound.
No kernel may reach another device: no remote copies, remote signals or barrier semaphores. Data moves between devices by JAX's collectives and lax.ppermute only.
A program may use at most 64 MiB of HBM per device.

v0:
```python
import jax
import jax.numpy as jnp
from jax import lax
from jax.sharding import PartitionSpec as P

D = 1024
K = 64


epsilon = 1e-06


def normalize(totals):
    squares = jnp.sum(totals * totals, axis=1)
    square_sum = lax.psum(squares, "feat")
    return (totals * lax.rsqrt(square_sum / D + epsilon)[:, None]).astype(jnp.bfloat16)


def body(embeddings, parent_ids, child_assignment):
    parents = lax.axis_size("rows")
    row_count = embeddings.shape[0]
    feature_width = embeddings.shape[1]
    parent = parent_ids[:, 0]
    capacity = 2 * row_count // parents
    parent_table = (parent[:, None] == jnp.arange(parents, dtype=jnp.int32)[None, :]).astype(
        jnp.int32
    )
    ranking = jnp.sum((jnp.cumsum(parent_table, axis=0) - 1) * parent_table, axis=1)
    outgoing = (
        jnp.zeros((parents, capacity, feature_width), embeddings.dtype)
        .at[parent, ranking]
        .set(embeddings)
    )
    labels = jnp.full((parents, capacity), -1, jnp.int32).at[parent, ranking].set(child_assignment)
    slot_rows = outgoing
    members = (labels[:, :, None] == jnp.arange(K, dtype=jnp.int32)[None, None, :]).astype(
        embeddings.dtype
    )
    block = jnp.einsum("pck,pcd->pkd", members, slot_rows, preferred_element_type=jnp.float32)
    totals = lax.psum_scatter(
        block.reshape(lax.axis_size("rows") * K, feature_width),
        "rows",
        scatter_dimension=0,
        tiled=True,
    )
    centroids = normalize(totals)
    shard_piece = lax.all_gather(centroids, "rows", axis=0, tiled=True)
    parent_span = shard_piece.shape[0] // K
    slot_rows = outgoing
    centre_part = shard_piece.reshape(parent_span, K, feature_width)
    inner_products = jnp.einsum(
        "pcd,pkd->pck", slot_rows, centre_part, preferred_element_type=jnp.float32
    )
    distance_scores = lax.psum(inner_products.astype(jnp.bfloat16), "feat").astype(jnp.float32)
    slot_fits = jnp.max(distance_scores, axis=2) / (0.25 * D)
    row_fit = slot_fits[parent, ranking]
    return (centroids, row_fit)


def solution(mesh):
    in_specs = (P("rows", "feat"), P("rows", None), P("rows"))
    out_specs = (P("rows", "feat"), P("rows"))
    return jax.shard_map(body, mesh=mesh, in_specs=in_specs, out_specs=out_specs, check_vma=False)
```

profile of v0, /device:TPU:8, one launch (start us, length us, event | category | flops | bytes accessed | tf_op | source)
XLA Modules:
  0.0 365.3 jit_solution(16139832244403144530)
XLA Ops:
  7.2 0.0 reduce-scatter.2.cloned.1.call-start
  7.2 0.0 copy-start
  7.2 0.8 fusion.6
  8.0 0.0 copy-start.1
  8.0 18.1 %reduce-window.6 = s32[64,16,128]{2,1,0:T(8,128)S(1)} reduce-window(s32[64,16,128]{2,1,0:T(8,128)S(1)} %fusion.6, s32[]{:T(128)} %constant.10.clone.1), window={size=1x1x128 pad=0_0x0_0x127_0}, to_apply=%region_0.0 | reduce-window | flops 16646144 | bytes 1048580 | tf_op jit(solution)/shard_map/reduce-window
  26.2 0.2 slice.10
  26.4 0.4 copy.7
  26.8 0.2 reduce-window.9
  27.0 0.2 add_add_fusion
  27.2 0.0 copy-done
  27.2 0.2 fusion.5
  27.5 0.1 and_reduce_fusion
  27.5 0.0 copy-done.1
  27.5 0.1 multiply_reduce_fusion.1
  27.6 8.2 %scatter_custom_fusion = s32[4096]{0:T(1024)S(1)} fusion(s32[2048]{0:T(1024)S(1)} %broadcast_select_fusion, s32[2048]{0:T(1024)} %param.5, s32[]{:T(128)} %constant.9.clone.1), kind=kCustom, calls=%fused_computation.25 | custom fusion | bytes 16896
  35.9 0.1 reshape.49
  35.9 10.4 %scatter_custom_fusion.1 = bf16[4096,256]{1,0:T(8,128)(2,1)S(1)} fusion(s32[2048]{0:T(1024)S(1)} %broadcast_select_fusion, bf16[2048,256]{1,0:T(8,128)(2,1)} %param.3, bf16[]{:T(256)} %constant.7.clone.1), kind=kCustom, calls=%fused_computation.6 | custom fusion | bytes 2097664
  46.3 2.6 fusion
  48.9 0.0 reduce-scatter.2.cloned.1.call-update
  48.9 0.0 all-gather.2.cloned.1.call-start
  49.0 145.9 %reduce-scatter.2.cloned.1.call-done = f32[64,256]{1,0:T(8,128)} async-done(((f32[4096,256]{1,0:T(8,128)}), f32[64,256]{1,0:T(8,128)}) %reduce-scatter.2.cloned.1.call-update) | async-done | bytes 65552 | tf_op jit(solution)/shard_map/reduce_scatter | solution.py:40
  194.9 0.9 multiply_reduce_fusion
  195.9 10.5 %psum.14 = f32[64]{0:T(128)S(1)} all-reduce(f32[64]{0:T(128)S(1)} %multiply_reduce_fusion), channel_id=1, replica_groups=mesh['rows'=64,'feat'=4] {'feat'}, use_global_device_ids=true, to_apply=%region_7.8 | all-reduce | flops 64 | bytes 512 | tf_op jit(solution)/shard_map/psum | solution.py:15
  206.4 1.5 multiply_convert_fusion
  207.9 0.0 all-gather.2.cloned.1.call-update
  207.9 0.0 all-reduce.2.cloned.1.call-start
  208.0 73.5 %all-gather.2.cloned.1.call-done = bf16[4096,256]{1,0:T(8,128)(2,1)} async-done(((bf16[64,256]{1,0:T(8,128)(2,1)}), bf16[4096,256]{1,0:T(8,128)(2,1)}) %all-gather.2.cloned.1.call-update) | async-done | bytes 2097168 | tf_op jit(solution)/shard_map/all_gather | solution.py:47
  281.4 3.3 convolution_convert_fusion
  284.7 0.0 all-reduce.2.cloned.1.call-update
  284.8 49.7 %all-reduce.2.cloned.1.call-done = bf16[64,64,64]{2,1,0:T(8,128)(2,1)} async-done(((bf16[64,64,64]{2,1,0:T(8,128)(2,1)}), bf16[64,64,64]{2,1,0:T(8,128)(2,1)}) %all-reduce.2.cloned.1.call-update) | async-done | bytes 524304 | tf_op jit(solution)/shard_map/psum | solution.py:54
  334.5 1.8 reduce_max.14
  336.3 22.4 %gather_fusion = f32[2048]{0:T(1024)} fusion(f32[64,64]{1,0:T(8,128)S(1)} %convert_multiply_fusion, s32[2048]{0:T(1024)S(1)} %bitcast.28), kind=kCustom, calls=%fused_computation | custom fusion | bytes 32768 | tf_op jit(solution)/shard_map/gather | solution.py:56
  (4 shorter events, 0.1 us)
Async XLA Ops:
  7.2 187.8 %reduce-scatter.2.cloned.1.call-start = ((), (), s32[]{:S(2)}) async-start(), calls=%async_computation.1 | async-start | bytes 4259840 | tf_op jit(solution)/shard_map/reduce_scatter | solution.py:40
  7.2 20.0 %copy-start = (s32[2048,1]{0,1:T(1,128)S(1)}, s32[2048,1]{0,1:T(1,128)}, u32[]{:S(2)}) copy-start(s32[2048,1]{0,1:T(1,128)} %param.4) | copy-start | bytes 24580
  8.0 19.5 %copy-start.1 = (s32[2]{0:T(128)S(1)}, s32[2]{0:T(128)}, u32[]{:S(2)}) copy-start(s32[2]{0:T(128)} %constant.28) | copy-start | bytes 28
  48.9 232.5 %all-gather.2.cloned.1.call-start = ((), (), s32[]{:S(2)}) async-start(), calls=%async_computation.2 | async-start | bytes 2129920 | tf_op jit(solution)/shard_map/all_gather | solution.py:47
  207.9 126.5 %all-reduce.2.cloned.1.call-start = ((), (), s32[]{:S(2)}) async-start(), calls=%async_computation.3 | async-start | bytes 2097152 | tf_op jit(solution)/shard_map/psum | solution.py:54
Sparse Core Ops, SparseCore 0:
  49.1 145.8 reduce-scatter.1
  208.1 73.3 all-gather.1
  284.9 49.5 all-reduce.1
where the time goes:
time: 366 us; the launch traced here: 365 us
  waiting for transfers between devices  269 us (73%)
  local copies, waits for them, and re-layouts  41.7 us (11%)
  other arithmetic  24.1 us (7%)
  between operations  13.8 us (4%)
  blocking collectives  10.5 us (3%)
  matrix products  5.9 us (2%)
    reduce_scatter x1, waiting for transfers between devices, body(): lax.psum_scatter(block.reshape(lax.axis_size('rows') * K, feature_width),...  146 us
    all_gather x1, waiting for transfers between devices, body(): shard_piece = lax.all_gather(centroids, 'rows', axis=0, tiled=True)  73.5 us
    psum x1, waiting for transfers between devices, body(): lax.psum(inner_products.astype(jnp.bfloat16), 'feat').astype(jnp.float32)  49.7 us
    gather x1, local copies, waits for them, and re-layouts, body(): row_fit = slot_fits[parent, ranking]  22.4 us
    unnamed x6, local copies, waits for them, and re-layouts  18.6 us
    another operation x2, other arithmetic  18.3 us
    psum x1, blocking collectives, normalize(): square_sum = lax.psum(squares, 'feat')  10.5 us
  transfers between devices with their start and end apart: 3, of which 3 were waited for; matrix products, arithmetic and copies ran while one was open for 0% of the time, Pallas kernels for 0%

commit v1 on v0

v1 whole, which is shorter than its diff:
```python
import functools

import jax
import jax.numpy as jnp
from jax import lax
from jax.experimental import pallas as pl
from jax.experimental.pallas import tpu as pltpu
from jax.sharding import Mesh, PartitionSpec as P

D = 1024
K = 64
EPS = 1e-06
NY, NZ, NC, NX = 4, 8, 2, 4
PARENTS = NY * NZ * NC
ROWS = 2048
WIDTH = 256
PIECE = NZ * K
BLOCK = 512
VMEM = 40 * 1024 * 1024

F32 = jnp.float32
BF16 = jnp.bfloat16


def call(kernel, out_shape, flops, n_bytes, n_smem, n_vmem):
    smem = pl.BlockSpec(memory_space=pltpu.SMEM)
    vmem = pl.BlockSpec(memory_space=pltpu.VMEM)
    return pl.pallas_call(
        kernel,
        out_shape=out_shape,
        in_specs=[smem] * n_smem + [vmem] * n_vmem,
        out_specs=jax.tree.map(lambda _: vmem, out_shape),
        compiler_params=pltpu.CompilerParams(vmem_limit_bytes=VMEM),
        cost_estimate=pl.CostEstimate(flops=flops, bytes_accessed=n_bytes, transcendentals=0),
    )


def sums_kernel(where_ref, code_ref, other_code_ref, rows_ref, other_rows_ref, out_ref):
    y, core = where_ref[0], where_ref[1]
    total = jnp.zeros((PIECE, WIDTH), F32)
    for codes, rows in ((code_ref, rows_ref), (other_code_ref, other_rows_ref)):
        for start in range(0, ROWS, BLOCK):
            code = codes[:, start : start + BLOCK]
            parent = code >> 6
            inside = ((parent >> 4) == y) & ((parent & 1) == core)
            local = jnp.where(inside, ((parent >> 1) & 7) * K + (code & 63), -1)
            child = lax.broadcasted_iota(jnp.int32, (PIECE, BLOCK), 0)
            member = (child == local).astype(F32).astype(BF16)
            total += jnp.dot(member, rows[start : start + BLOCK, :], preferred_element_type=F32)
    out_ref[...] = total.astype(out_ref.dtype)


def merge_kernel(own_ref, a_ref, b_ref, c_ref, out_ref):
    total = own_ref[...] + a_ref[...].astype(F32) + b_ref[...].astype(F32) + c_ref[...].astype(F32)
    out_ref[...] = total.astype(BF16)


def totals_kernel(parts_ref, totals_ref, copies_ref):
    total = parts_ref[0:K, :].astype(F32)
    for z in range(1, NZ):
        total += parts_ref[z * K : (z + 1) * K, :].astype(F32)
    totals_ref[...] = total
    rounded = total.astype(BF16)
    for z in range(NZ):
        copies_ref[z * K : (z + 1) * K, :] = rounded


def scores_kernel(where_ref, parent_ref, rows_ref, *refs):
    own_refs, other_refs, out_ref = refs[:NY], refs[NY : 2 * NY], refs[2 * NY]
    y, core = where_ref[0], where_ref[1]
    lane = lax.broadcasted_iota(jnp.int32, (K, PARENTS), 1)
    squares = jnp.zeros((K, PARENTS), F32)
    for step in range(NY):
        source = (y + NY - step) & (NY - 1)
        for side, refs_of_side in ((core, own_refs), (1 - core, other_refs)):
            for z in range(NZ):
                number = source * 16 + z * 2 + side
                block = refs_of_side[step][z * K : (z + 1) * K, :].astype(F32)
                square = jnp.sum(block * block, axis=1, keepdims=True)
                squares = jnp.where(lane == number, square, squares)
    high = squares.astype(BF16)
    low = (squares - high.astype(F32)).astype(BF16)
    out_ref[:, ROWS : ROWS + PARENTS] = high
    out_ref[:, ROWS + PARENTS : ROWS + 2 * PARENTS] = low
    for start in range(0, ROWS, BLOCK):
        rows = rows_ref[start : start + BLOCK, :]
        parent = parent_ref[:, start : start + BLOCK]
        best = jnp.zeros((K, BLOCK), F32)
        for step in range(NY):
            source = (y + NY - step) & (NY - 1)
            for side, refs_of_side in ((core, own_refs), (1 - core, other_refs)):
                product = lax.dot_general(
                    refs_of_side[step][...], rows, (((1,), (1,)), ((), ())), preferred_element_type=F32
                )
                for z in range(NZ):
                    number = source * 16 + z * 2 + side
                    best = jnp.where(parent == number, product[z * K : (z + 1) * K, :], best)
        out_ref[:, start : start + BLOCK] = best.astype(BF16)


def finish_kernel(where_ref, parent_ref, a_ref, b_ref, c_ref, d_ref, totals_ref, centroids_ref, fit_ref):
    y, core, z = where_ref[0], where_ref[1], where_ref[2]
    refs = (a_ref, b_ref, c_ref, d_ref)

    def added(start, size):
        parts = [ref[:, start : start + size].astype(F32) for ref in refs]
        return (parts[0] + parts[1]) + (parts[2] + parts[3])

    squares = added(ROWS, 2 * PARENTS)
    squares = squares[:, :PARENTS] + squares[:, PARENTS:]
    scale = lax.rsqrt(squares / D + EPS)
    lane = lax.broadcasted_iota(jnp.int32, (K, PARENTS), 1)
    own = jnp.sum(jnp.where(lane == y * 16 + z * 2 + core, scale, 0.0), axis=1, keepdims=True)
    centroids_ref[...] = (totals_ref[...] * own).astype(BF16)
    high = scale.astype(BF16)
    low = (scale - high.astype(F32)).astype(BF16)
    for start in range(0, ROWS, BLOCK):
        parent = parent_ref[:, start : start + BLOCK]
        number = lax.broadcasted_iota(jnp.int32, (PARENTS, BLOCK), 0)
        chosen = (number == parent).astype(F32).astype(BF16)
        factor = jnp.dot(high, chosen, preferred_element_type=F32) + jnp.dot(
            low, chosen, preferred_element_type=F32
        )
        scores = added(start, BLOCK) * factor
        fit_ref[:, start : start + BLOCK] = jnp.max(scores, axis=0, keepdims=True) / (0.25 * D)


def shift(x, axis, size, by):
    return lax.ppermute(x, axis, [(i, (i + by) % size) for i in range(size)])


def body(embeddings, parent_ids, child_assignment):
    y, z, core = lax.axis_index("y"), lax.axis_index("z"), lax.axis_index("core")
    parent = parent_ids.reshape(1, ROWS)
    code = parent * K + child_assignment.reshape(1, ROWS)
    other_rows = shift(embeddings, "core", NC, 1)
    other_code = shift(code, "core", NC, 1)

    def sums(by, dtype):
        where = jnp.stack([(y + by) % NY, core])
        return call(
            sums_kernel, jax.ShapeDtypeStruct((PIECE, WIDTH), dtype), 2 * PIECE * WIDTH * 2 * ROWS, 3 << 20, 1, 4
        )(where, code, other_code, embeddings, other_rows)

    arrived = [shift(sums(by, BF16), "y", NY, by) for by in (2, 1, 3)]
    merged = call(merge_kernel, jax.ShapeDtypeStruct((PIECE, WIDTH), BF16), 0, 2 << 20, 0, 4)(
        sums(0, F32), *arrived
    )
    parts = lax.all_to_all(merged, "z", 0, 0, tiled=True)
    totals, copies = call(
        totals_kernel,
        (jax.ShapeDtypeStruct((K, WIDTH), F32), jax.ShapeDtypeStruct((PIECE, WIDTH), BF16)),
        0, 1 << 20, 0, 1,
    )(parts)
    mine = lax.all_to_all(copies, "z", 0, 0, tiled=True)
    far = shift(mine, "y", NY, 2)
    own_side = [mine, shift(mine, "y", NY, 1), far, shift(mine, "y", NY, 3)]
    other_side = [shift(piece, "core", NC, 1) for piece in own_side]
    where = jnp.stack([y, core, z])
    partial = call(
        scores_kernel, jax.ShapeDtypeStruct((K, ROWS + 2 * PARENTS), BF16), 2 * ROWS * 4096 * WIDTH, 4 << 20, 1, 10
    )(where, parent, embeddings, *own_side, *other_side)
    partials = [partial] + [shift(partial, "feat", NX, by) for by in (2, 1, 3)]
    centroids, fit = call(
        finish_kernel,
        (jax.ShapeDtypeStruct((K, WIDTH), BF16), jax.ShapeDtypeStruct((1, ROWS), F32)),
        2 * K * PARENTS * ROWS * 2, 2 << 20, 1, 6,
    )(where, parent, *partials, totals)
    return centroids, fit.reshape(ROWS)


def solution(mesh):
    split = Mesh(mesh.devices.reshape(NY, NZ, NC, NX), ("y", "z", "core", "feat"))
    rows = ("y", "z", "core")
    in_specs = (P(rows, "feat"), P(rows, None), P(rows))
    out_specs = (P(rows, "feat"), P(rows))
    return jax.shard_map(body, mesh=split, in_specs=in_specs, out_specs=out_specs, check_vma=False)
```

time: 366 us -> 96.2 us (0.26)
  waiting for transfers between devices: 269 us -> 29.2 us
  local copies, waits for them, and re-layouts: 41.7 us -> 1.24 us
  other arithmetic: 24.1 us -> 1.09 us
  blocking collectives: 10.5 us -> 32.1 us
  starting transfers between devices: 0.12 us -> 15.9 us
  Pallas kernels: 0 us -> 15.2 us
  between operations: 13.8 us -> 0.73 us
  matrix products: 5.9 us -> 0 us
    reduce_scatter x1 -> x0, waiting for transfers between devices: 146 us -> none  [body(): lax.psum_scatter(block.reshape(lax.axis_size('rows') * K, feature_width),...]
    all_gather x1 -> x0, waiting for transfers between devices: 73.5 us -> none  [body(): shard_piece = lax.all_gather(centroids, 'rows', axis=0, tiled=True)]
    psum x1 -> x0, waiting for transfers between devices: 49.7 us -> none  [body(): lax.psum(inner_products.astype(jnp.bfloat16), 'feat').astype(jnp.float32)]
    all_to_all x0 -> x2, blocking collectives: none -> 32.1 us  [the longest x1 19.2 us: body(): parts = lax.all_to_all(merged, 'z', 0, 0, tiled=True)]
    ppermute x0 -> x15, waiting for transfers between devices: none -> 29.2 us  [shift(): return lax.ppermute(x, axis, [(i, (i + by) % size) for i in range(size)])]
    gather x1 -> x0, local copies, waits for them, and re-layouts: 22.4 us -> none  [body(): row_fit = slot_fits[parent, ranking]]
    another operation x2 -> x5, other arithmetic: 18.3 us -> 0.37 us  [the longest x4 0.3 us: sums(): where = jnp.stack([(y + by) % NY, core])]
    unnamed x6 -> x8, local copies, waits for them, and re-layouts: 18.6 us -> 1.24 us
  transfers between devices with their start and end apart: 3 -> 15, of which waited for: 3 -> 11; matrix products, arithmetic and copies ran while one was open for 0% -> 1% of each run, Pallas kernels for 0% -> 6%
where the time goes in v1:
time: 96.2 us; the launch traced here: 95.4 us
  blocking collectives  32.1 us (33%)
  waiting for transfers between devices  29.2 us (30%)
  starting transfers between devices  15.9 us (17%)
  Pallas kernels  15.2 us (16%)
  local copies, waits for them, and re-layouts  1.24 us (1%)
  other arithmetic  1.09 us (1%)
    ppermute x15, waiting for transfers between devices, shift(): return lax.ppermute(x, axis, [(i, (i + by) % size) for i in range(size)])  29.2 us
    all_to_all x1, blocking collectives, body(): parts = lax.all_to_all(merged, 'z', 0, 0, tiled=True)  19.2 us
    ppermute x15, starting transfers between devices, shift(): return lax.ppermute(x, axis, [(i, (i + by) % size) for i in range(size)])  15.9 us
    all_to_all x1, blocking collectives, body(): mine = lax.all_to_all(copies, 'z', 0, 0, tiled=True)  12.9 us
    pallas_call x4, Pallas kernels, sums(): call(sums_kernel, jax.ShapeDtypeStruct((PIECE, WIDTH), dtype), 2 * PIECE...  7.85 us
    pallas_call x1, Pallas kernels, body(): call(scores_kernel, jax.ShapeDtypeStruct((K, ROWS + 2 * PARENTS), BF16),...  5.6 us
  transfers between devices with their start and end apart: 15, of which 11 were waited for; matrix products, arithmetic and copies ran while one was open for 1% of the time, Pallas kernels for 6%

profile of v1, /device:TPU:8, one launch (start us, length us, event | category | flops | bytes accessed | tf_op | source)
XLA Modules:
  0.0 95.4 jit_solution(13080116472284373026)
XLA Ops:
  0.6 0.1 collective-permute-start.1
  0.7 0.7 broadcast_multiply_fusion
  1.5 0.6 collective-permute-start
  2.3 1.1 %collective-permute-done.other_code_ref = s32[1,2048]{1,0:T(1,128)S(1)} collective-permute-done((s32[1,2048]{1,0:T(1,128)S(1)}, s32[1,2048]{1,0:T(1,128)S(1)}, u32[]{:S(2)}, u32[]{:S(2)}) %collective-permute-start) | collective-permute-done | bytes 8224 | tf_op jit(solution)/shard_map/ppermute | solution.py:129
  3.4 0.2 collective-permute-done.1.other_rows_ref
  3.6 1.2 %copy-done.1 = bf16[2048,256]{1,0:T(8,128)(2,1)S(1)} copy-done((bf16[2048,256]{1,0:T(8,128)(2,1)S(1)}, bf16[2048,256]{1,0:T(8,128)(2,1)}, u32[]{:S(2)}) %copy-start.1) | copy-done | bytes 1048600
  4.8 1.8 %shard_map.51 = bf16[512,256]{1,0:T(8,128)(2,1)S(1)} custom-call(s32[2]{0:T(128)S(1)} %pad_add_fusion.2.where_ref, s32[1,2048]{1,0:T(1,128)S(1)} %bitcast.26, s32[1,2048]{1,0:T(1,128)S(1)} %collective-permute-done.other_code_ref, bf16[2048,256]{1,0:T(8,128)(2,1)S(1)} %copy-done.1, bf16[2048,256]{1,0:T(8,128)(2,1)S(1)} %collective-permute-done.1.other_rows_ref), custom_call_target="tpu_custom_call" | custom-call | flops 1073741824 | bytes 3145728 | tf_op jit(solution)/shard_map/pallas_call | solution.py:141
  6.6 2.4 %collective-permute-start.2 = (bf16[512,256]{1,0:T(8,128)(2,1)S(1)}, bf16[512,256]{1,0:T(8,128)(2,1)S(1)}, u32[]{:S(2)}, u32[]{:S(2)}) collective-permute-start(bf16[512,256]{1,0:T(8,128)(2,1)S(1)} %shard_map.51), channel_id=1, source_target_pairs={{0,128},{64,192},{128,0},{192,64},{1,129},{65,193},{129,1},{193,65... | collective-permute-start | bytes 786440 | tf_op jit(solution)/shard_map/ppermute | solution.py:129
  9.0 1.8 %shard_map.52 = bf16[512,256]{1,0:T(8,128)(2,1)S(1)} custom-call(s32[2]{0:T(128)S(1)} %pad_add_fusion.3.where_ref, s32[1,2048]{1,0:T(1,128)S(1)} %bitcast.27, s32[1,2048]{1,0:T(1,128)S(1)} %collective-permute-done.other_code_ref, bf16[2048,256]{1,0:T(8,128)(2,1)S(1)} %copy-done.1, bf16[2048,256]{1,0:T(8,128)(2,1)S(1)} %collective-permute-done.1.other_rows_ref), custom_call_target="tpu_custom_call" | custom-call | flops 1073741824 | bytes 3145728 | tf_op jit(solution)/shard_map/pallas_call | solution.py:141
  10.8 1.4 %collective-permute-start.3 = (bf16[512,256]{1,0:T(8,128)(2,1)S(1)}, bf16[512,256]{1,0:T(8,128)(2,1)S(1)}, u32[]{:S(2)}, u32[]{:S(2)}) collective-permute-start(bf16[512,256]{1,0:T(8,128)(2,1)S(1)} %shard_map.52), channel_id=1, source_target_pairs={{0,64},{64,128},{128,192},{192,0},{1,65},{65,129},{129,193},{193,1... | collective-permute-start | bytes 786440 | tf_op jit(solution)/shard_map/ppermute | solution.py:129
  12.2 2.5 %shard_map.53 = bf16[512,256]{1,0:T(8,128)(2,1)} custom-call(s32[2]{0:T(128)S(1)} %pad_add_fusion.4.where_ref, s32[1,2048]{1,0:T(1,128)S(1)} %bitcast.28, s32[1,2048]{1,0:T(1,128)S(1)} %collective-permute-done.other_code_ref, bf16[2048,256]{1,0:T(8,128)(2,1)S(1)} %copy-done.1, bf16[2048,256]{1,0:T(8,128)(2,1)S(1)} %collective-permute-done.1.other_rows_ref), custom_call_target="tpu_custom_call" | custom-call | flops 1073741824 | bytes 3145728 | tf_op jit(solution)/shard_map/pallas_call | solution.py:141
  14.7 0.7 collective-permute-start.4
  15.5 1.8 %shard_map.50.own_ref = f32[512,256]{1,0:T(8,128)S(1)} custom-call(s32[2]{0:T(128)S(1)} %pad_add_fusion.1.where_ref, s32[1,2048]{1,0:T(1,128)S(1)} %bitcast.29, s32[1,2048]{1,0:T(1,128)S(1)} %collective-permute-done.other_code_ref, bf16[2048,256]{1,0:T(8,128)(2,1)S(1)} %copy-done.2, bf16[2048,256]{1,0:T(8,128)(2,1)S(1)} %collective-permute-done.1.other_rows_ref), custom_call_target="tpu_custom_call" | custom-call | flops 1073741824 | bytes 3145728 | tf_op jit(solution)/shard_map/pallas_call | solution.py:141
  17.3 5.0 %collective-permute-done.3.b_ref = bf16[512,256]{1,0:T(8,128)(2,1)S(1)} collective-permute-done((bf16[512,256]{1,0:T(8,128)(2,1)S(1)}, bf16[512,256]{1,0:T(8,128)(2,1)S(1)}, u32[]{:S(2)}, u32[]{:S(2)}) %collective-permute-start.3) | collective-permute-done | bytes 262176 | tf_op jit(solution)/shard_map/ppermute | solution.py:129
  22.3 0.4 collective-permute-done.4.c_ref
  22.7 0.1 shard_map.54
  22.9 19.2 %all_to_all.22 = bf16[8,64,256]{2,1,0:T(8,128)(2,1)S(1)} all-to-all(bf16[8,64,256]{2,1,0:T(8,128)(2,1)S(1)} %bitcast.16), channel_id=1, replica_groups=mesh['y'=4,'z'=8,'core'=2,'feat'=4] {'z'}, dimensions={0} | all-to-all | bytes 524288 | tf_op jit(solution)/shard_map/all_to_all | solution.py:149
  42.2 12.9 %all_to_all.23 = bf16[8,64,256]{2,1,0:T(8,128)(2,1)S(1)} all-to-all(bf16[8,64,256]{2,1,0:T(8,128)(2,1)S(1)} %bitcast.22), channel_id=1, replica_groups=mesh['y'=4,'z'=8,'core'=2,'feat'=4] {'z'}, dimensions={0} | all-to-all | bytes 524288 | tf_op jit(solution)/shard_map/all_to_all | solution.py:155
  55.0 0.7 collective-permute-start.7
  55.7 3.2 %collective-permute-start.6 = (bf16[512,256]{1,0:T(8,128)(2,1)S(1)}, bf16[512,256]{1,0:T(8,128)(2,1)S(1)}, u32[]{:S(2)}, u32[]{:S(2)}) collective-permute-start(bf16[512,256]{1,0:T(8,128)(2,1)S(1)} %bitcast.18), channel_id=1, source_target_pairs={{0,128},{64,192},{128,0},{192,64},{1,129},{65,193},{129,1},{193,65... | collective-permute-start | bytes 786440 | tf_op jit(solution)/shard_map/ppermute | solution.py:129
  58.9 1.8 %collective-permute-start.5 = (bf16[512,256]{1,0:T(8,128)(2,1)S(1)}, bf16[512,256]{1,0:T(8,128)(2,1)S(1)}, u32[]{:S(2)}, u32[]{:S(2)}) collective-permute-start(bf16[512,256]{1,0:T(8,128)(2,1)S(1)} %bitcast.19), channel_id=1, source_target_pairs={{0,64},{64,128},{128,192},{192,0},{1,65},{65,129},{129,193},{193,1... | collective-permute-start | bytes 786440 | tf_op jit(solution)/shard_map/ppermute | solution.py:129
  60.7 3.9 %collective-permute-done.7.refs_3_ = bf16[512,256]{1,0:T(8,128)(2,1)S(1)} collective-permute-done((bf16[512,256]{1,0:T(8,128)(2,1)S(1)}, bf16[512,256]{1,0:T(8,128)(2,1)S(1)}, u32[]{:S(2)}, u32[]{:S(2)}) %collective-permute-start.7) | collective-permute-done | bytes 262176 | tf_op jit(solution)/shard_map/ppermute | solution.py:129
  64.6 3.1 %collective-permute-done.6.refs_2_ = bf16[512,256]{1,0:T(8,128)(2,1)S(1)} collective-permute-done((bf16[512,256]{1,0:T(8,128)(2,1)S(1)}, bf16[512,256]{1,0:T(8,128)(2,1)S(1)}, u32[]{:S(2)}, u32[]{:S(2)}) %collective-permute-start.6) | collective-permute-done | bytes 262176 | tf_op jit(solution)/shard_map/ppermute | solution.py:129
  67.7 0.6 collective-permute-done.5.refs_1_
  68.4 0.8 collective-permute-done.10.refs_6_
  69.2 0.6 collective-permute-done.9.refs_5_
  69.9 5.6 %shard_map.56.a_ref = bf16[64,2176]{1,0:T(8,128)(2,1)S(1)} custom-call(s32[3]{0:T(128)S(1)} %pad_add_fusion.where_ref, s32[1,2048]{1,0:T(1,128)S(1)} %bitcast.23, bf16[2048,256]{1,0:T(8,128)(2,1)S(1)} %copy-done.2, bf16[512,256]{1,0:T(8,128)(2,1)S(1)} %bitcast.21, bf16[512,256]{1,0:T(8,128)(2,1)S(1)} %collective-permute-done.5.refs_1_, ...), custom_call_target="tpu_custom_call" | custom-call | flops 4294967296 | bytes 4194304 | tf_op jit(solution)/shard_map/pallas_call | solution.py:160
  75.5 2.8 %collective-permute-start.14 = (bf16[64,2176]{1,0:T(8,128)(2,1)S(1)}, bf16[64,2176]{1,0:T(8,128)(2,1)S(1)}, u32[]{:S(2)}, u32[]{:S(2)}) collective-permute-start(bf16[64,2176]{1,0:T(8,128)(2,1)S(1)} %shard_map.56.a_ref), channel_id=1, source_target_pairs={{0,3},{1,0},{2,1},{3,2},{4,7},{5,4},{6,5},{7,6},{8,11},{9,8},{10,9... | collective-permute-start | bytes 835592 | tf_op jit(solution)/shard_map/ppermute | solution.py:129
  78.3 2.3 %collective-permute-start.12 = (bf16[64,2176]{1,0:T(8,128)(2,1)S(1)}, bf16[64,2176]{1,0:T(8,128)(2,1)S(1)}, u32[]{:S(2)}, u32[]{:S(2)}) collective-permute-start(bf16[64,2176]{1,0:T(8,128)(2,1)S(1)} %shard_map.56.a_ref), channel_id=1, source_target_pairs={{0,2},{1,3},{2,0},{3,1},{4,6},{5,7},{6,4},{7,5},{8,10},{9,11},{10,... | collective-permute-start | bytes 835592 | tf_op jit(solution)/shard_map/ppermute | solution.py:129
  80.6 9.9 %collective-permute-done.14.d_ref = bf16[64,2176]{1,0:T(8,128)(2,1)S(1)} collective-permute-done((bf16[64,2176]{1,0:T(8,128)(2,1)S(1)}, bf16[64,2176]{1,0:T(8,128)(2,1)S(1)}, u32[]{:S(2)}, u32[]{:S(2)}) %collective-permute-start.14) | collective-permute-done | bytes 278560 | tf_op jit(solution)/shard_map/ppermute | solution.py:129
  90.5 3.4 %collective-permute-done.13.c_ref = bf16[64,2176]{1,0:T(8,128)(2,1)S(1)} collective-permute-done((bf16[64,2176]{1,0:T(8,128)(2,1)S(1)}, bf16[64,2176]{1,0:T(8,128)(2,1)S(1)}, u32[]{:S(2)}, u32[]{:S(2)}) %collective-permute-start.13) | collective-permute-done | bytes 278560 | tf_op jit(solution)/shard_map/ppermute | solution.py:129
  93.9 1.5 %shard_map.57 = (bf16[64,256]{1,0:T(8,128)(2,1)}, f32[1,2048]{1,0:T(1,128)}) custom-call(s32[3]{0:T(128)S(1)} %pad_add_fusion.where_ref, s32[1,2048]{1,0:T(1,128)S(1)} %bitcast.24, bf16[64,2176]{1,0:T(8,128)(2,1)S(1)} %shard_map.56.a_ref, bf16[64,2176]{1,0:T(8,128)(2,1)S(1)} %collective-permute-done.12.b_ref, ...), custom_call_target="tpu_custom_call" | custom-call | flops 33554432 | bytes 2097152 | tf_op jit(solution)/shard_map/pallas_call | solution.py:164
  (23 shorter events, 0.5 us)
Async XLA Ops:
  0.6 0.8 copy-start.3
  0.6 3.0 %collective-permute-start.1 = (bf16[2048,256]{1,0:T(8,128)(2,1)}, bf16[2048,256]{1,0:T(8,128)(2,1)S(1)}, u32[]{:S(2)}, u32[]{:S(2)}) collective-permute-start(bf16[2048,256]{1,0:T(8,128)(2,1)} %rows_ref.9), channel_id=1, source_target_pairs={{0,4},{4,0},{1,5},{5,1},{2,6},{6,2},{3,7},{7,3},{8,12},{12,8},{9,1... | collective-permute-start | bytes 3145736 | tf_op jit(solution)/shard_map/ppermute | solution.py:129
  1.5 1.9 %collective-permute-start = (s32[1,2048]{1,0:T(1,128)S(1)}, s32[1,2048]{1,0:T(1,128)S(1)}, u32[]{:S(2)}, u32[]{:S(2)}) collective-permute-start(s32[1,2048]{1,0:T(1,128)S(1)} %bitcast.25), channel_id=1, source_target_pairs={{0,4},{4,0},{1,5},{5,1},{2,6},{6,2},{3,7},{7,3},{8,12},{12,8},{9,1... | collective-permute-start | bytes 24584 | tf_op jit(solution)/shard_map/ppermute | solution.py:129
  3.6 1.2 %copy-start.1 = (bf16[2048,256]{1,0:T(8,128)(2,1)S(1)}, bf16[2048,256]{1,0:T(8,128)(2,1)}, u32[]{:S(2)}) copy-start(bf16[2048,256]{1,0:T(8,128)(2,1)} %rows_ref.9) | copy-start | bytes 3145732
  6.6 10.7 %collective-permute-start.2 = (bf16[512,256]{1,0:T(8,128)(2,1)S(1)}, bf16[512,256]{1,0:T(8,128)(2,1)S(1)}, u32[]{:S(2)}, u32[]{:S(2)}) collective-permute-start(bf16[512,256]{1,0:T(8,128)(2,1)S(1)} %shard_map.51), channel_id=1, source_target_pairs={{0,128},{64,192},{128,0},{192,64},{1,129},{65,193},{129,1},{193,65... | collective-permute-start | bytes 786440 | tf_op jit(solution)/shard_map/ppermute | solution.py:129
  10.8 4.7 %copy-start.2 = (bf16[2048,256]{1,0:T(8,128)(2,1)S(1)}, bf16[2048,256]{1,0:T(8,128)(2,1)}, u32[]{:S(2)}) copy-start(bf16[2048,256]{1,0:T(8,128)(2,1)} %rows_ref.9) | copy-start | bytes 3145732
  10.8 11.5 %collective-permute-start.3 = (bf16[512,256]{1,0:T(8,128)(2,1)S(1)}, bf16[512,256]{1,0:T(8,128)(2,1)S(1)}, u32[]{:S(2)}, u32[]{:S(2)}) collective-permute-start(bf16[512,256]{1,0:T(8,128)(2,1)S(1)} %shard_map.52), channel_id=1, source_target_pairs={{0,64},{64,128},{128,192},{192,0},{1,65},{65,129},{129,193},{193,1... | collective-permute-start | bytes 786440 | tf_op jit(solution)/shard_map/ppermute | solution.py:129
  14.7 8.0 %collective-permute-start.4 = (bf16[512,256]{1,0:T(8,128)(2,1)}, bf16[512,256]{1,0:T(8,128)(2,1)S(1)}, u32[]{:S(2)}, u32[]{:S(2)}) collective-permute-start(bf16[512,256]{1,0:T(8,128)(2,1)} %shard_map.53), channel_id=1, source_target_pairs={{0,192},{64,0},{128,64},{192,128},{1,193},{65,1},{129,65},{193,129... | collective-permute-start | bytes 786440 | tf_op jit(solution)/shard_map/ppermute | solution.py:129
  55.0 14.8 %copy-start = (s32[2048,1]{0,1:T(1,128)S(1)}, s32[2048,1]{0,1:T(1,128)}, u32[]{:S(2)}) copy-start(s32[2048,1]{0,1:T(1,128)} %param.4) | copy-start | bytes 24580
  55.0 9.5 %collective-permute-start.7 = (bf16[512,256]{1,0:T(8,128)(2,1)S(1)}, bf16[512,256]{1,0:T(8,128)(2,1)S(1)}, u32[]{:S(2)}, u32[]{:S(2)}) collective-permute-start(bf16[512,256]{1,0:T(8,128)(2,1)S(1)} %bitcast.17), channel_id=1, source_target_pairs={{0,192},{64,0},{128,64},{192,128},{1,193},{65,1},{129,65},{193,129... | collective-permute-start | bytes 786440 | tf_op jit(solution)/shard_map/ppermute | solution.py:129
  55.7 11.9 %collective-permute-start.6 = (bf16[512,256]{1,0:T(8,128)(2,1)S(1)}, bf16[512,256]{1,0:T(8,128)(2,1)S(1)}, u32[]{:S(2)}, u32[]{:S(2)}) collective-permute-start(bf16[512,256]{1,0:T(8,128)(2,1)S(1)} %bitcast.18), channel_id=1, source_target_pairs={{0,128},{64,192},{128,0},{192,64},{1,129},{65,193},{129,1},{193,65... | collective-permute-start | bytes 786440 | tf_op jit(solution)/shard_map/ppermute | solution.py:129
  58.9 9.4 %collective-permute-start.5 = (bf16[512,256]{1,0:T(8,128)(2,1)S(1)}, bf16[512,256]{1,0:T(8,128)(2,1)S(1)}, u32[]{:S(2)}, u32[]{:S(2)}) collective-permute-start(bf16[512,256]{1,0:T(8,128)(2,1)S(1)} %bitcast.19), channel_id=1, source_target_pairs={{0,64},{64,128},{128,192},{192,0},{1,65},{65,129},{129,193},{193,1... | collective-permute-start | bytes 786440 | tf_op jit(solution)/shard_map/ppermute | solution.py:129
  60.7 7.7 %collective-permute-start.8 = (bf16[512,256]{1,0:T(8,128)(2,1)S(1)}, bf16[512,256]{1,0:T(8,128)(2,1)S(1)}, u32[]{:S(2)}, u32[]{:S(2)}) collective-permute-start(bf16[512,256]{1,0:T(8,128)(2,1)S(1)} %bitcast.20), channel_id=1, source_target_pairs={{0,4},{4,0},{1,5},{5,1},{2,6},{6,2},{3,7},{7,3},{8,12},{12,8},{9,1... | collective-permute-start | bytes 786440 | tf_op jit(solution)/shard_map/ppermute | solution.py:129
  64.6 3.8 %collective-permute-start.11 = (bf16[512,256]{1,0:T(8,128)(2,1)S(1)}, bf16[512,256]{1,0:T(8,128)(2,1)S(1)}, u32[]{:S(2)}, u32[]{:S(2)}) collective-permute-start(bf16[512,256]{1,0:T(8,128)(2,1)S(1)} %collective-permute-done.7.refs_3_), channel_id=1, source_target_pairs={{0,4},{4,0},{1,5},{5,1},{2,6},{6,2},{3,7},{7,3},{8,12},{12,8},{9,1... | collective-permute-start | bytes 786440 | tf_op jit(solution)/shard_map/ppermute | solution.py:129
  67.7 1.5 %collective-permute-start.10 = (bf16[512,256]{1,0:T(8,128)(2,1)S(1)}, bf16[512,256]{1,0:T(8,128)(2,1)S(1)}, u32[]{:S(2)}, u32[]{:S(2)}) collective-permute-start(bf16[512,256]{1,0:T(8,128)(2,1)S(1)} %collective-permute-done.6.refs_2_), channel_id=1, source_target_pairs={{0,4},{4,0},{1,5},{5,1},{2,6},{6,2},{3,7},{7,3},{8,12},{12,8},{9,1... | collective-permute-start | bytes 786440 | tf_op jit(solution)/shard_map/ppermute | solution.py:129
  68.3 1.5 %collective-permute-start.9 = (bf16[512,256]{1,0:T(8,128)(2,1)S(1)}, bf16[512,256]{1,0:T(8,128)(2,1)S(1)}, u32[]{:S(2)}, u32[]{:S(2)}) collective-permute-start(bf16[512,256]{1,0:T(8,128)(2,1)S(1)} %collective-permute-done.5.refs_1_), channel_id=1, source_target_pairs={{0,4},{4,0},{1,5},{5,1},{2,6},{6,2},{3,7},{7,3},{8,12},{12,8},{9,1... | collective-permute-start | bytes 786440 | tf_op jit(solution)/shard_map/ppermute | solution.py:129
  75.5 15.1 %collective-permute-start.14 = (bf16[64,2176]{1,0:T(8,128)(2,1)S(1)}, bf16[64,2176]{1,0:T(8,128)(2,1)S(1)}, u32[]{:S(2)}, u32[]{:S(2)}) collective-permute-start(bf16[64,2176]{1,0:T(8,128)(2,1)S(1)} %shard_map.56.a_ref), channel_id=1, source_target_pairs={{0,3},{1,0},{2,1},{3,2},{4,7},{5,4},{6,5},{7,6},{8,11},{9,8},{10,9... | collective-permute-start | bytes 835592 | tf_op jit(solution)/shard_map/ppermute | solution.py:129
  78.3 15.6 %collective-permute-start.13 = (bf16[64,2176]{1,0:T(8,128)(2,1)S(1)}, bf16[64,2176]{1,0:T(8,128)(2,1)S(1)}, u32[]{:S(2)}, u32[]{:S(2)}) collective-permute-start(bf16[64,2176]{1,0:T(8,128)(2,1)S(1)} %shard_map.56.a_ref), channel_id=1, source_target_pairs={{0,1},{1,2},{2,3},{3,0},{4,5},{5,6},{6,7},{7,4},{8,9},{9,10},{10,1... | collective-permute-start | bytes 835592 | tf_op jit(solution)/shard_map/ppermute | solution.py:129
  78.3 15.6 %collective-permute-start.12 = (bf16[64,2176]{1,0:T(8,128)(2,1)S(1)}, bf16[64,2176]{1,0:T(8,128)(2,1)S(1)}, u32[]{:S(2)}, u32[]{:S(2)}) collective-permute-start(bf16[64,2176]{1,0:T(8,128)(2,1)S(1)} %shard_map.56.a_ref), channel_id=1, source_target_pairs={{0,2},{1,3},{2,0},{3,1},{4,6},{5,7},{6,4},{7,5},{8,10},{9,11},{10,... | collective-permute-start | bytes 835592 | tf_op jit(solution)/shard_map/ppermute | solution.py:129

commit v2 on v1

v2 whole, which is shorter than its diff:
```python
import functools

import jax
import jax.numpy as jnp
from jax import lax
from jax.experimental import pallas as pl
from jax.experimental.pallas import tpu as pltpu
from jax.sharding import Mesh, PartitionSpec as P

D = 1024
K = 64
EPS = 1e-06
NY, NZ, NC, NX = 4, 8, 2, 4
PARENTS = NY * NZ * NC
ROWS = 2048
WIDTH = 256
PIECE = NZ * K
HALF = PIECE // 2
SPLIT = ROWS // 2
BLOCK = 512
VMEM = 24 * 1024 * 1024
LONG = 1 << 32

F32 = jnp.float32
BF16 = jnp.bfloat16


def call(kernel, out_shape, operands, behind=(), flops=1000, far=0, scratch=()):
    vmem = pl.BlockSpec(memory_space=pltpu.VMEM)
    hbm = pl.BlockSpec(memory_space=pltpu.HBM)
    count = len(operands)

    def skipping(*refs):
        kernel(*refs[:count], *refs[count + len(behind) :])

    return pl.pallas_call(
        skipping,
        out_shape=out_shape,
        in_specs=[hbm] * far + [vmem] * (count - far + len(behind)),
        out_specs=jax.tree.map(lambda _: vmem, out_shape),
        scratch_shapes=list(scratch),
        compiler_params=pltpu.CompilerParams(vmem_limit_bytes=VMEM),
        cost_estimate=pl.CostEstimate(flops=flops, bytes_accessed=1000, transcendentals=0),
    )(*operands, *behind)


def add_members(totals, halves, parents, children, rows, start):
    y, core = lax.axis_index("y"), lax.axis_index("core")
    span = slice(start, start + BLOCK)
    parent = parents[:, span]
    block = rows[span, :]
    child = lax.broadcasted_iota(jnp.int32, (HALF, BLOCK), 0)
    for number, (k, upper) in enumerate(halves):
        inside = ((parent >> 4) == (y ^ k)) & ((parent & 1) == core)
        local = jnp.where(inside, ((parent >> 1) & 7) * K + children[:, span] - upper * HALF, -1)
        member = (child == local).astype(F32).astype(BF16)
        totals[number] += jnp.dot(member, block, preferred_element_type=F32)


def sums_kernel(halves, groups, *refs):
    outs, so_far = refs[-len(halves) :], refs[3 * groups : -len(halves)]
    totals = [x[...].astype(F32) for x in so_far] or [jnp.zeros((HALF, WIDTH), F32) for _ in halves]
    for group in range(groups):
        for start in range(0, ROWS, BLOCK):
            add_members(totals, halves, *refs[3 * group : 3 * group + 3], start)
    for out, total in zip(outs, totals):
        out[...] = total.astype(out.dtype)


def first_sums_kernel(halves, parents_ref, children_ref, rows_ref, *refs):
    outs = refs[: len(halves)]
    parents, children, rows, sems = refs[len(halves) :]
    copies = [
        pltpu.make_async_copy(parents_ref, parents, sems.at[0]),
        pltpu.make_async_copy(children_ref, children, sems.at[1]),
    ]
    for number, start in enumerate(range(0, ROWS, BLOCK)):
        span = pl.ds(start, BLOCK)
        copies.append(pltpu.make_async_copy(rows_ref.at[span], rows.at[span], sems.at[2 + number]))
    for copy in copies:
        copy.start()
    copies[0].wait()
    copies[1].wait()
    totals = [jnp.zeros((HALF, WIDTH), F32) for _ in halves]
    for number, start in enumerate(range(0, ROWS, BLOCK)):
        copies[2 + number].wait()
        add_members(totals, halves, parents, children, rows, start)
    for out, total in zip(outs, totals):
        out[...] = total


def merge_kernel(low_ref, high_ref, low_a, low_b, high_a, high_b, out_ref):
    out_ref[:HALF, :] = (low_ref[...] + low_a[...].astype(F32) + low_b[...].astype(F32)).astype(BF16)
    out_ref[HALF:, :] = (high_ref[...] + high_a[...].astype(F32) + high_b[...].astype(F32)).astype(BF16)


def totals_kernel(parts_ref, totals_ref, copies_ref):
    total = parts_ref[0:K, :].astype(F32)
    for z in range(1, NZ):
        total += parts_ref[z * K : (z + 1) * K, :].astype(F32)
    totals_ref[...] = total
    rounded = total.astype(BF16)
    for z in range(NZ):
        copies_ref[z * K : (z + 1) * K, :] = rounded


def scores_kernel(groups, blocks, first, with_squares, *refs):
    y, core = lax.axis_index("y"), lax.axis_index("core")
    group_refs, refs = refs[: 2 * groups], refs[2 * groups :]
    block_refs, refs = refs[: len(blocks)], refs[len(blocks) :]
    numbers = [(y ^ k) * 16 + 2 * z + core for k, z, _ in blocks]
    scores_in = squares_in = None
    if not first:
        scores_in, refs = refs[:groups], refs[groups:]
        if with_squares:
            squares_in, refs = refs[0], refs[1:]
    if with_squares:
        lane = lax.broadcasted_iota(jnp.int32, (K, PARENTS), 1)
        squares = jnp.zeros((K, PARENTS), F32) if first else squares_in[...]
        for number, block_ref, (_, _, count) in zip(numbers, block_refs, blocks):
            for z in range(count):
                block = block_ref[z * K : (z + 1) * K, :].astype(F32)
                square = jnp.sum(block * block, axis=1, keepdims=True)
                squares = jnp.where(lane == number + 2 * z, square, squares)
        refs[groups][...] = squares
    for group in range(groups):
        parents, rows_ref = group_refs[2 * group : 2 * group + 2]
        for start in range(0, ROWS, BLOCK):
            span = slice(start, start + BLOCK)
            rows, parent = rows_ref[span, :], parents[:, span]
            chosen = jnp.zeros((K, BLOCK), F32) if first else scores_in[group][:, span].astype(F32)
            for number, block_ref, (_, _, count) in zip(numbers, block_refs, blocks):
                product = lax.dot_general(
                    block_ref[...], rows, (((1,), (1,)), ((), ())), preferred_element_type=F32
                )
                for z in range(count):
                    chosen = jnp.where(parent == number + 2 * z, product[z * K : (z + 1) * K, :], chosen)
            refs[group][:, span] = chosen.astype(BF16)


def put_squares(out_ref, squares):
    high = squares.astype(BF16)
    out_ref[:, SPLIT : SPLIT + PARENTS] = high
    out_ref[:, SPLIT + PARENTS :] = (squares - high.astype(F32)).astype(BF16)


def get_squares(ref):
    return ref[:, SPLIT : SPLIT + PARENTS].astype(F32) + ref[:, SPLIT + PARENTS :].astype(F32)


def join_kernel(own_ref, arrived_ref, squares_ref, other_squares_ref, a_ref, b_ref):
    a_ref[...] = own_ref[:, :SPLIT] + arrived_ref[:, :SPLIT]
    b_ref[:, :SPLIT] = own_ref[:, SPLIT:] + arrived_ref[:, SPLIT:]
    put_squares(b_ref, squares_ref[...] + other_squares_ref[...])


def add_kernel(x_ref, y_ref, out_ref):
    scores = x_ref[:, :SPLIT].astype(F32) + y_ref[:, :SPLIT].astype(F32)
    out_ref[:, :SPLIT] = scores.astype(BF16)
    if out_ref.shape[1] > SPLIT:
        put_squares(out_ref, get_squares(x_ref) + get_squares(y_ref))


def finish_kernel(parent_ref, a_ref, other_a_ref, b_ref, other_b_ref, totals_ref, centroids_ref, fit_ref):
    y, z, core = lax.axis_index("y"), lax.axis_index("z"), lax.axis_index("core")
    scale = lax.rsqrt((get_squares(b_ref) + get_squares(other_b_ref)) / D + EPS)
    lane = lax.broadcasted_iota(jnp.int32, (K, PARENTS), 1)
    own = jnp.sum(jnp.where(lane == y * 16 + z * 2 + core, scale, 0.0), axis=1, keepdims=True)
    centroids_ref[...] = (totals_ref[...] * own).astype(BF16)
    high = scale.astype(BF16)
    low = (scale - high.astype(F32)).astype(BF16)
    for start in range(0, ROWS, BLOCK):
        parent = parent_ref[:, start : start + BLOCK]
        number = lax.broadcasted_iota(jnp.int32, (PARENTS, BLOCK), 0)
        chosen = (number == parent).astype(F32).astype(BF16)
        factor = jnp.dot(high, chosen, preferred_element_type=F32) + jnp.dot(
            low, chosen, preferred_element_type=F32
        )
        x_ref, y_ref = (a_ref, other_a_ref) if start < SPLIT else (b_ref, other_b_ref)
        at = start % SPLIT
        scores = x_ref[:, at : at + BLOCK].astype(F32) + y_ref[:, at : at + BLOCK].astype(F32)
        fit_ref[:, start : start + BLOCK] = jnp.max(scores * factor, axis=0, keepdims=True) / (0.25 * D)


def swap(x):
    return lax.ppermute(x, "core", [(0, 1), (1, 0)])


def left(x, axis):
    return lax.ppermute(x, axis, [(0, 1), (1, 0), (2, 3), (3, 2)])


def right(x, axis):
    return lax.ppermute(x, axis, [(0, 3), (3, 0), (1, 2), (2, 1)])


def body(embeddings, parent_ids, child_assignment):
    own = (parent_ids.reshape(1, ROWS), child_assignment.reshape(1, ROWS), embeddings)
    other = tuple(swap(x) for x in own)

    def halves_of(dtype):
        return (jax.ShapeDtypeStruct((HALF, WIDTH), dtype),) * 2

    def sums(halves, dtype, groups, so_far=(), behind=(), flops=1000):
        return call(
            functools.partial(sums_kernel, halves, len(groups)),
            halves_of(dtype),
            [x for group in groups for x in group] + list(so_far),
            behind=behind,
            flops=flops,
        )

    halves = ((2, 0), (2, 1))
    started = call(
        functools.partial(first_sums_kernel, halves),
        halves_of(F32),
        list(own),
        far=3,
        scratch=[
            pltpu.VMEM((1, ROWS), jnp.int32),
            pltpu.VMEM((1, ROWS), jnp.int32),
            pltpu.VMEM((ROWS, WIDTH), BF16),
            pltpu.SemaphoreType.DMA((2 + ROWS // BLOCK,)),
        ],
    )
    far_low, far_high = sums(halves, BF16, [other], started)
    got_low, got_high = left(far_low, "y"), right(far_high, "y")
    left_low, right_high = sums(((1, 0), (3, 1)), BF16, [own, other], behind=[far_low, far_high], flops=LONG)
    left_high, right_low = sums(
        ((1, 1), (3, 0)), BF16, [own, other], [got_high, got_low], behind=[left_low, right_high]
    )
    kept = sums(((0, 0), (0, 1)), F32, [own, other], behind=[left_high, right_low])
    merged = call(
        merge_kernel,
        jax.ShapeDtypeStruct((PIECE, WIDTH), BF16),
        [*kept, left(left_low, "y"), right(right_low, "y"), left(left_high, "y"), right(right_high, "y")],
    )
    parts = lax.all_to_all(merged, "z", 0, 0, tiled=True)
    totals, copies = call(
        totals_kernel,
        (jax.ShapeDtypeStruct((K, WIDTH), F32), jax.ShapeDtypeStruct((PIECE, WIDTH), BF16)),
        [parts],
    )
    mine = lax.all_to_all(copies, "z", 0, 0, tiled=True)

    low, high = mine[:HALF], mine[HALF:]
    left_low, right_high = left(low, "y"), right(high, "y")
    left_high, right_low = left(high, "y"), right(low, "y")
    far_low, far_high = right(left_low, "y"), left(right_high, "y")

    own_rows, other_rows = [own[0], own[2]], [other[0], other[2]]
    plain = jax.ShapeDtypeStruct((K, ROWS), BF16)
    squared = jax.ShapeDtypeStruct((K, PARENTS), F32)
    state = call(
        functools.partial(scores_kernel, 2, ((0, 0, NZ),), True, True),
        (plain, plain, squared),
        [*own_rows, *other_rows, mine],
    )
    blocks = ((1, 0, 4), (1, 4, 4), (3, 0, 4), (3, 4, 4))
    state = call(
        functools.partial(scores_kernel, 2, blocks, False, True),
        (plain, plain, squared),
        [*own_rows, *other_rows, left_low, left_high, right_low, right_high, *state],
        flops=LONG,
    )
    blocks = ((2, 0, 4), (2, 4, 4))
    sent, squares = call(
        functools.partial(scores_kernel, 1, blocks, False, True),
        (plain, squared),
        [*other_rows, far_low, far_high, *state[1:]],
    )
    (kept,) = call(
        functools.partial(scores_kernel, 1, blocks, False, False),
        (plain,),
        [*own_rows, far_low, far_high, state[0]],
        behind=[sent],
    )
    message = jax.ShapeDtypeStruct((K, SPLIT), BF16)
    long_message = jax.ShapeDtypeStruct((K, SPLIT + 2 * PARENTS), BF16)
    a, b = call(join_kernel, (message, long_message), [kept, swap(sent), squares, swap(squares)])

    a = call(add_kernel, message, [a, left(a, "feat")])
    b = call(add_kernel, long_message, [b, right(b, "feat")])
    centroids, fit = call(
        finish_kernel,
        (jax.ShapeDtypeStruct((K, WIDTH), BF16), jax.ShapeDtypeStruct((1, ROWS), F32)),
        [own[0], a, right(a, "feat"), b, left(b, "feat"), totals],
    )
    return centroids, fit.reshape(ROWS)


def solution(mesh):
    split = Mesh(mesh.devices.reshape(NY, NZ, NC, NX), ("y", "z", "core", "feat"))
    rows = ("y", "z", "core")
    in_specs = (P(rows, "feat"), P(rows, None), P(rows))
    out_specs = (P(rows, "feat"), P(rows))
    return jax.shard_map(body, mesh=split, in_specs=in_specs, out_specs=out_specs, check_vma=False)
```

time: 96.2 us -> 85.4 us (0.89)
  waiting for transfers between devices: 29.2 us -> 12.1 us
  starting transfers between devices: 15.9 us -> 25.5 us
  Pallas kernels: 15.2 us -> 12.3 us
  local copies, waits for them, and re-layouts: 1.24 us -> 2.65 us
  blocking collectives: 32.1 us -> 30.8 us
  other arithmetic: 1.09 us -> 0 us
    ppermute x15 -> x21, waiting for transfers between devices: 29.2 us -> 12.1 us  [the longest x8 8.22 us: right(): return lax.ppermute(x, axis, [(0, 3), (3, 0), (1, 2), (2, 1)])]
    ppermute x15 -> x21, starting transfers between devices: 15.9 us -> 25.5 us  [the longest x8 12.9 us: right(): return lax.ppermute(x, axis, [(0, 3), (3, 0), (1, 2), (2, 1)])]
    pallas_call x8 -> x15, Pallas kernels: 15.2 us -> 12.3 us  [call(): pl.pallas_call(skipping, out_shape=out_shape, in_specs=[hbm] * far + [vme...]
    unnamed x8 -> x10, local copies, waits for them, and re-layouts: 1.24 us -> 2.63 us
    all_to_all x1, blocking collectives: 19.2 us -> 17.9 us  [body(): parts = lax.all_to_all(merged, 'z', 0, 0, tiled=True)]
  transfers between devices with their start and end apart: 15 -> 21, of which waited for: 11 -> 7; matrix products, arithmetic and copies ran while one was open for 1% -> 0% of each run, Pallas kernels for 6% -> 11%
where the time goes in v2:
time: 85.4 us; the launch traced here: 84.2 us
  blocking collectives  30.8 us (36%)
  starting transfers between devices  25.5 us (30%)
  Pallas kernels  12.3 us (14%)
  waiting for transfers between devices  12.1 us (14%)
  local copies, waits for them, and re-layouts  2.65 us (3%)
    all_to_all x1, blocking collectives, body(): parts = lax.all_to_all(merged, 'z', 0, 0, tiled=True)  17.9 us
    ppermute x8, starting transfers between devices, right(): return lax.ppermute(x, axis, [(0, 3), (3, 0), (1, 2), (2, 1)])  12.9 us
    all_to_all x1, blocking collectives, body(): mine = lax.all_to_all(copies, 'z', 0, 0, tiled=True)  12.9 us
    pallas_call x15, Pallas kernels, call(): pl.pallas_call(skipping, out_shape=out_shape, in_specs=[hbm] * far + [vme...  12.3 us
    ppermute x8, starting transfers between devices, left(): return lax.ppermute(x, axis, [(0, 1), (1, 0), (2, 3), (3, 2)])  11.3 us
    ppermute x8, waiting for transfers between devices, right(): return lax.ppermute(x, axis, [(0, 3), (3, 0), (1, 2), (2, 1)])  8.22 us
    ppermute x8, waiting for transfers between devices, left(): return lax.ppermute(x, axis, [(0, 1), (1, 0), (2, 3), (3, 2)])  3.6 us
    unnamed x10, local copies, waits for them, and re-layouts  2.63 us
  transfers between devices with their start and end apart: 21, of which 7 were waited for; matrix products, arithmetic and copies ran while one was open for 0% of the time, Pallas kernels for 11%

profile of v2, /device:TPU:8, one launch (start us, length us, event | category | flops | bytes accessed | tf_op | source)
XLA Modules:
  0.0 84.2 jit_solution(10711622962659015286)
XLA Ops:
  1.3 1.2 %copy-done = bf16[2048,256]{1,0:T(8,128)(2,1)S(1)} copy-done((bf16[2048,256]{1,0:T(8,128)(2,1)S(1)}, bf16[2048,256]{1,0:T(8,128)(2,1)}, u32[]{:S(2)}) %copy-start) | copy-done | bytes 1048600
  2.6 0.7 copy-done.2
  3.3 0.7 copy-done.4
  3.9 1.1 %shard_map.50 = (f32[256,256]{1,0:T(8,128)S(1)}, f32[256,256]{1,0:T(8,128)S(1)}) custom-call(s32[1,2048]{1,0:T(1,128)S(1)} %bitcast.13, s32[1,2048]{1,0:T(1,128)S(1)} %bitcast.23, bf16[2048,256]{1,0:T(8,128)(2,1)S(1)} %copy-done), custom_call_target="tpu_custom_call" | custom-call | flops 1000 | bytes 1000 | tf_op jit(solution)/shard_map/pallas_call | solution.py:36
  5.1 0.7 shard_map.51
  5.8 1.7 %collective-permute-start.3 = (bf16[256,256]{1,0:T(8,128)(2,1)S(1)}, bf16[256,256]{1,0:T(8,128)(2,1)S(1)}, u32[]{:S(2)}, u32[]{:S(2)}) collective-permute-start(bf16[256,256]{1,0:T(8,128)(2,1)S(1)} %get-tuple-element.28.refs_7_), channel_id=1, source_target_pairs={{0,192},{192,0},{64,128},{128,64},{1,193},{193,1},{65,129},{129,65... | collective-permute-start | bytes 393224 | tf_op jit(solution)/shard_map/ppermute | solution.py:194
  7.5 1.9 %collective-permute-start.4 = (bf16[256,256]{1,0:T(8,128)(2,1)S(1)}, bf16[256,256]{1,0:T(8,128)(2,1)S(1)}, u32[]{:S(2)}, u32[]{:S(2)}) collective-permute-start(bf16[256,256]{1,0:T(8,128)(2,1)S(1)} %get-tuple-element.29.refs_6_), channel_id=1, source_target_pairs={{0,64},{64,0},{128,192},{192,128},{1,65},{65,1},{129,193},{193,129... | collective-permute-start | bytes 393224 | tf_op jit(solution)/shard_map/ppermute | solution.py:190
  9.4 1.2 %shard_map.52 = (bf16[256,256]{1,0:T(8,128)(2,1)S(1)}, bf16[256,256]{1,0:T(8,128)(2,1)S(1)}) custom-call(s32[1,2048]{1,0:T(1,128)S(1)} %bitcast.14, s32[1,2048]{1,0:T(1,128)S(1)} %bitcast.24, bf16[2048,256]{1,0:T(8,128)(2,1)S(1)} %copy-done.1, s32[1,2048]{1,0:T(1,128)S(1)} %collective-permute-done.refs_0_.refs_3_.refs_2_, ...), custom_call_target="tpu_custom_call" | custom-call | flops 4294967296 | bytes 1000 | tf_op jit(solution)/shard_map/pallas_call | solution.py:36
  10.9 1.3 %collective-permute-start.8 = (bf16[256,256]{1,0:T(8,128)(2,1)S(1)}, bf16[256,256]{1,0:T(8,128)(2,1)S(1)}, u32[]{:S(2)}, u32[]{:S(2)}) collective-permute-start(bf16[256,256]{1,0:T(8,128)(2,1)S(1)} %get-tuple-element.31.refs_9_), channel_id=1, source_target_pairs={{0,192},{192,0},{64,128},{128,64},{1,193},{193,1},{65,129},{129,65... | collective-permute-start | bytes 393224 | tf_op jit(solution)/shard_map/ppermute | solution.py:194
  12.2 1.1 %collective-permute-done.4.refs_7_ = bf16[256,256]{1,0:T(8,128)(2,1)S(1)} collective-permute-done((bf16[256,256]{1,0:T(8,128)(2,1)S(1)}, bf16[256,256]{1,0:T(8,128)(2,1)S(1)}, u32[]{:S(2)}, u32[]{:S(2)}) %collective-permute-start.4) | collective-permute-done | bytes 131104 | tf_op jit(solution)/shard_map/ppermute | solution.py:190
  13.3 1.2 %shard_map.53 = (bf16[256,256]{1,0:T(8,128)(2,1)S(1)}, bf16[256,256]{1,0:T(8,128)(2,1)S(1)}) custom-call(s32[1,2048]{1,0:T(1,128)S(1)} %bitcast.15, s32[1,2048]{1,0:T(1,128)S(1)} %bitcast.25, bf16[2048,256]{1,0:T(8,128)(2,1)S(1)} %copy-done.1, s32[1,2048]{1,0:T(1,128)S(1)} %collective-permute-done.refs_0_.refs_3_.refs_2_, ...), custom_call_target="tpu_custom_call" | custom-call | flops 1000 | bytes 1000 | tf_op jit(solution)/shard_map/pallas_call | solution.py:36
  14.5 1.4 %collective-permute-start.6 = (bf16[256,256]{1,0:T(8,128)(2,1)S(1)}, bf16[256,256]{1,0:T(8,128)(2,1)S(1)}, u32[]{:S(2)}, u32[]{:S(2)}) collective-permute-start(bf16[256,256]{1,0:T(8,128)(2,1)S(1)} %get-tuple-element.33.refs_7_), channel_id=1, source_target_pairs={{0,192},{192,0},{64,128},{128,64},{1,193},{193,1},{65,129},{129,65... | collective-permute-start | bytes 393224 | tf_op jit(solution)/shard_map/ppermute | solution.py:194
  15.9 3.1 %collective-permute-start.7 = (bf16[256,256]{1,0:T(8,128)(2,1)S(1)}, bf16[256,256]{1,0:T(8,128)(2,1)S(1)}, u32[]{:S(2)}, u32[]{:S(2)}) collective-permute-start(bf16[256,256]{1,0:T(8,128)(2,1)S(1)} %get-tuple-element.32.refs_6_), channel_id=1, source_target_pairs={{0,64},{64,0},{128,192},{192,128},{1,65},{65,1},{129,193},{193,129... | collective-permute-start | bytes 393224 | tf_op jit(solution)/shard_map/ppermute | solution.py:190
  19.0 1.2 %shard_map.54 = (f32[256,256]{1,0:T(8,128)S(1)}, f32[256,256]{1,0:T(8,128)S(1)}) custom-call(s32[1,2048]{1,0:T(1,128)S(1)} %bitcast.16, s32[1,2048]{1,0:T(1,128)S(1)} %bitcast.26, bf16[2048,256]{1,0:T(8,128)(2,1)S(1)} %copy-done.1, s32[1,2048]{1,0:T(1,128)S(1)} %collective-permute-done.refs_0_.refs_3_.refs_2_, ...), custom_call_target="tpu_custom_call" | custom-call | flops 1000 | bytes 1000 | tf_op jit(solution)/shard_map/pallas_call | solution.py:36
  20.3 1.7 %collective-permute-done.7.refs_4_ = bf16[256,256]{1,0:T(8,128)(2,1)S(1)} collective-permute-done((bf16[256,256]{1,0:T(8,128)(2,1)S(1)}, bf16[256,256]{1,0:T(8,128)(2,1)S(1)}, u32[]{:S(2)}, u32[]{:S(2)}) %collective-permute-start.7) | collective-permute-done | bytes 131104 | tf_op jit(solution)/shard_map/ppermute | solution.py:190
  22.1 17.9 %all_to_all.22 = bf16[8,64,256]{2,1,0:T(8,128)(2,1)S(1)} all-to-all(bf16[8,64,256]{2,1,0:T(8,128)(2,1)S(1)} %bitcast.10), channel_id=1, replica_groups=mesh['y'=4,'z'=8,'core'=2,'feat'=4] {'z'}, dimensions={0} | all-to-all | bytes 524288 | tf_op jit(solution)/shard_map/all_to_all | solution.py:238
  40.0 12.9 %all_to_all.23 = bf16[8,64,256]{2,1,0:T(8,128)(2,1)S(1)} all-to-all(bf16[8,64,256]{2,1,0:T(8,128)(2,1)S(1)} %bitcast.21), channel_id=1, replica_groups=mesh['y'=4,'z'=8,'core'=2,'feat'=4] {'z'}, dimensions={0} | all-to-all | bytes 524288 | tf_op jit(solution)/shard_map/all_to_all | solution.py:244
  52.9 2.2 %collective-permute-start.9 = (bf16[256,256]{1,0:T(8,128)(2,1)S(1)}, bf16[256,256]{1,0:T(8,128)(2,1)S(1)}, u32[]{:S(2)}, u32[]{:S(2)}) collective-permute-start(bf16[256,256]{1,0:T(8,128)(2,1)S(1)} %bitcast.27), channel_id=1, source_target_pairs={{0,64},{64,0},{128,192},{192,128},{1,65},{65,1},{129,193},{193,129... | collective-permute-start | bytes 393224 | tf_op jit(solution)/shard_map/ppermute | solution.py:190
  55.1 1.4 %collective-permute-start.11 = (bf16[256,256]{1,0:T(8,128)(2,1)S(1)}, bf16[256,256]{1,0:T(8,128)(2,1)S(1)}, u32[]{:S(2)}, u32[]{:S(2)}) collective-permute-start(bf16[256,256]{1,0:T(8,128)(2,1)S(1)} %bitcast.29), channel_id=1, source_target_pairs={{0,192},{192,0},{64,128},{128,64},{1,193},{193,1},{65,129},{129,65... | collective-permute-start | bytes 393224 | tf_op jit(solution)/shard_map/ppermute | solution.py:194
  56.5 0.7 collective-permute-start.13
  57.3 0.6 collective-permute-start.14
  57.9 1.3 %shard_map.57 = (bf16[64,2048]{1,0:T(8,128)(2,1)S(1)}, bf16[64,2048]{1,0:T(8,128)(2,1)S(1)}, f32[64,64]{1,0:T(8,128)S(1)}) custom-call(s32[1,2048]{1,0:T(1,128)S(1)} %bitcast.17, bf16[2048,256]{1,0:T(8,128)(2,1)S(1)} %copy-done.1, s32[1,2048]{1,0:T(1,128)S(1)} %collective-permute-done.refs_0_.refs_3_.refs_2_, ...), custom_call_target="tpu_custom_call" | custom-call | flops 1000 | bytes 1000 | tf_op jit(solution)/shard_map/pallas_call | solution.py:36
  59.2 1.5 %collective-permute-start.10 = (bf16[256,256]{1,0:T(8,128)(2,1)S(1)}, bf16[256,256]{1,0:T(8,128)(2,1)S(1)}, u32[]{:S(2)}, u32[]{:S(2)}) collective-permute-start(bf16[256,256]{1,0:T(8,128)(2,1)S(1)} %collective-permute-done.9.refs_4_), channel_id=1, source_target_pairs={{0,192},{192,0},{64,128},{128,64},{1,193},{193,1},{65,129},{129,65... | collective-permute-start | bytes 393224 | tf_op jit(solution)/shard_map/ppermute | solution.py:194
  60.7 2.7 %collective-permute-start.12 = (bf16[256,256]{1,0:T(8,128)(2,1)S(1)}, bf16[256,256]{1,0:T(8,128)(2,1)S(1)}, u32[]{:S(2)}, u32[]{:S(2)}) collective-permute-start(bf16[256,256]{1,0:T(8,128)(2,1)S(1)} %collective-permute-done.11.refs_7_), channel_id=1, source_target_pairs={{0,64},{64,0},{128,192},{192,128},{1,65},{65,1},{129,193},{193,129... | collective-permute-start | bytes 393224 | tf_op jit(solution)/shard_map/ppermute | solution.py:190
  63.4 2.5 %shard_map.58 = (bf16[64,2048]{1,0:T(8,128)(2,1)S(1)}, bf16[64,2048]{1,0:T(8,128)(2,1)S(1)}, f32[64,64]{1,0:T(8,128)S(1)}) custom-call(s32[1,2048]{1,0:T(1,128)S(1)} %bitcast.18, bf16[2048,256]{1,0:T(8,128)(2,1)S(1)} %copy-done.1, s32[1,2048]{1,0:T(1,128)S(1)} %collective-permute-done.refs_0_.refs_3_.refs_2_, ...), custom_call_target="tpu_custom_call" | custom-call | flops 4294967296 | bytes 1000 | tf_op jit(solution)/shard_map/pallas_call | solution.py:36
  66.3 0.8 shard_map.59
  67.7 0.8 shard_map.60.refs_0_
  68.8 2.8 %collective-permute-start.19 = (bf16[64,1152]{1,0:T(8,128)(2,1)S(1)}, bf16[64,1152]{1,0:T(8,128)(2,1)S(1)}, u32[]{:S(2)}, u32[]{:S(2)}) collective-permute-start(bf16[64,1152]{1,0:T(8,128)(2,1)S(1)} %get-tuple-element.46.refs_0_), channel_id=1, source_target_pairs={{0,3},{3,0},{1,2},{2,1},{4,7},{7,4},{5,6},{6,5},{8,11},{11,8},{9,1... | collective-permute-start | bytes 442376 | tf_op jit(solution)/shard_map/ppermute | solution.py:194
  71.9 4.1 %collective-permute-done.19.refs_1_ = bf16[64,1152]{1,0:T(8,128)(2,1)S(1)} collective-permute-done((bf16[64,1152]{1,0:T(8,128)(2,1)S(1)}, bf16[64,1152]{1,0:T(8,128)(2,1)S(1)}, u32[]{:S(2)}, u32[]{:S(2)}) %collective-permute-start.19) | collective-permute-done | bytes 147488 | tf_op jit(solution)/shard_map/ppermute | solution.py:194
  76.9 2.2 %collective-permute-start.18 = (bf16[64,1024]{1,0:T(8,128)(2,1)S(1)}, bf16[64,1024]{1,0:T(8,128)(2,1)S(1)}, u32[]{:S(2)}, u32[]{:S(2)}) collective-permute-start(bf16[64,1024]{1,0:T(8,128)(2,1)S(1)} %shard_map.62.refs_1_), channel_id=1, source_target_pairs={{0,3},{3,0},{1,2},{2,1},{4,7},{7,4},{5,6},{6,5},{8,11},{11,8},{9,1... | collective-permute-start | bytes 393224 | tf_op jit(solution)/shard_map/ppermute | solution.py:194
  79.1 4.1 %collective-permute-done.18.refs_2_ = bf16[64,1024]{1,0:T(8,128)(2,1)S(1)} collective-permute-done((bf16[64,1024]{1,0:T(8,128)(2,1)S(1)}, bf16[64,1024]{1,0:T(8,128)(2,1)S(1)}, u32[]{:S(2)}, u32[]{:S(2)}) %collective-permute-start.18) | collective-permute-done | bytes 131104 | tf_op jit(solution)/shard_map/ppermute | solution.py:194
  83.2 1.0 %shard_map.64 = (bf16[64,256]{1,0:T(8,128)(2,1)}, f32[1,2048]{1,0:T(1,128)}) custom-call(s32[1,2048]{1,0:T(1,128)S(1)} %bitcast.20, bf16[64,1024]{1,0:T(8,128)(2,1)S(1)} %shard_map.62.refs_1_, bf16[64,1024]{1,0:T(8,128)(2,1)S(1)} %collective-permute-done.18.refs_2_, bf16[64,1152]{1,0:T(8,128)(2,1)S(1)} %shard_map.63.refs_3_, ...), custom_call_target="tpu_custom_call" | custom-call | flops 1000 | bytes 1000 | tf_op jit(solution)/shard_map/pallas_call | solution.py:36
  (38 shorter events, 3.7 us)
Async XLA Ops:
  0.6 4.5 %collective-permute-start.2 = (bf16[2048,256]{1,0:T(8,128)(2,1)}, bf16[2048,256]{1,0:T(8,128)(2,1)S(1)}, u32[]{:S(2)}, u32[]{:S(2)}) collective-permute-start(bf16[2048,256]{1,0:T(8,128)(2,1)} %refs_1_.5), channel_id=1, source_target_pairs={{0,4},{4,0},{1,5},{5,1},{2,6},{6,2},{3,7},{7,3},{8,12},{12,8},{9,1... | collective-permute-start | bytes 3145736 | tf_op jit(solution)/shard_map/ppermute | solution.py:186
  0.7 4.4 %collective-permute-start = (s32[1,2048]{1,0:T(1,128)}, s32[1,2048]{1,0:T(1,128)S(1)}, u32[]{:S(2)}, u32[]{:S(2)}) collective-permute-start(s32[1,2048]{1,0:T(1,128)} %bitcast.12), channel_id=1, source_target_pairs={{0,4},{4,0},{1,5},{5,1},{2,6},{6,2},{3,7},{7,3},{8,12},{12,8},{9,1... | collective-permute-start | bytes 24584 | tf_op jit(solution)/shard_map/ppermute | solution.py:186
  1.2 3.9 %collective-permute-start.1 = (s32[1,2048]{1,0:T(1,128)}, s32[1,2048]{1,0:T(1,128)S(1)}, u32[]{:S(2)}, u32[]{:S(2)}) collective-permute-start(s32[1,2048]{1,0:T(1,128)} %bitcast.22), channel_id=1, source_target_pairs={{0,4},{4,0},{1,5},{5,1},{2,6},{6,2},{3,7},{7,3},{8,12},{12,8},{9,1... | collective-permute-start | bytes 24584 | tf_op jit(solution)/shard_map/ppermute | solution.py:186
  1.3 1.2 %copy-start = (bf16[2048,256]{1,0:T(8,128)(2,1)S(1)}, bf16[2048,256]{1,0:T(8,128)(2,1)}, u32[]{:S(2)}) copy-start(bf16[2048,256]{1,0:T(8,128)(2,1)} %refs_1_.5) | copy-start | bytes 3145732
  2.6 0.7 copy-start.2
  3.3 0.7 copy-start.4
  5.1 4.3 %copy-start.1 = (bf16[2048,256]{1,0:T(8,128)(2,1)S(1)}, bf16[2048,256]{1,0:T(8,128)(2,1)}, u32[]{:S(2)}) copy-start(bf16[2048,256]{1,0:T(8,128)(2,1)} %refs_1_.5) | copy-start | bytes 3145732
  5.1 4.3 %copy-start.3 = (s32[2048,1]{0,1:T(1,128)S(1)}, s32[2048,1]{0,1:T(1,128)}, u32[]{:S(2)}) copy-start(s32[2048,1]{0,1:T(1,128)} %param.4) | copy-start | bytes 24580
  5.8 6.3 %collective-permute-start.3 = (bf16[256,256]{1,0:T(8,128)(2,1)S(1)}, bf16[256,256]{1,0:T(8,128)(2,1)S(1)}, u32[]{:S(2)}, u32[]{:S(2)}) collective-permute-start(bf16[256,256]{1,0:T(8,128)(2,1)S(1)} %get-tuple-element.28.refs_7_), channel_id=1, source_target_pairs={{0,192},{192,0},{64,128},{128,64},{1,193},{193,1},{65,129},{129,65... | collective-permute-start | bytes 393224 | tf_op jit(solution)/shard_map/ppermute | solution.py:194
  7.5 5.7 %collective-permute-start.4 = (bf16[256,256]{1,0:T(8,128)(2,1)S(1)}, bf16[256,256]{1,0:T(8,128)(2,1)S(1)}, u32[]{:S(2)}, u32[]{:S(2)}) collective-permute-start(bf16[256,256]{1,0:T(8,128)(2,1)S(1)} %get-tuple-element.29.refs_6_), channel_id=1, source_target_pairs={{0,64},{64,0},{128,192},{192,128},{1,65},{65,1},{129,193},{193,129... | collective-permute-start | bytes 393224 | tf_op jit(solution)/shard_map/ppermute | solution.py:190
  10.7 9.6 %collective-permute-start.5 = (bf16[256,256]{1,0:T(8,128)(2,1)S(1)}, bf16[256,256]{1,0:T(8,128)(2,1)S(1)}, u32[]{:S(2)}, u32[]{:S(2)}) collective-permute-start(bf16[256,256]{1,0:T(8,128)(2,1)S(1)} %get-tuple-element.30.refs_8_), channel_id=1, source_target_pairs={{0,64},{64,0},{128,192},{192,128},{1,65},{65,1},{129,193},{193,129... | collective-permute-start | bytes 393224 | tf_op jit(solution)/shard_map/ppermute | solution.py:190
  10.9 9.4 %collective-permute-start.8 = (bf16[256,256]{1,0:T(8,128)(2,1)S(1)}, bf16[256,256]{1,0:T(8,128)(2,1)S(1)}, u32[]{:S(2)}, u32[]{:S(2)}) collective-permute-start(bf16[256,256]{1,0:T(8,128)(2,1)S(1)} %get-tuple-element.31.refs_9_), channel_id=1, source_target_pairs={{0,192},{192,0},{64,128},{128,64},{1,193},{193,1},{65,129},{129,65... | collective-permute-start | bytes 393224 | tf_op jit(solution)/shard_map/ppermute | solution.py:194
  14.5 5.8 %collective-permute-start.6 = (bf16[256,256]{1,0:T(8,128)(2,1)S(1)}, bf16[256,256]{1,0:T(8,128)(2,1)S(1)}, u32[]{:S(2)}, u32[]{:S(2)}) collective-permute-start(bf16[256,256]{1,0:T(8,128)(2,1)S(1)} %get-tuple-element.33.refs_7_), channel_id=1, source_target_pairs={{0,192},{192,0},{64,128},{128,64},{1,193},{193,1},{65,129},{129,65... | collective-permute-start | bytes 393224 | tf_op jit(solution)/shard_map/ppermute | solution.py:194
  15.9 6.0 %collective-permute-start.7 = (bf16[256,256]{1,0:T(8,128)(2,1)S(1)}, bf16[256,256]{1,0:T(8,128)(2,1)S(1)}, u32[]{:S(2)}, u32[]{:S(2)}) collective-permute-start(bf16[256,256]{1,0:T(8,128)(2,1)S(1)} %get-tuple-element.32.refs_6_), channel_id=1, source_target_pairs={{0,64},{64,0},{128,192},{192,128},{1,65},{65,1},{129,193},{193,129... | collective-permute-start | bytes 393224 | tf_op jit(solution)/shard_map/ppermute | solution.py:190
  52.9 6.3 %collective-permute-start.9 = (bf16[256,256]{1,0:T(8,128)(2,1)S(1)}, bf16[256,256]{1,0:T(8,128)(2,1)S(1)}, u32[]{:S(2)}, u32[]{:S(2)}) collective-permute-start(bf16[256,256]{1,0:T(8,128)(2,1)S(1)} %bitcast.27), channel_id=1, source_target_pairs={{0,64},{64,0},{128,192},{192,128},{1,65},{65,1},{129,193},{193,129... | collective-permute-start | bytes 393224 | tf_op jit(solution)/shard_map/ppermute | solution.py:190
  55.1 5.6 %collective-permute-start.11 = (bf16[256,256]{1,0:T(8,128)(2,1)S(1)}, bf16[256,256]{1,0:T(8,128)(2,1)S(1)}, u32[]{:S(2)}, u32[]{:S(2)}) collective-permute-start(bf16[256,256]{1,0:T(8,128)(2,1)S(1)} %bitcast.29), channel_id=1, source_target_pairs={{0,192},{192,0},{64,128},{128,64},{1,193},{193,1},{65,129},{129,65... | collective-permute-start | bytes 393224 | tf_op jit(solution)/shard_map/ppermute | solution.py:194
  56.5 6.8 %collective-permute-start.13 = (bf16[256,256]{1,0:T(8,128)(2,1)S(1)}, bf16[256,256]{1,0:T(8,128)(2,1)S(1)}, u32[]{:S(2)}, u32[]{:S(2)}) collective-permute-start(bf16[256,256]{1,0:T(8,128)(2,1)S(1)} %bitcast.30), channel_id=1, source_target_pairs={{0,64},{64,0},{128,192},{192,128},{1,65},{65,1},{129,193},{193,129... | collective-permute-start | bytes 393224 | tf_op jit(solution)/shard_map/ppermute | solution.py:190
  57.3 6.1 %collective-permute-start.14 = (bf16[256,256]{1,0:T(8,128)(2,1)S(1)}, bf16[256,256]{1,0:T(8,128)(2,1)S(1)}, u32[]{:S(2)}, u32[]{:S(2)}) collective-permute-start(bf16[256,256]{1,0:T(8,128)(2,1)S(1)} %bitcast.28), channel_id=1, source_target_pairs={{0,192},{192,0},{64,128},{128,64},{1,193},{193,1},{65,129},{129,65... | collective-permute-start | bytes 393224 | tf_op jit(solution)/shard_map/ppermute | solution.py:194
  59.2 6.7 %collective-permute-start.10 = (bf16[256,256]{1,0:T(8,128)(2,1)S(1)}, bf16[256,256]{1,0:T(8,128)(2,1)S(1)}, u32[]{:S(2)}, u32[]{:S(2)}) collective-permute-start(bf16[256,256]{1,0:T(8,128)(2,1)S(1)} %collective-permute-done.9.refs_4_), channel_id=1, source_target_pairs={{0,192},{192,0},{64,128},{128,64},{1,193},{193,1},{65,129},{129,65... | collective-permute-start | bytes 393224 | tf_op jit(solution)/shard_map/ppermute | solution.py:194
  60.7 5.6 %collective-permute-start.12 = (bf16[256,256]{1,0:T(8,128)(2,1)S(1)}, bf16[256,256]{1,0:T(8,128)(2,1)S(1)}, u32[]{:S(2)}, u32[]{:S(2)}) collective-permute-start(bf16[256,256]{1,0:T(8,128)(2,1)S(1)} %collective-permute-done.11.refs_7_), channel_id=1, source_target_pairs={{0,64},{64,0},{128,192},{192,128},{1,65},{65,1},{129,193},{193,129... | collective-permute-start | bytes 393224 | tf_op jit(solution)/shard_map/ppermute | solution.py:190
  67.1 1.7 %collective-permute-start.15 = (bf16[64,2048]{1,0:T(8,128)(2,1)S(1)}, bf16[64,2048]{1,0:T(8,128)(2,1)S(1)}, u32[]{:S(2)}, u32[]{:S(2)}) collective-permute-start(bf16[64,2048]{1,0:T(8,128)(2,1)S(1)} %get-tuple-element.43.refs_5_), channel_id=1, source_target_pairs={{0,4},{4,0},{1,5},{5,1},{2,6},{6,2},{3,7},{7,3},{8,12},{12,8},{9,1... | collective-permute-start | bytes 786440 | tf_op jit(solution)/shard_map/ppermute | solution.py:186
  67.2 1.6 %collective-permute-start.16 = (f32[64,64]{1,0:T(8,128)S(1)}, f32[64,64]{1,0:T(8,128)S(1)}, u32[]{:S(2)}, u32[]{:S(2)}) collective-permute-start(f32[64,64]{1,0:T(8,128)S(1)} %get-tuple-element.44.refs_2_), channel_id=1, source_target_pairs={{0,4},{4,0},{1,5},{5,1},{2,6},{6,2},{3,7},{7,3},{8,12},{12,8},{9,1... | collective-permute-start | bytes 49160 | tf_op jit(solution)/shard_map/ppermute | solution.py:186
  68.8 7.1 %collective-permute-start.19 = (bf16[64,1152]{1,0:T(8,128)(2,1)S(1)}, bf16[64,1152]{1,0:T(8,128)(2,1)S(1)}, u32[]{:S(2)}, u32[]{:S(2)}) collective-permute-start(bf16[64,1152]{1,0:T(8,128)(2,1)S(1)} %get-tuple-element.46.refs_0_), channel_id=1, source_target_pairs={{0,3},{3,0},{1,2},{2,1},{4,7},{7,4},{5,6},{6,5},{8,11},{11,8},{9,1... | collective-permute-start | bytes 442376 | tf_op jit(solution)/shard_map/ppermute | solution.py:194
  71.7 5.3 %collective-permute-start.17 = (bf16[64,1024]{1,0:T(8,128)(2,1)S(1)}, bf16[64,1024]{1,0:T(8,128)(2,1)S(1)}, u32[]{:S(2)}, u32[]{:S(2)}) collective-permute-start(bf16[64,1024]{1,0:T(8,128)(2,1)S(1)} %get-tuple-element.45.refs_0_), channel_id=1, source_target_pairs={{0,1},{1,0},{2,3},{3,2},{4,5},{5,4},{6,7},{7,6},{8,9},{9,8},{10,11... | collective-permute-start | bytes 393224 | tf_op jit(solution)/shard_map/ppermute | solution.py:190
  76.2 7.0 %collective-permute-start.20 = (bf16[64,1152]{1,0:T(8,128)(2,1)S(1)}, bf16[64,1152]{1,0:T(8,128)(2,1)S(1)}, u32[]{:S(2)}, u32[]{:S(2)}) collective-permute-start(bf16[64,1152]{1,0:T(8,128)(2,1)S(1)} %shard_map.63.refs_3_), channel_id=1, source_target_pairs={{0,1},{1,0},{2,3},{3,2},{4,5},{5,4},{6,7},{7,6},{8,9},{9,8},{10,11... | collective-permute-start | bytes 442376 | tf_op jit(solution)/shard_map/ppermute | solution.py:190
  76.9 6.3 %collective-permute-start.18 = (bf16[64,1024]{1,0:T(8,128)(2,1)S(1)}, bf16[64,1024]{1,0:T(8,128)(2,1)S(1)}, u32[]{:S(2)}, u32[]{:S(2)}) collective-permute-start(bf16[64,1024]{1,0:T(8,128)(2,1)S(1)} %shard_map.62.refs_1_), channel_id=1, source_target_pairs={{0,3},{3,0},{1,2},{2,1},{4,7},{7,4},{5,6},{6,5},{8,11},{11,8},{9,1... | collective-permute-start | bytes 393224 | tf_op jit(solution)/shard_map/ppermute | solution.py:194

commit v3 on v2

v3 whole, which is shorter than its diff:
```python
import functools

import jax
import jax.numpy as jnp
from jax import lax
from jax.experimental import pallas as pl
from jax.experimental.pallas import tpu as pltpu
from jax.sharding import Mesh, PartitionSpec as P

D = 1024
K = 64
EPS = 1e-06
NY, NZ, NC, NX = 4, 8, 2, 4
PARENTS = NY * NZ * NC
ROWS = 2048
WIDTH = 256
PIECE = NZ * K
HALF = PIECE // 2
SPLIT = ROWS // 2
BLOCK = 512
VMEM = 24 * 1024 * 1024
LONG = 1 << 32

F32 = jnp.float32
BF16 = jnp.bfloat16


def call(kernel, out_shape, operands, behind=(), flops=1000):
    vmem = pl.BlockSpec(memory_space=pltpu.VMEM)
    count = len(operands)

    def skipping(*refs):
        kernel(*refs[:count], *refs[count + len(behind) :])

    return pl.pallas_call(
        skipping,
        out_shape=out_shape,
        in_specs=[vmem] * (count + len(behind)),
        out_specs=jax.tree.map(lambda _: vmem, out_shape),
        compiler_params=pltpu.CompilerParams(vmem_limit_bytes=VMEM),
        cost_estimate=pl.CostEstimate(flops=flops, bytes_accessed=1000, transcendentals=0),
    )(*operands, *behind)


def add_members(totals, halves, codes, rows, start):
    y, core = lax.axis_index("y"), lax.axis_index("core")
    span = slice(start, start + BLOCK)
    code = codes[:, span]
    parent = code >> 6
    block = rows[span, :]
    child = lax.broadcasted_iota(jnp.int32, (HALF, BLOCK), 0)
    for number, (k, upper) in enumerate(halves):
        inside = ((parent >> 4) == (y ^ k)) & ((parent & 1) == core)
        local = jnp.where(inside, ((parent >> 1) & 7) * K + (code & (K - 1)) - upper * HALF, -1)
        member = (child == local).astype(F32).astype(BF16)
        totals[number] += jnp.dot(member, block, preferred_element_type=F32)


def sums_kernel(halves, groups, *refs):
    outs, so_far = refs[-len(halves) :], refs[2 * groups : -len(halves)]
    totals = [x[...].astype(F32) for x in so_far] or [jnp.zeros((HALF, WIDTH), F32) for _ in halves]
    for group in range(groups):
        for start in range(0, ROWS, BLOCK):
            add_members(totals, halves, *refs[2 * group : 2 * group + 2], start)
    for out, total in zip(outs, totals):
        out[...] = total.astype(out.dtype)


def hand_on_kernel(own_ref, got_ref, out_ref):
    out_ref[...] = (own_ref[...] + got_ref[...].astype(F32)).astype(BF16)


def merge_kernel(low_ref, high_ref, low_a, low_b, high_a, high_b, out_ref):
    out_ref[:HALF, :] = (low_ref[...] + low_a[...].astype(F32) + low_b[...].astype(F32)).astype(BF16)
    out_ref[HALF:, :] = (high_ref[...] + high_a[...].astype(F32) + high_b[...].astype(F32)).astype(BF16)


def totals_kernel(parts_ref, totals_ref, copies_ref):
    total = parts_ref[0:K, :].astype(F32)
    for z in range(1, NZ):
        total += parts_ref[z * K : (z + 1) * K, :].astype(F32)
    totals_ref[...] = total
    rounded = total.astype(BF16)
    for z in range(NZ):
        copies_ref[z * K : (z + 1) * K, :] = rounded


def scores_kernel(groups, blocks, first, with_squares, packed, span, *refs):
    y, core = lax.axis_index("y"), lax.axis_index("core")
    group_refs, refs = refs[: 2 * groups], refs[2 * groups :]
    block_refs, refs = refs[: len(blocks)], refs[len(blocks) :]
    numbers = [(y ^ k) * 16 + 2 * z + core for k, z, _ in blocks]
    scores_in = squares_in = None
    if not first:
        scores_in, refs = refs[:groups], refs[groups:]
        if with_squares:
            squares_in, refs = refs[0], refs[1:]
    if with_squares:
        lane = lax.broadcasted_iota(jnp.int32, (K, PARENTS), 1)
        squares = jnp.zeros((K, PARENTS), F32) if first else squares_in[...]
        for number, block_ref, (_, _, count) in zip(numbers, block_refs, blocks):
            for z in range(count):
                block = block_ref[z * K : (z + 1) * K, :].astype(F32)
                square = jnp.sum(block * block, axis=1, keepdims=True)
                squares = jnp.where(lane == number + 2 * z, square, squares)
        if packed:
            put_squares(refs[0], squares, SPLIT)
        else:
            refs[groups][...] = squares
    for group in range(groups):
        codes, rows_ref = group_refs[2 * group : 2 * group + 2]
        for start in range(*span, BLOCK):
            part = slice(start, start + BLOCK)
            rows, parent = rows_ref[part, :], codes[:, part] >> 6
            chosen = jnp.zeros((K, BLOCK), F32) if first else scores_in[group][:, part].astype(F32)
            for number, block_ref, (_, _, count) in zip(numbers, block_refs, blocks):
                product = lax.dot_general(
                    block_ref[...], rows, (((1,), (1,)), ((), ())), preferred_element_type=F32
                )
                for z in range(count):
                    chosen = jnp.where(parent == number + 2 * z, product[z * K : (z + 1) * K, :], chosen)
            refs[group][:, start - span[0] : start - span[0] + BLOCK] = chosen.astype(BF16)


def put_squares(out_ref, squares, at):
    high = squares.astype(BF16)
    out_ref[:, at : at + PARENTS] = high
    out_ref[:, at + PARENTS : at + 2 * PARENTS] = (squares - high.astype(F32)).astype(BF16)


def get_squares(ref, at):
    return ref[:, at : at + PARENTS].astype(F32) + ref[:, at + PARENTS : at + 2 * PARENTS].astype(F32)


def join_kernel(own_ref, sent_ref, arrived_ref, out_ref):
    out_ref[:, :SPLIT] = own_ref[...] + arrived_ref[:, :SPLIT]
    if out_ref.shape[1] > SPLIT:
        out_ref[:, SPLIT:] = sent_ref[:, SPLIT:] + arrived_ref[:, SPLIT:]


def add_kernel(x_ref, y_ref, out_ref):
    scores = x_ref[:, :SPLIT].astype(F32) + y_ref[:, :SPLIT].astype(F32)
    out_ref[:, :SPLIT] = scores.astype(BF16)
    if out_ref.shape[1] > SPLIT:
        put_squares(out_ref, get_squares(x_ref, SPLIT) + get_squares(y_ref, SPLIT), SPLIT)


def best_rows(code_ref, at, x_ref, y_ref, scale, fit_ref):
    high = scale.astype(BF16)
    low = (scale - high.astype(F32)).astype(BF16)
    for start in range(0, SPLIT, BLOCK):
        part = slice(start, start + BLOCK)
        parent = code_ref[:, at + start : at + start + BLOCK] >> 6
        number = lax.broadcasted_iota(jnp.int32, (PARENTS, BLOCK), 0)
        chosen = (number == parent).astype(F32).astype(BF16)
        factor = jnp.dot(high, chosen, preferred_element_type=F32) + jnp.dot(
            low, chosen, preferred_element_type=F32
        )
        scores = x_ref[:, part].astype(F32) + y_ref[:, part].astype(F32)
        fit_ref[:, at + start : at + start + BLOCK] = jnp.max(scores * factor, axis=0, keepdims=True) / (
            0.25 * D
        )


def finish_first_kernel(code_ref, x_ref, y_ref, totals_ref, scale_ref, centroids_ref, fit_ref):
    y, z, core = lax.axis_index("y"), lax.axis_index("z"), lax.axis_index("core")
    scale = lax.rsqrt((get_squares(x_ref, SPLIT) + get_squares(y_ref, SPLIT)) / D + EPS)
    scale_ref[...] = scale
    lane = lax.broadcasted_iota(jnp.int32, (K, PARENTS), 1)
    own = jnp.sum(jnp.where(lane == y * 16 + z * 2 + core, scale, 0.0), axis=1, keepdims=True)
    centroids_ref[...] = (totals_ref[...] * own).astype(BF16)
    best_rows(code_ref, 0, x_ref, y_ref, scale, fit_ref)


def finish_kernel(code_ref, x_ref, y_ref, scale_ref, first_ref, fit_ref):
    fit_ref[:, :SPLIT] = first_ref[...]
    best_rows(code_ref, SPLIT, x_ref, y_ref, scale_ref[...], fit_ref)


def swap(x):
    return lax.ppermute(x, "core", [(0, 1), (1, 0)])


def left(x, axis):
    return lax.ppermute(x, axis, [(0, 1), (1, 0), (2, 3), (3, 2)])


def right(x, axis):
    return lax.ppermute(x, axis, [(0, 3), (3, 0), (1, 2), (2, 1)])


def body(embeddings, parent_ids, child_assignment):
    code = parent_ids.reshape(1, ROWS) * K + child_assignment.reshape(1, ROWS)
    own = (code, embeddings)
    other = tuple(swap(x) for x in own)

    def halves_of(dtype):
        return (jax.ShapeDtypeStruct((HALF, WIDTH), dtype),) * 2

    def sums(halves, dtype, groups, so_far=(), behind=(), flops=1000):
        return call(
            functools.partial(sums_kernel, halves, len(groups)),
            halves_of(dtype),
            [x for group in groups for x in group] + list(so_far),
            behind=behind,
            flops=flops,
        )

    halves = ((2, 0), (2, 1))
    far_low, far_high = sums(halves, BF16, [other], sums(halves, F32, [own]))
    got_low, got_high = left(far_low, "y"), right(far_high, "y")
    left_low, right_high = sums(((1, 0), (3, 1)), BF16, [own, other], behind=[far_low, far_high], flops=LONG)
    own_high, own_low = sums(((1, 1), (3, 0)), F32, [own, other], behind=[left_low, right_high])
    half = jax.ShapeDtypeStruct((HALF, WIDTH), BF16)
    right_low = call(hand_on_kernel, half, [own_low, got_low])
    left_high = call(hand_on_kernel, half, [own_high, got_high])
    kept = sums(((0, 0), (0, 1)), F32, [own, other], behind=[left_high, right_low])
    merged = call(
        merge_kernel,
        jax.ShapeDtypeStruct((PIECE, WIDTH), BF16),
        [*kept, left(left_low, "y"), right(right_low, "y"), left(left_high, "y"), right(right_high, "y")],
    )
    parts = lax.all_to_all(merged, "z", 0, 0, tiled=True)
    totals, copies = call(
        totals_kernel,
        (jax.ShapeDtypeStruct((K, WIDTH), F32), jax.ShapeDtypeStruct((PIECE, WIDTH), BF16)),
        [parts],
    )
    mine = lax.all_to_all(copies, "z", 0, 0, tiled=True)

    low, high = mine[:HALF], mine[HALF:]
    left_low, right_high = left(low, "y"), right(high, "y")
    left_high, right_low = left(high, "y"), right(low, "y")
    far_low, far_high = right(left_low, "y"), left(right_high, "y")

    plain = jax.ShapeDtypeStruct((K, ROWS), BF16)
    squared = jax.ShapeDtypeStruct((K, PARENTS), F32)
    blocks = ((0, 0, NZ), (1, 0, 4), (1, 4, 4), (3, 0, 4), (3, 4, 4))
    state = call(
        functools.partial(scores_kernel, 2, blocks, True, True, False, (0, ROWS)),
        (plain, plain, squared),
        [*own, *other, mine, left_low, left_high, right_low, right_high],
        flops=LONG,
    )
    blocks = ((2, 0, 4), (2, 4, 4))
    message = jax.ShapeDtypeStruct((K, SPLIT), BF16)
    long_message = jax.ShapeDtypeStruct((K, SPLIT + 2 * PARENTS), BF16)
    spans = ((0, SPLIT), (SPLIT, ROWS))
    (sent_a,) = call(
        functools.partial(scores_kernel, 1, blocks, False, True, True, spans[0]),
        (long_message,),
        [*other, far_low, far_high, *state[1:]],
    )
    (sent_b,) = call(
        functools.partial(scores_kernel, 1, blocks, False, False, False, spans[1]),
        (message,),
        [*other, far_low, far_high, state[1]],
        behind=[sent_a],
    )
    got_a, got_b = swap(sent_a), swap(sent_b)
    (kept_a,) = call(
        functools.partial(scores_kernel, 1, blocks, False, False, False, spans[0]),
        (message,),
        [*own, far_low, far_high, state[0]],
        behind=[sent_b],
    )
    a = call(join_kernel, long_message, [kept_a, sent_a, got_a])
    (kept_b,) = call(
        functools.partial(scores_kernel, 1, blocks, False, False, False, spans[1]),
        (message,),
        [*own, far_low, far_high, state[0]],
        behind=[a],
    )
    b = call(join_kernel, message, [kept_b, sent_b, got_b])

    a = call(add_kernel, long_message, [a, left(a, "feat")])
    b = call(add_kernel, message, [b, right(b, "feat")])
    scale, centroids, first = call(
        finish_first_kernel,
        (
            jax.ShapeDtypeStruct((K, PARENTS), F32),
            jax.ShapeDtypeStruct((K, WIDTH), BF16),
            jax.ShapeDtypeStruct((1, SPLIT), F32),
        ),
        [code, a, right(a, "feat"), totals],
    )
    fit = call(
        finish_kernel, jax.ShapeDtypeStruct((1, ROWS), F32), [code, b, left(b, "feat"), scale, first]
    )
    return centroids, fit.reshape(ROWS)


def solution(mesh):
    split = Mesh(mesh.devices.reshape(NY, NZ, NC, NX), ("y", "z", "core", "feat"))
    rows = ("y", "z", "core")
    in_specs = (P(rows, "feat"), P(rows, None), P(rows))
    out_specs = (P(rows, "feat"), P(rows))
    return jax.shard_map(body, mesh=split, in_specs=in_specs, out_specs=out_specs, check_vma=False)
```

time: 85.4 us -> 82.4 us (0.965)
  waiting for transfers between devices: 12.1 us -> 9.04 us
  local copies, waits for them, and re-layouts: 2.65 us -> 1.25 us
    ppermute x8, starting transfers between devices: 11.3 us -> 14.6 us  [left(): return lax.ppermute(x, axis, [(0, 1), (1, 0), (2, 3), (3, 2)])]
    ppermute x8, starting transfers between devices: 12.9 us -> 9.92 us  [right(): return lax.ppermute(x, axis, [(0, 3), (3, 0), (1, 2), (2, 1)])]
    ppermute x8, waiting for transfers between devices: 8.22 us -> 6.03 us  [right(): return lax.ppermute(x, axis, [(0, 3), (3, 0), (1, 2), (2, 1)])]
    unnamed x10 -> x6, local copies, waits for them, and re-layouts: 2.63 us -> 1.23 us
    all_to_all x1, blocking collectives: 17.9 us -> 18.7 us  [body(): parts = lax.all_to_all(merged, 'z', 0, 0, tiled=True)]
    pallas_call x15 -> x20, Pallas kernels: 12.3 us -> 12.7 us  [call(): pl.pallas_call(skipping, out_shape=out_shape, in_specs=[vmem] * (count +...]
  transfers between devices with their start and end apart: 21 -> 20, of which waited for: 7 -> 7; matrix products, arithmetic and copies ran while one was open for 0% -> 1% of each run, Pallas kernels for 11% -> 13%
where the time goes in v3:
time: 82.4 us; the launch traced here: 82 us
  blocking collectives  31.6 us (38%)
  starting transfers between devices  25.8 us (31%)
  Pallas kernels  12.7 us (15%)
  waiting for transfers between devices  9.04 us (11%)
  local copies, waits for them, and re-layouts  1.25 us (2%)
  between operations  0.87 us (1%)
    all_to_all x1, blocking collectives, body(): parts = lax.all_to_all(merged, 'z', 0, 0, tiled=True)  18.7 us
    ppermute x8, starting transfers between devices, left(): return lax.ppermute(x, axis, [(0, 1), (1, 0), (2, 3), (3, 2)])  14.6 us
    all_to_all x1, blocking collectives, body(): mine = lax.all_to_all(copies, 'z', 0, 0, tiled=True)  12.9 us
    pallas_call x20, Pallas kernels, call(): pl.pallas_call(skipping, out_shape=out_shape, in_specs=[vmem] * (count +...  12.7 us
    ppermute x8, starting transfers between devices, right(): return lax.ppermute(x, axis, [(0, 3), (3, 0), (1, 2), (2, 1)])  9.92 us
    ppermute x8, waiting for transfers between devices, right(): return lax.ppermute(x, axis, [(0, 3), (3, 0), (1, 2), (2, 1)])  6.03 us
    ppermute x8, waiting for transfers between devices, left(): return lax.ppermute(x, axis, [(0, 1), (1, 0), (2, 3), (3, 2)])  3 us
  transfers between devices with their start and end apart: 20, of which 7 were waited for; matrix products, arithmetic and copies ran while one was open for 1% of the time, Pallas kernels for 13%

profile of v3, /device:TPU:8, one launch (start us, length us, event | category | flops | bytes accessed | tf_op | source)
XLA Modules:
  0.0 82.0 jit_solution(1694017878998390124)
XLA Ops:
  0.7 0.7 broadcast_multiply_fusion
  1.5 0.6 collective-permute-start
  2.0 1.2 %copy-done = bf16[2048,256]{1,0:T(8,128)(2,1)S(1)} copy-done((bf16[2048,256]{1,0:T(8,128)(2,1)S(1)}, bf16[2048,256]{1,0:T(8,128)(2,1)}, u32[]{:S(2)}) %copy-start) | copy-done | bytes 1048600
  3.3 0.7 shard_map.50
  4.0 0.7 shard_map.51
  4.7 2.3 %collective-permute-start.3 = (bf16[256,256]{1,0:T(8,128)(2,1)S(1)}, bf16[256,256]{1,0:T(8,128)(2,1)S(1)}, u32[]{:S(2)}, u32[]{:S(2)}) collective-permute-start(bf16[256,256]{1,0:T(8,128)(2,1)S(1)} %get-tuple-element.22.refs_4_), channel_id=1, source_target_pairs={{0,64},{64,0},{128,192},{192,128},{1,65},{65,1},{129,193},{193,129... | collective-permute-start | bytes 393224 | tf_op jit(solution)/shard_map/ppermute | solution.py:185
  7.0 0.7 collective-permute-start.2
  7.7 1.2 %shard_map.52 = (bf16[256,256]{1,0:T(8,128)(2,1)S(1)}, bf16[256,256]{1,0:T(8,128)(2,1)S(1)}) custom-call(s32[1,2048]{1,0:T(1,128)S(1)} %bitcast.14, bf16[2048,256]{1,0:T(8,128)(2,1)S(1)} %copy-done.1, s32[1,2048]{1,0:T(1,128)S(1)} %collective-permute-done.refs_0_.refs_2_, bf16[2048,256]{1,0:T(8,128)(2,1)S(1)} %collective-permute-done.1.refs_1_.refs_3_, ...), custom_call_target="tpu_custom_call" | custom-call | flops 4294967296 | bytes 1000 | tf_op jit(solution)/shard_map/pallas_call | solution.py:35
  8.9 1.4 %collective-permute-start.4 = (bf16[256,256]{1,0:T(8,128)(2,1)S(1)}, bf16[256,256]{1,0:T(8,128)(2,1)S(1)}, u32[]{:S(2)}, u32[]{:S(2)}) collective-permute-start(bf16[256,256]{1,0:T(8,128)(2,1)S(1)} %get-tuple-element.24.refs_4_), channel_id=1, source_target_pairs={{0,64},{64,0},{128,192},{192,128},{1,65},{65,1},{129,193},{193,129... | collective-permute-start | bytes 393224 | tf_op jit(solution)/shard_map/ppermute | solution.py:185
  10.4 0.7 collective-permute-start.7
  11.1 1.2 %shard_map.53 = (f32[256,256]{1,0:T(8,128)S(1)}, f32[256,256]{1,0:T(8,128)S(1)}) custom-call(s32[1,2048]{1,0:T(1,128)S(1)} %bitcast.15, bf16[2048,256]{1,0:T(8,128)(2,1)S(1)} %copy-done.1, s32[1,2048]{1,0:T(1,128)S(1)} %collective-permute-done.refs_0_.refs_2_, bf16[2048,256]{1,0:T(8,128)(2,1)S(1)} %collective-permute-done.1.refs_1_.refs_3_, ...), custom_call_target="tpu_custom_call" | custom-call | flops 1000 | bytes 1000 | tf_op jit(solution)/shard_map/pallas_call | solution.py:35
  12.4 1.4 %collective-permute-start.5 = (bf16[256,256]{1,0:T(8,128)(2,1)S(1)}, bf16[256,256]{1,0:T(8,128)(2,1)S(1)}, u32[]{:S(2)}, u32[]{:S(2)}) collective-permute-start(bf16[256,256]{1,0:T(8,128)(2,1)S(1)} %shard_map.55.refs_5_), channel_id=1, source_target_pairs={{0,192},{192,0},{64,128},{128,64},{1,193},{193,1},{65,129},{129,65... | collective-permute-start | bytes 393224 | tf_op jit(solution)/shard_map/ppermute | solution.py:189
  13.8 2.0 %collective-permute-start.6 = (bf16[256,256]{1,0:T(8,128)(2,1)S(1)}, bf16[256,256]{1,0:T(8,128)(2,1)S(1)}, u32[]{:S(2)}, u32[]{:S(2)}) collective-permute-start(bf16[256,256]{1,0:T(8,128)(2,1)S(1)} %shard_map.54.refs_4_), channel_id=1, source_target_pairs={{0,64},{64,0},{128,192},{192,128},{1,65},{65,1},{129,193},{193,129... | collective-permute-start | bytes 393224 | tf_op jit(solution)/shard_map/ppermute | solution.py:185
  15.8 1.2 %shard_map.56 = (f32[256,256]{1,0:T(8,128)S(1)}, f32[256,256]{1,0:T(8,128)S(1)}) custom-call(s32[1,2048]{1,0:T(1,128)S(1)} %bitcast.16, bf16[2048,256]{1,0:T(8,128)(2,1)S(1)} %copy-done.1, s32[1,2048]{1,0:T(1,128)S(1)} %collective-permute-done.refs_0_.refs_2_, bf16[2048,256]{1,0:T(8,128)(2,1)S(1)} %collective-permute-done.1.refs_1_.refs_3_, ...), custom_call_target="tpu_custom_call" | custom-call | flops 1000 | bytes 1000 | tf_op jit(solution)/shard_map/pallas_call | solution.py:35
  17.0 1.1 %collective-permute-done.5.refs_3_ = bf16[256,256]{1,0:T(8,128)(2,1)S(1)} collective-permute-done((bf16[256,256]{1,0:T(8,128)(2,1)S(1)}, bf16[256,256]{1,0:T(8,128)(2,1)S(1)}, u32[]{:S(2)}, u32[]{:S(2)}) %collective-permute-start.5) | collective-permute-done | bytes 131104 | tf_op jit(solution)/shard_map/ppermute | solution.py:189
  18.1 0.7 collective-permute-done.6.refs_4_
  18.9 18.7 %all_to_all.22 = bf16[8,64,256]{2,1,0:T(8,128)(2,1)S(1)} all-to-all(bf16[8,64,256]{2,1,0:T(8,128)(2,1)S(1)} %bitcast.9), channel_id=1, replica_groups=mesh['y'=4,'z'=8,'core'=2,'feat'=4] {'z'}, dimensions={0} | all-to-all | bytes 524288 | tf_op jit(solution)/shard_map/all_to_all | solution.py:223
  37.7 12.9 %all_to_all.23 = bf16[8,64,256]{2,1,0:T(8,128)(2,1)S(1)} all-to-all(bf16[8,64,256]{2,1,0:T(8,128)(2,1)S(1)} %bitcast.22), channel_id=1, replica_groups=mesh['y'=4,'z'=8,'core'=2,'feat'=4] {'z'}, dimensions={0} | all-to-all | bytes 524288 | tf_op jit(solution)/shard_map/all_to_all | solution.py:229
  51.2 2.5 %collective-permute-start.8 = (bf16[256,256]{1,0:T(8,128)(2,1)S(1)}, bf16[256,256]{1,0:T(8,128)(2,1)S(1)}, u32[]{:S(2)}, u32[]{:S(2)}) collective-permute-start(bf16[256,256]{1,0:T(8,128)(2,1)S(1)} %bitcast.23), channel_id=1, source_target_pairs={{0,64},{64,0},{128,192},{192,128},{1,65},{65,1},{129,193},{193,129... | collective-permute-start | bytes 393224 | tf_op jit(solution)/shard_map/ppermute | solution.py:185
  53.7 1.5 %collective-permute-start.13 = (bf16[256,256]{1,0:T(8,128)(2,1)S(1)}, bf16[256,256]{1,0:T(8,128)(2,1)S(1)}, u32[]{:S(2)}, u32[]{:S(2)}) collective-permute-start(bf16[256,256]{1,0:T(8,128)(2,1)S(1)} %bitcast.24), channel_id=1, source_target_pairs={{0,192},{192,0},{64,128},{128,64},{1,193},{193,1},{65,129},{129,65... | collective-permute-start | bytes 393224 | tf_op jit(solution)/shard_map/ppermute | solution.py:189
  55.7 4.4 %collective-permute-start.11 = (bf16[256,256]{1,0:T(8,128)(2,1)S(1)}, bf16[256,256]{1,0:T(8,128)(2,1)S(1)}, u32[]{:S(2)}, u32[]{:S(2)}) collective-permute-start(bf16[256,256]{1,0:T(8,128)(2,1)S(1)} %collective-permute-done.10.refs_8_), channel_id=1, source_target_pairs={{0,64},{64,0},{128,192},{192,128},{1,65},{65,1},{129,193},{193,129... | collective-permute-start | bytes 393224 | tf_op jit(solution)/shard_map/ppermute | solution.py:185
  60.2 3.6 %shard_map.59 = (bf16[64,2048]{1,0:T(8,128)(2,1)S(1)}, bf16[64,2048]{1,0:T(8,128)(2,1)S(1)}, f32[64,64]{1,0:T(8,128)S(1)}) custom-call(s32[1,2048]{1,0:T(1,128)S(1)} %bitcast.17, bf16[2048,256]{1,0:T(8,128)(2,1)S(1)} %copy-done.1, s32[1,2048]{1,0:T(1,128)S(1)} %collective-permute-done.refs_0_.refs_2_, ...), custom_call_target="tpu_custom_call" | custom-call | flops 4294967296 | bytes 1000 | tf_op jit(solution)/shard_map/pallas_call | solution.py:35
  63.8 1.3 %collective-permute-done.9.refs_2_ = bf16[256,256]{1,0:T(8,128)(2,1)S(1)} collective-permute-done((bf16[256,256]{1,0:T(8,128)(2,1)S(1)}, bf16[256,256]{1,0:T(8,128)(2,1)S(1)}, u32[]{:S(2)}, u32[]{:S(2)}) %collective-permute-start.9) | collective-permute-done | bytes 131104 | tf_op jit(solution)/shard_map/ppermute | solution.py:189
  66.1 0.6 collective-permute-start.17
  67.2 1.6 %collective-permute-start.15 = (bf16[64,1152]{1,0:T(8,128)(2,1)S(1)}, bf16[64,1152]{1,0:T(8,128)(2,1)S(1)}, u32[]{:S(2)}, u32[]{:S(2)}) collective-permute-start(bf16[64,1152]{1,0:T(8,128)(2,1)S(1)} %shard_map.63.refs_0_.refs_5_), channel_id=1, source_target_pairs={{0,1},{1,0},{2,3},{3,2},{4,5},{5,4},{6,7},{7,6},{8,9},{9,8},{10,11... | collective-permute-start | bytes 442376 | tf_op jit(solution)/shard_map/ppermute | solution.py:185
  69.3 2.2 %collective-permute-start.18 = (bf16[64,1024]{1,0:T(8,128)(2,1)S(1)}, bf16[64,1024]{1,0:T(8,128)(2,1)S(1)}, u32[]{:S(2)}, u32[]{:S(2)}) collective-permute-start(bf16[64,1024]{1,0:T(8,128)(2,1)S(1)} %shard_map.67.refs_0_), channel_id=1, source_target_pairs={{0,3},{3,0},{1,2},{2,1},{4,7},{7,4},{5,6},{6,5},{8,11},{11,8},{9,1... | collective-permute-start | bytes 393224 | tf_op jit(solution)/shard_map/ppermute | solution.py:189
  71.5 1.6 %collective-permute-done.15.refs_1_ = bf16[64,1152]{1,0:T(8,128)(2,1)S(1)} collective-permute-done((bf16[64,1152]{1,0:T(8,128)(2,1)S(1)}, bf16[64,1152]{1,0:T(8,128)(2,1)S(1)}, u32[]{:S(2)}, u32[]{:S(2)}) %collective-permute-start.15) | collective-permute-done | bytes 147488 | tf_op jit(solution)/shard_map/ppermute | solution.py:185
  73.3 2.8 %collective-permute-start.16 = (bf16[64,1152]{1,0:T(8,128)(2,1)S(1)}, bf16[64,1152]{1,0:T(8,128)(2,1)S(1)}, u32[]{:S(2)}, u32[]{:S(2)}) collective-permute-start(bf16[64,1152]{1,0:T(8,128)(2,1)S(1)} %shard_map.64.refs_1_), channel_id=1, source_target_pairs={{0,3},{3,0},{1,2},{2,1},{4,7},{7,4},{5,6},{6,5},{8,11},{11,8},{9,1... | collective-permute-start | bytes 442376 | tf_op jit(solution)/shard_map/ppermute | solution.py:189
  76.4 3.2 %collective-permute-done.16.refs_2_ = bf16[64,1152]{1,0:T(8,128)(2,1)S(1)} collective-permute-done((bf16[64,1152]{1,0:T(8,128)(2,1)S(1)}, bf16[64,1152]{1,0:T(8,128)(2,1)S(1)}, u32[]{:S(2)}, u32[]{:S(2)}) %collective-permute-start.16) | collective-permute-done | bytes 147488 | tf_op jit(solution)/shard_map/ppermute | solution.py:189
  79.7 0.8 shard_map.65
  80.5 0.7 collective-permute-done.19.refs_2_
  81.2 0.8 %shard_map.69 = f32[1,2048]{1,0:T(1,128)} custom-call(s32[1,2048]{1,0:T(1,128)S(1)} %bitcast.21, bf16[64,1024]{1,0:T(8,128)(2,1)S(1)} %shard_map.68.refs_1_, bf16[64,1024]{1,0:T(8,128)(2,1)S(1)} %collective-permute-done.19.refs_2_, f32[64,64]{1,0:T(8,128)S(1)} %get-tuple-element.36.refs_3_, f32[1,1024]{1,0:T(1,128)S(1)} %get-tuple-element.37.refs_4_), custom_call_target="tpu_custom_call" | custom-call | flops 1000 | bytes 1000 | tf_op jit(solution)/shard_map/pallas_call | solution.py:35
  (39 shorter events, 4.0 us)
Async XLA Ops:
  0.6 0.8 %copy-start.2 = (s32[2048]{0:T(1024)S(1)}, s32[2048]{0:T(1024)}, u32[]{:S(2)}) copy-start(s32[2048]{0:T(1024)} %param.5) | copy-start | bytes 24580
  0.6 3.4 %collective-permute-start.1 = (bf16[2048,256]{1,0:T(8,128)(2,1)}, bf16[2048,256]{1,0:T(8,128)(2,1)S(1)}, u32[]{:S(2)}, u32[]{:S(2)}) collective-permute-start(bf16[2048,256]{1,0:T(8,128)(2,1)} %refs_1_.13), channel_id=1, source_target_pairs={{0,4},{4,0},{1,5},{5,1},{2,6},{6,2},{3,7},{7,3},{8,12},{12,8},{9,1... | collective-permute-start | bytes 3145736 | tf_op jit(solution)/shard_map/ppermute | solution.py:181
  1.5 2.5 %collective-permute-start = (s32[1,2048]{1,0:T(1,128)S(1)}, s32[1,2048]{1,0:T(1,128)S(1)}, u32[]{:S(2)}, u32[]{:S(2)}) collective-permute-start(s32[1,2048]{1,0:T(1,128)S(1)} %bitcast.12), channel_id=1, source_target_pairs={{0,4},{4,0},{1,5},{5,1},{2,6},{6,2},{3,7},{7,3},{8,12},{12,8},{9,1... | collective-permute-start | bytes 24584 | tf_op jit(solution)/shard_map/ppermute | solution.py:181
  2.0 1.2 %copy-start = (bf16[2048,256]{1,0:T(8,128)(2,1)S(1)}, bf16[2048,256]{1,0:T(8,128)(2,1)}, u32[]{:S(2)}) copy-start(bf16[2048,256]{1,0:T(8,128)(2,1)} %refs_1_.13) | copy-start | bytes 3145732
  4.0 3.7 %copy-start.1 = (bf16[2048,256]{1,0:T(8,128)(2,1)S(1)}, bf16[2048,256]{1,0:T(8,128)(2,1)}, u32[]{:S(2)}) copy-start(bf16[2048,256]{1,0:T(8,128)(2,1)} %refs_1_.13) | copy-start | bytes 3145732
  4.7 7.6 %collective-permute-start.3 = (bf16[256,256]{1,0:T(8,128)(2,1)S(1)}, bf16[256,256]{1,0:T(8,128)(2,1)S(1)}, u32[]{:S(2)}, u32[]{:S(2)}) collective-permute-start(bf16[256,256]{1,0:T(8,128)(2,1)S(1)} %get-tuple-element.22.refs_4_), channel_id=1, source_target_pairs={{0,64},{64,0},{128,192},{192,128},{1,65},{65,1},{129,193},{193,129... | collective-permute-start | bytes 393224 | tf_op jit(solution)/shard_map/ppermute | solution.py:185
  7.0 6.8 %collective-permute-start.2 = (bf16[256,256]{1,0:T(8,128)(2,1)S(1)}, bf16[256,256]{1,0:T(8,128)(2,1)S(1)}, u32[]{:S(2)}, u32[]{:S(2)}) collective-permute-start(bf16[256,256]{1,0:T(8,128)(2,1)S(1)} %get-tuple-element.23.refs_5_), channel_id=1, source_target_pairs={{0,192},{192,0},{64,128},{128,64},{1,193},{193,1},{65,129},{129,65... | collective-permute-start | bytes 393224 | tf_op jit(solution)/shard_map/ppermute | solution.py:189
  8.9 8.1 %collective-permute-start.4 = (bf16[256,256]{1,0:T(8,128)(2,1)S(1)}, bf16[256,256]{1,0:T(8,128)(2,1)S(1)}, u32[]{:S(2)}, u32[]{:S(2)}) collective-permute-start(bf16[256,256]{1,0:T(8,128)(2,1)S(1)} %get-tuple-element.24.refs_4_), channel_id=1, source_target_pairs={{0,64},{64,0},{128,192},{192,128},{1,65},{65,1},{129,193},{193,129... | collective-permute-start | bytes 393224 | tf_op jit(solution)/shard_map/ppermute | solution.py:185
  10.4 6.7 %collective-permute-start.7 = (bf16[256,256]{1,0:T(8,128)(2,1)S(1)}, bf16[256,256]{1,0:T(8,128)(2,1)S(1)}, u32[]{:S(2)}, u32[]{:S(2)}) collective-permute-start(bf16[256,256]{1,0:T(8,128)(2,1)S(1)} %get-tuple-element.25.refs_5_), channel_id=1, source_target_pairs={{0,192},{192,0},{64,128},{128,64},{1,193},{193,1},{65,129},{129,65... | collective-permute-start | bytes 393224 | tf_op jit(solution)/shard_map/ppermute | solution.py:189
  12.4 5.8 %collective-permute-start.5 = (bf16[256,256]{1,0:T(8,128)(2,1)S(1)}, bf16[256,256]{1,0:T(8,128)(2,1)S(1)}, u32[]{:S(2)}, u32[]{:S(2)}) collective-permute-start(bf16[256,256]{1,0:T(8,128)(2,1)S(1)} %shard_map.55.refs_5_), channel_id=1, source_target_pairs={{0,192},{192,0},{64,128},{128,64},{1,193},{193,1},{65,129},{129,65... | collective-permute-start | bytes 393224 | tf_op jit(solution)/shard_map/ppermute | solution.py:189
  13.8 5.1 %collective-permute-start.6 = (bf16[256,256]{1,0:T(8,128)(2,1)S(1)}, bf16[256,256]{1,0:T(8,128)(2,1)S(1)}, u32[]{:S(2)}, u32[]{:S(2)}) collective-permute-start(bf16[256,256]{1,0:T(8,128)(2,1)S(1)} %shard_map.54.refs_4_), channel_id=1, source_target_pairs={{0,64},{64,0},{128,192},{192,128},{1,65},{65,1},{129,193},{193,129... | collective-permute-start | bytes 393224 | tf_op jit(solution)/shard_map/ppermute | solution.py:185
  50.6 5.1 %collective-permute-start.10 = (bf16[256,256]{1,0:T(8,128)(2,1)S(1)}, bf16[256,256]{1,0:T(8,128)(2,1)S(1)}, u32[]{:S(2)}, u32[]{:S(2)}) collective-permute-start(bf16[256,256]{1,0:T(8,128)(2,1)S(1)} %bitcast.25), channel_id=1, source_target_pairs={{0,192},{192,0},{64,128},{128,64},{1,193},{193,1},{65,129},{129,65... | collective-permute-start | bytes 393224 | tf_op jit(solution)/shard_map/ppermute | solution.py:189
  51.2 8.9 %collective-permute-start.8 = (bf16[256,256]{1,0:T(8,128)(2,1)S(1)}, bf16[256,256]{1,0:T(8,128)(2,1)S(1)}, u32[]{:S(2)}, u32[]{:S(2)}) collective-permute-start(bf16[256,256]{1,0:T(8,128)(2,1)S(1)} %bitcast.23), channel_id=1, source_target_pairs={{0,64},{64,0},{128,192},{192,128},{1,65},{65,1},{129,193},{193,129... | collective-permute-start | bytes 393224 | tf_op jit(solution)/shard_map/ppermute | solution.py:185
  53.7 6.5 %collective-permute-start.12 = (bf16[256,256]{1,0:T(8,128)(2,1)S(1)}, bf16[256,256]{1,0:T(8,128)(2,1)S(1)}, u32[]{:S(2)}, u32[]{:S(2)}) collective-permute-start(bf16[256,256]{1,0:T(8,128)(2,1)S(1)} %bitcast.26), channel_id=1, source_target_pairs={{0,64},{64,0},{128,192},{192,128},{1,65},{65,1},{129,193},{193,129... | collective-permute-start | bytes 393224 | tf_op jit(solution)/shard_map/ppermute | solution.py:185
  53.7 6.5 %collective-permute-start.13 = (bf16[256,256]{1,0:T(8,128)(2,1)S(1)}, bf16[256,256]{1,0:T(8,128)(2,1)S(1)}, u32[]{:S(2)}, u32[]{:S(2)}) collective-permute-start(bf16[256,256]{1,0:T(8,128)(2,1)S(1)} %bitcast.24), channel_id=1, source_target_pairs={{0,192},{192,0},{64,128},{128,64},{1,193},{193,1},{65,129},{129,65... | collective-permute-start | bytes 393224 | tf_op jit(solution)/shard_map/ppermute | solution.py:189
  55.7 8.1 %collective-permute-start.11 = (bf16[256,256]{1,0:T(8,128)(2,1)S(1)}, bf16[256,256]{1,0:T(8,128)(2,1)S(1)}, u32[]{:S(2)}, u32[]{:S(2)}) collective-permute-start(bf16[256,256]{1,0:T(8,128)(2,1)S(1)} %collective-permute-done.10.refs_8_), channel_id=1, source_target_pairs={{0,64},{64,0},{128,192},{192,128},{1,65},{65,1},{129,193},{193,129... | collective-permute-start | bytes 393224 | tf_op jit(solution)/shard_map/ppermute | solution.py:185
  60.1 5.0 %collective-permute-start.9 = (bf16[256,256]{1,0:T(8,128)(2,1)S(1)}, bf16[256,256]{1,0:T(8,128)(2,1)S(1)}, u32[]{:S(2)}, u32[]{:S(2)}) collective-permute-start(bf16[256,256]{1,0:T(8,128)(2,1)S(1)} %collective-permute-done.8.refs_5_), channel_id=1, source_target_pairs={{0,192},{192,0},{64,128},{128,64},{1,193},{193,1},{65,129},{129,65... | collective-permute-start | bytes 393224 | tf_op jit(solution)/shard_map/ppermute | solution.py:189
  65.6 1.6 %collective-permute-start.14 = (bf16[64,1152]{1,0:T(8,128)(2,1)S(1)}, bf16[64,1152]{1,0:T(8,128)(2,1)S(1)}, u32[]{:S(2)}, u32[]{:S(2)}) collective-permute-start(bf16[64,1152]{1,0:T(8,128)(2,1)S(1)} %shard_map.60.refs_5_.refs_1_), channel_id=1, source_target_pairs={{0,4},{4,0},{1,5},{5,1},{2,6},{6,2},{3,7},{7,3},{8,12},{12,8},{9,1... | collective-permute-start | bytes 442376 | tf_op jit(solution)/shard_map/ppermute | solution.py:181
  66.1 3.2 %collective-permute-start.17 = (bf16[64,1024]{1,0:T(8,128)(2,1)S(1)}, bf16[64,1024]{1,0:T(8,128)(2,1)S(1)}, u32[]{:S(2)}, u32[]{:S(2)}) collective-permute-start(bf16[64,1024]{1,0:T(8,128)(2,1)S(1)} %shard_map.61.refs_5_.refs_1_), channel_id=1, source_target_pairs={{0,4},{4,0},{1,5},{5,1},{2,6},{6,2},{3,7},{7,3},{8,12},{12,8},{9,1... | collective-permute-start | bytes 393224 | tf_op jit(solution)/shard_map/ppermute | solution.py:181
  67.2 5.9 %collective-permute-start.15 = (bf16[64,1152]{1,0:T(8,128)(2,1)S(1)}, bf16[64,1152]{1,0:T(8,128)(2,1)S(1)}, u32[]{:S(2)}, u32[]{:S(2)}) collective-permute-start(bf16[64,1152]{1,0:T(8,128)(2,1)S(1)} %shard_map.63.refs_0_.refs_5_), channel_id=1, source_target_pairs={{0,1},{1,0},{2,3},{3,2},{4,5},{5,4},{6,7},{7,6},{8,9},{9,8},{10,11... | collective-permute-start | bytes 442376 | tf_op jit(solution)/shard_map/ppermute | solution.py:185
  69.3 6.7 %collective-permute-start.18 = (bf16[64,1024]{1,0:T(8,128)(2,1)S(1)}, bf16[64,1024]{1,0:T(8,128)(2,1)S(1)}, u32[]{:S(2)}, u32[]{:S(2)}) collective-permute-start(bf16[64,1024]{1,0:T(8,128)(2,1)S(1)} %shard_map.67.refs_0_), channel_id=1, source_target_pairs={{0,3},{3,0},{1,2},{2,1},{4,7},{7,4},{5,6},{6,5},{8,11},{11,8},{9,1... | collective-permute-start | bytes 393224 | tf_op jit(solution)/shard_map/ppermute | solution.py:189
  73.3 6.4 %collective-permute-start.16 = (bf16[64,1152]{1,0:T(8,128)(2,1)S(1)}, bf16[64,1152]{1,0:T(8,128)(2,1)S(1)}, u32[]{:S(2)}, u32[]{:S(2)}) collective-permute-start(bf16[64,1152]{1,0:T(8,128)(2,1)S(1)} %shard_map.64.refs_1_), channel_id=1, source_target_pairs={{0,3},{3,0},{1,2},{2,1},{4,7},{7,4},{5,6},{6,5},{8,11},{11,8},{9,1... | collective-permute-start | bytes 442376 | tf_op jit(solution)/shard_map/ppermute | solution.py:189
  76.1 5.1 %collective-permute-start.19 = (bf16[64,1024]{1,0:T(8,128)(2,1)S(1)}, bf16[64,1024]{1,0:T(8,128)(2,1)S(1)}, u32[]{:S(2)}, u32[]{:S(2)}) collective-permute-start(bf16[64,1024]{1,0:T(8,128)(2,1)S(1)} %shard_map.68.refs_1_), channel_id=1, source_target_pairs={{0,1},{1,0},{2,3},{3,2},{4,5},{5,4},{6,7},{7,6},{8,9},{9,8},{10,11... | collective-permute-start | bytes 393224 | tf_op jit(solution)/shard_map/ppermute | solution.py:185

commit v4 on v3

--- a/solution.py
+++ b/solution.py
@@ -85,11 +85,15 @@
         copies_ref[z * K : (z + 1) * K, :] = rounded
 
 
+def turned(k, core):
+    return k ^ (2 * core) if k & 1 else k
+
+
 def scores_kernel(groups, blocks, first, with_squares, packed, span, *refs):
     y, core = lax.axis_index("y"), lax.axis_index("core")
     group_refs, refs = refs[: 2 * groups], refs[2 * groups :]
     block_refs, refs = refs[: len(blocks)], refs[len(blocks) :]
-    numbers = [(y ^ k) * 16 + 2 * z + core for k, z, _ in blocks]
+    numbers = [(y ^ turned(k, core)) * 16 + 2 * z + core for k, z, _ in blocks]
     scores_in = squares_in = None
     if not first:
         scores_in, refs = refs[:groups], refs[groups:]
@@ -145,36 +149,39 @@
         put_squares(out_ref, get_squares(x_ref, SPLIT) + get_squares(y_ref, SPLIT), SPLIT)
 
 
-def best_rows(code_ref, at, x_ref, y_ref, scale, fit_ref):
+def factors(code, scale):
     high = scale.astype(BF16)
     low = (scale - high.astype(F32)).astype(BF16)
-    for start in range(0, SPLIT, BLOCK):
-        part = slice(start, start + BLOCK)
-        parent = code_ref[:, at + start : at + start + BLOCK] >> 6
-        number = lax.broadcasted_iota(jnp.int32, (PARENTS, BLOCK), 0)
-        chosen = (number == parent).astype(F32).astype(BF16)
-        factor = jnp.dot(high, chosen, preferred_element_type=F32) + jnp.dot(
-            low, chosen, preferred_element_type=F32
-        )
-        scores = x_ref[:, part].astype(F32) + y_ref[:, part].astype(F32)
-        fit_ref[:, at + start : at + start + BLOCK] = jnp.max(scores * factor, axis=0, keepdims=True) / (
-            0.25 * D
-        )
-
-
-def finish_first_kernel(code_ref, x_ref, y_ref, totals_ref, scale_ref, centroids_ref, fit_ref):
+    number = lax.broadcasted_iota(jnp.int32, (PARENTS, BLOCK), 0)
+    chosen = (number == code >> 6).astype(F32).astype(BF16)
+    return jnp.dot(high, chosen, preferred_element_type=F32) + jnp.dot(
+        low, chosen, preferred_element_type=F32
+    )
+
+
+def best(x, y, factor):
+    return jnp.max((x.astype(F32) + y.astype(F32)) * factor, axis=0, keepdims=True) / (0.25 * D)
+
+
+def finish_first_kernel(code_ref, x_ref, y_ref, totals_ref, factor_ref, centroids_ref, fit_ref):
     y, z, core = lax.axis_index("y"), lax.axis_index("z"), lax.axis_index("core")
     scale = lax.rsqrt((get_squares(x_ref, SPLIT) + get_squares(y_ref, SPLIT)) / D + EPS)
-    scale_ref[...] = scale
     lane = lax.broadcasted_iota(jnp.int32, (K, PARENTS), 1)
     own = jnp.sum(jnp.where(lane == y * 16 + z * 2 + core, scale, 0.0), axis=1, keepdims=True)
     centroids_ref[...] = (totals_ref[...] * own).astype(BF16)
-    best_rows(code_ref, 0, x_ref, y_ref, scale, fit_ref)
-
-
-def finish_kernel(code_ref, x_ref, y_ref, scale_ref, first_ref, fit_ref):
+    for start in range(0, SPLIT, BLOCK):
+        part, later = slice(start, start + BLOCK), slice(SPLIT + start, SPLIT + start + BLOCK)
+        fit_ref[:, part] = best(x_ref[:, part], y_ref[:, part], factors(code_ref[:, part], scale))
+        factor_ref[:, part] = factors(code_ref[:, later], scale)
+
+
+def finish_kernel(x_ref, y_ref, factor_ref, first_ref, fit_ref):
     fit_ref[:, :SPLIT] = first_ref[...]
-    best_rows(code_ref, SPLIT, x_ref, y_ref, scale_ref[...], fit_ref)
+    fit_ref[:, SPLIT:] = best(x_ref[...], y_ref[...], factor_ref[...])
+
+
+def copy_kernel(x_ref, out_ref):
+    out_ref[...] = x_ref[...]
 
 
 def swap(x):
@@ -189,8 +196,14 @@
     return lax.ppermute(x, axis, [(0, 3), (3, 0), (1, 2), (2, 1)])
 
 
+def turn(x, k):
+    pairs = [(2 * i + core, 2 * (i ^ turned(k, core)) + core) for core in range(NC) for i in range(NY)]
+    return lax.ppermute(x, ("y", "core"), pairs)
+
+
 def body(embeddings, parent_ids, child_assignment):
     code = parent_ids.reshape(1, ROWS) * K + child_assignment.reshape(1, ROWS)
+    code = call(copy_kernel, jax.ShapeDtypeStruct((1, ROWS), jnp.int32), [code], flops=LONG)
     own = (code, embeddings)
     other = tuple(swap(x) for x in own)
 
@@ -229,9 +242,9 @@
     mine = lax.all_to_all(copies, "z", 0, 0, tiled=True)
 
     low, high = mine[:HALF], mine[HALF:]
-    left_low, right_high = left(low, "y"), right(high, "y")
-    left_high, right_low = left(high, "y"), right(low, "y")
-    far_low, far_high = right(left_low, "y"), left(right_high, "y")
+    left_low, right_high = turn(low, 1), turn(high, 3)
+    left_high, right_low = turn(high, 1), turn(low, 3)
+    far_low, far_high = turn(left_low, 3), turn(right_high, 1)
 
     plain = jax.ShapeDtypeStruct((K, ROWS), BF16)
     squared = jax.ShapeDtypeStruct((K, PARENTS), F32)
@@ -275,17 +288,17 @@
 
     a = call(add_kernel, long_message, [a, left(a, "feat")])
     b = call(add_kernel, message, [b, right(b, "feat")])
-    scale, centroids, first = call(
+    factor, centroids, first = call(
         finish_first_kernel,
         (
-            jax.ShapeDtypeStruct((K, PARENTS), F32),
+            jax.ShapeDtypeStruct((K, SPLIT), F32),
             jax.ShapeDtypeStruct((K, WIDTH), BF16),
             jax.ShapeDtypeStruct((1, SPLIT), F32),
         ),
         [code, a, right(a, "feat"), totals],
     )
     fit = call(
-        finish_kernel, jax.ShapeDtypeStruct((1, ROWS), F32), [code, b, left(b, "feat"), scale, first]
+        finish_kernel, jax.ShapeDtypeStruct((1, ROWS), F32), [b, left(b, "feat"), factor, first]
     )
     return centroids, fit.reshape(ROWS)
 

time: 82.4 us -> 81.1 us (0.984)
  starting transfers between devices: 25.8 us -> 24.2 us
  waiting for transfers between devices: 9.04 us -> 9.92 us
    ppermute x0 -> x6, starting transfers between devices: none -> 7.55 us  [turn(): return lax.ppermute(x, ('y', 'core'), pairs)]
    ppermute x8 -> x5, starting transfers between devices: 14.6 us -> 7.56 us  [left(): return lax.ppermute(x, axis, [(0, 1), (1, 0), (2, 3), (3, 2)])]
    ppermute x0 -> x6, waiting for transfers between devices: none -> 2.37 us  [turn(): return lax.ppermute(x, ('y', 'core'), pairs)]
    ppermute x8 -> x5, starting transfers between devices: 9.92 us -> 7.75 us  [right(): return lax.ppermute(x, axis, [(0, 3), (3, 0), (1, 2), (2, 1)])]
    ppermute x8 -> x5, waiting for transfers between devices: 6.03 us -> 4.36 us  [right(): return lax.ppermute(x, axis, [(0, 3), (3, 0), (1, 2), (2, 1)])]
    pallas_call x20 -> x21, Pallas kernels: 12.7 us -> 12.6 us  [call(): pl.pallas_call(skipping, out_shape=out_shape, in_specs=[vmem] * (count +...]
    ppermute x8 -> x5, waiting for transfers between devices: 3 us -> 3 us  [left(): return lax.ppermute(x, axis, [(0, 1), (1, 0), (2, 3), (3, 2)])]
  transfers between devices with their start and end apart: 20 -> 20, of which waited for: 7 -> 8; matrix products, arithmetic and copies ran while one was open for 1% -> 1% of each run, Pallas kernels for 13% -> 13%
where the time goes in v4:
time: 81.1 us; the launch traced here: 80.6 us
  blocking collectives  31.6 us (39%)
  starting transfers between devices  24.2 us (30%)
  Pallas kernels  12.6 us (16%)
  waiting for transfers between devices  9.92 us (12%)
  between operations  0.86 us (1%)
    all_to_all x1, blocking collectives, body(): parts = lax.all_to_all(merged, 'z', 0, 0, tiled=True)  18.7 us
    all_to_all x1, blocking collectives, body(): mine = lax.all_to_all(copies, 'z', 0, 0, tiled=True)  12.9 us
    pallas_call x21, Pallas kernels, call(): pl.pallas_call(skipping, out_shape=out_shape, in_specs=[vmem] * (count +...  12.6 us
    ppermute x5, starting transfers between devices, right(): return lax.ppermute(x, axis, [(0, 3), (3, 0), (1, 2), (2, 1)])  7.75 us
    ppermute x5, starting transfers between devices, left(): return lax.ppermute(x, axis, [(0, 1), (1, 0), (2, 3), (3, 2)])  7.56 us
    ppermute x6, starting transfers between devices, turn(): return lax.ppermute(x, ('y', 'core'), pairs)  7.55 us
    ppermute x5, waiting for transfers between devices, right(): return lax.ppermute(x, axis, [(0, 3), (3, 0), (1, 2), (2, 1)])  4.36 us
    ppermute x5, waiting for transfers between devices, left(): return lax.ppermute(x, axis, [(0, 1), (1, 0), (2, 3), (3, 2)])  3 us
  transfers between devices with their start and end apart: 20, of which 8 were waited for; matrix products, arithmetic and copies ran while one was open for 1% of the time, Pallas kernels for 13%

profile of v4, /device:TPU:8, one launch (start us, length us, event | category | flops | bytes accessed | tf_op | source)
XLA Modules:
  0.0 80.6 jit_solution(17112746590887283313)
XLA Ops:
  0.7 0.7 broadcast_multiply_fusion
  1.5 0.6 collective-permute-start
  2.1 0.6 copy-done
  2.7 0.7 shard_map.51
  3.6 0.7 shard_map.52
  4.3 2.3 %collective-permute-start.3 = (bf16[256,256]{1,0:T(8,128)(2,1)S(1)}, bf16[256,256]{1,0:T(8,128)(2,1)S(1)}, u32[]{:S(2)}, u32[]{:S(2)}) collective-permute-start(bf16[256,256]{1,0:T(8,128)(2,1)S(1)} %get-tuple-element.22.refs_4_), channel_id=1, source_target_pairs={{0,64},{64,0},{128,192},{192,128},{1,65},{65,1},{129,193},{193,129... | collective-permute-start | bytes 393224 | tf_op jit(solution)/shard_map/ppermute | solution.py:192
  6.6 0.7 collective-permute-start.2
  7.3 1.2 %shard_map.53 = (bf16[256,256]{1,0:T(8,128)(2,1)S(1)}, bf16[256,256]{1,0:T(8,128)(2,1)S(1)}) custom-call(s32[1,2048]{1,0:T(1,128)S(1)} %shard_map.50.refs_0_, bf16[2048,256]{1,0:T(8,128)(2,1)S(1)} %copy-done, s32[1,2048]{1,0:T(1,128)S(1)} %collective-permute-done.refs_0_.refs_2_, bf16[2048,256]{1,0:T(8,128)(2,1)S(1)} %collective-permute-done.1.refs_1_.refs_3_, ...), custom_call_target="tpu_custom_call" | custom-call | flops 4294967296 | bytes 1000 | tf_op jit(solution)/shard_map/pallas_call | solution.py:35
  8.5 1.4 %collective-permute-start.4 = (bf16[256,256]{1,0:T(8,128)(2,1)S(1)}, bf16[256,256]{1,0:T(8,128)(2,1)S(1)}, u32[]{:S(2)}, u32[]{:S(2)}) collective-permute-start(bf16[256,256]{1,0:T(8,128)(2,1)S(1)} %get-tuple-element.24.refs_4_), channel_id=1, source_target_pairs={{0,64},{64,0},{128,192},{192,128},{1,65},{65,1},{129,193},{193,129... | collective-permute-start | bytes 393224 | tf_op jit(solution)/shard_map/ppermute | solution.py:192
  9.9 0.7 collective-permute-start.7
  10.6 1.2 %shard_map.54 = (f32[256,256]{1,0:T(8,128)S(1)}, f32[256,256]{1,0:T(8,128)S(1)}) custom-call(s32[1,2048]{1,0:T(1,128)S(1)} %shard_map.50.refs_0_, bf16[2048,256]{1,0:T(8,128)(2,1)S(1)} %copy-done, s32[1,2048]{1,0:T(1,128)S(1)} %collective-permute-done.refs_0_.refs_2_, bf16[2048,256]{1,0:T(8,128)(2,1)S(1)} %collective-permute-done.1.refs_1_.refs_3_, ...), custom_call_target="tpu_custom_call" | custom-call | flops 1000 | bytes 1000 | tf_op jit(solution)/shard_map/pallas_call | solution.py:35
  11.9 1.4 %collective-permute-start.5 = (bf16[256,256]{1,0:T(8,128)(2,1)S(1)}, bf16[256,256]{1,0:T(8,128)(2,1)S(1)}, u32[]{:S(2)}, u32[]{:S(2)}) collective-permute-start(bf16[256,256]{1,0:T(8,128)(2,1)S(1)} %shard_map.56.refs_5_), channel_id=1, source_target_pairs={{0,192},{192,0},{64,128},{128,64},{1,193},{193,1},{65,129},{129,65... | collective-permute-start | bytes 393224 | tf_op jit(solution)/shard_map/ppermute | solution.py:196
  13.4 2.0 %collective-permute-start.6 = (bf16[256,256]{1,0:T(8,128)(2,1)S(1)}, bf16[256,256]{1,0:T(8,128)(2,1)S(1)}, u32[]{:S(2)}, u32[]{:S(2)}) collective-permute-start(bf16[256,256]{1,0:T(8,128)(2,1)S(1)} %shard_map.55.refs_4_), channel_id=1, source_target_pairs={{0,64},{64,0},{128,192},{192,128},{1,65},{65,1},{129,193},{193,129... | collective-permute-start | bytes 393224 | tf_op jit(solution)/shard_map/ppermute | solution.py:192
  15.3 1.2 %shard_map.57 = (f32[256,256]{1,0:T(8,128)S(1)}, f32[256,256]{1,0:T(8,128)S(1)}) custom-call(s32[1,2048]{1,0:T(1,128)S(1)} %shard_map.50.refs_0_, bf16[2048,256]{1,0:T(8,128)(2,1)S(1)} %copy-done, s32[1,2048]{1,0:T(1,128)S(1)} %collective-permute-done.refs_0_.refs_2_, bf16[2048,256]{1,0:T(8,128)(2,1)S(1)} %collective-permute-done.1.refs_1_.refs_3_, ...), custom_call_target="tpu_custom_call" | custom-call | flops 1000 | bytes 1000 | tf_op jit(solution)/shard_map/pallas_call | solution.py:35
  16.6 1.1 %collective-permute-done.5.refs_3_ = bf16[256,256]{1,0:T(8,128)(2,1)S(1)} collective-permute-done((bf16[256,256]{1,0:T(8,128)(2,1)S(1)}, bf16[256,256]{1,0:T(8,128)(2,1)S(1)}, u32[]{:S(2)}, u32[]{:S(2)}) %collective-permute-start.5) | collective-permute-done | bytes 131104 | tf_op jit(solution)/shard_map/ppermute | solution.py:196
  17.7 0.7 collective-permute-done.6.refs_4_
  18.5 18.7 %all_to_all.22 = bf16[8,64,256]{2,1,0:T(8,128)(2,1)S(1)} all-to-all(bf16[8,64,256]{2,1,0:T(8,128)(2,1)S(1)} %bitcast.9), channel_id=1, replica_groups=mesh['y'=4,'z'=8,'core'=2,'feat'=4] {'z'}, dimensions={0} | all-to-all | bytes 524288 | tf_op jit(solution)/shard_map/all_to_all | solution.py:236
  37.3 12.9 %all_to_all.23 = bf16[8,64,256]{2,1,0:T(8,128)(2,1)S(1)} all-to-all(bf16[8,64,256]{2,1,0:T(8,128)(2,1)S(1)} %bitcast.12), channel_id=1, replica_groups=mesh['y'=4,'z'=8,'core'=2,'feat'=4] {'z'}, dimensions={0} | all-to-all | bytes 524288 | tf_op jit(solution)/shard_map/all_to_all | solution.py:242
  50.8 2.5 %collective-permute-start.8 = (bf16[256,256]{1,0:T(8,128)(2,1)S(1)}, bf16[256,256]{1,0:T(8,128)(2,1)S(1)}, u32[]{:S(2)}, u32[]{:S(2)}) collective-permute-start(bf16[256,256]{1,0:T(8,128)(2,1)S(1)} %bitcast.14), channel_id=1, source_target_pairs={{0,64},{64,0},{128,192},{192,128},{4,196},{68,132},{132,68},{196,4... | collective-permute-start | bytes 393224 | tf_op jit(solution)/shard_map/ppermute | solution.py:201
  53.3 1.5 %collective-permute-start.13 = (bf16[256,256]{1,0:T(8,128)(2,1)S(1)}, bf16[256,256]{1,0:T(8,128)(2,1)S(1)}, u32[]{:S(2)}, u32[]{:S(2)}) collective-permute-start(bf16[256,256]{1,0:T(8,128)(2,1)S(1)} %bitcast.15), channel_id=1, source_target_pairs={{0,192},{64,128},{128,64},{192,0},{4,68},{68,4},{132,196},{196,132... | collective-permute-start | bytes 393224 | tf_op jit(solution)/shard_map/ppermute | solution.py:201
  54.9 1.3 %collective-permute-done.10.refs_8_ = bf16[256,256]{1,0:T(8,128)(2,1)S(1)} collective-permute-done((bf16[256,256]{1,0:T(8,128)(2,1)S(1)}, bf16[256,256]{1,0:T(8,128)(2,1)S(1)}, u32[]{:S(2)}, u32[]{:S(2)}) %collective-permute-start.10) | collective-permute-done | bytes 131104 | tf_op jit(solution)/shard_map/ppermute | solution.py:201
  56.2 2.6 %collective-permute-start.11 = (bf16[256,256]{1,0:T(8,128)(2,1)S(1)}, bf16[256,256]{1,0:T(8,128)(2,1)S(1)}, u32[]{:S(2)}, u32[]{:S(2)}) collective-permute-start(bf16[256,256]{1,0:T(8,128)(2,1)S(1)} %collective-permute-done.10.refs_8_), channel_id=1, source_target_pairs={{0,64},{64,0},{128,192},{192,128},{4,196},{68,132},{132,68},{196,4... | collective-permute-start | bytes 393224 | tf_op jit(solution)/shard_map/ppermute | solution.py:201
  59.1 3.6 %shard_map.60 = (bf16[64,2048]{1,0:T(8,128)(2,1)S(1)}, bf16[64,2048]{1,0:T(8,128)(2,1)S(1)}, f32[64,64]{1,0:T(8,128)S(1)}) custom-call(s32[1,2048]{1,0:T(1,128)S(1)} %shard_map.50.refs_0_, bf16[2048,256]{1,0:T(8,128)(2,1)S(1)} %copy-done, s32[1,2048]{1,0:T(1,128)S(1)} %collective-permute-done.refs_0_.refs_2_, ...), custom_call_target="tpu_custom_call" | custom-call | flops 4294967296 | bytes 1000 | tf_op jit(solution)/shard_map/pallas_call | solution.py:35
  62.7 1.0 %collective-permute-done.9.refs_2_ = bf16[256,256]{1,0:T(8,128)(2,1)S(1)} collective-permute-done((bf16[256,256]{1,0:T(8,128)(2,1)S(1)}, bf16[256,256]{1,0:T(8,128)(2,1)S(1)}, u32[]{:S(2)}, u32[]{:S(2)}) %collective-permute-start.9) | collective-permute-done | bytes 131104 | tf_op jit(solution)/shard_map/ppermute | solution.py:201
  66.0 1.6 %collective-permute-start.15 = (bf16[64,1152]{1,0:T(8,128)(2,1)S(1)}, bf16[64,1152]{1,0:T(8,128)(2,1)S(1)}, u32[]{:S(2)}, u32[]{:S(2)}) collective-permute-start(bf16[64,1152]{1,0:T(8,128)(2,1)S(1)} %shard_map.64.refs_0_.refs_5_), channel_id=1, source_target_pairs={{0,1},{1,0},{2,3},{3,2},{4,5},{5,4},{6,7},{7,6},{8,9},{9,8},{10,11... | collective-permute-start | bytes 442376 | tf_op jit(solution)/shard_map/ppermute | solution.py:192
  68.1 2.2 %collective-permute-start.18 = (bf16[64,1024]{1,0:T(8,128)(2,1)S(1)}, bf16[64,1024]{1,0:T(8,128)(2,1)S(1)}, u32[]{:S(2)}, u32[]{:S(2)}) collective-permute-start(bf16[64,1024]{1,0:T(8,128)(2,1)S(1)} %shard_map.68.refs_0_), channel_id=1, source_target_pairs={{0,3},{3,0},{1,2},{2,1},{4,7},{7,4},{5,6},{6,5},{8,11},{11,8},{9,1... | collective-permute-start | bytes 393224 | tf_op jit(solution)/shard_map/ppermute | solution.py:196
  70.2 1.6 %collective-permute-done.15.refs_1_ = bf16[64,1152]{1,0:T(8,128)(2,1)S(1)} collective-permute-done((bf16[64,1152]{1,0:T(8,128)(2,1)S(1)}, bf16[64,1152]{1,0:T(8,128)(2,1)S(1)}, u32[]{:S(2)}, u32[]{:S(2)}) %collective-permute-start.15) | collective-permute-done | bytes 147488 | tf_op jit(solution)/shard_map/ppermute | solution.py:192
  72.0 2.8 %collective-permute-start.16 = (bf16[64,1152]{1,0:T(8,128)(2,1)S(1)}, bf16[64,1152]{1,0:T(8,128)(2,1)S(1)}, u32[]{:S(2)}, u32[]{:S(2)}) collective-permute-start(bf16[64,1152]{1,0:T(8,128)(2,1)S(1)} %shard_map.65.refs_1_), channel_id=1, source_target_pairs={{0,3},{3,0},{1,2},{2,1},{4,7},{7,4},{5,6},{6,5},{8,11},{11,8},{9,1... | collective-permute-start | bytes 442376 | tf_op jit(solution)/shard_map/ppermute | solution.py:196
  75.1 3.2 %collective-permute-done.16.refs_2_ = bf16[64,1152]{1,0:T(8,128)(2,1)S(1)} collective-permute-done((bf16[64,1152]{1,0:T(8,128)(2,1)S(1)}, bf16[64,1152]{1,0:T(8,128)(2,1)S(1)}, u32[]{:S(2)}, u32[]{:S(2)}) %collective-permute-start.16) | collective-permute-done | bytes 147488 | tf_op jit(solution)/shard_map/ppermute | solution.py:196
  78.4 0.8 %shard_map.66 = (f32[64,1024]{1,0:T(8,128)S(1)}, bf16[64,256]{1,0:T(8,128)(2,1)}, f32[1,1024]{1,0:T(1,128)S(1)}) custom-call(s32[1,2048]{1,0:T(1,128)S(1)} %shard_map.50.refs_0_, bf16[64,1152]{1,0:T(8,128)(2,1)S(1)} %shard_map.65.refs_1_, bf16[64,1152]{1,0:T(8,128)(2,1)S(1)} %collective-permute-done.16.refs_2_, f32[64,256]{1,0:T(8,128)S(1)} %get-tuple-element.34.refs_3_), custom_call_target="tpu_custom_call" | custom-call | flops 1000 | bytes 1000 | tf_op jit(solution)/shard_map/pallas_call | solution.py:35
  79.2 0.7 collective-permute-done.19.refs_1_
  79.9 0.7 shard_map.70
  (38 shorter events, 4.5 us)
Async XLA Ops:
  0.6 0.8 %copy-start.1 = (s32[2048]{0:T(1024)S(1)}, s32[2048]{0:T(1024)}, u32[]{:S(2)}) copy-start(s32[2048]{0:T(1024)} %param.5) | copy-start | bytes 24580
  0.6 3.0 %collective-permute-start.1 = (bf16[2048,256]{1,0:T(8,128)(2,1)}, bf16[2048,256]{1,0:T(8,128)(2,1)S(1)}, u32[]{:S(2)}, u32[]{:S(2)}) collective-permute-start(bf16[2048,256]{1,0:T(8,128)(2,1)} %refs_1_.13), channel_id=1, source_target_pairs={{0,4},{4,0},{1,5},{5,1},{2,6},{6,2},{3,7},{7,3},{8,12},{12,8},{9,1... | collective-permute-start | bytes 3145736 | tf_op jit(solution)/shard_map/ppermute | solution.py:188
  1.5 1.2 %copy-start = (bf16[2048,256]{1,0:T(8,128)(2,1)S(1)}, bf16[2048,256]{1,0:T(8,128)(2,1)}, u32[]{:S(2)}) copy-start(bf16[2048,256]{1,0:T(8,128)(2,1)} %refs_1_.13) | copy-start | bytes 3145732
  1.5 1.9 %collective-permute-start = (s32[1,2048]{1,0:T(1,128)S(1)}, s32[1,2048]{1,0:T(1,128)S(1)}, u32[]{:S(2)}, u32[]{:S(2)}) collective-permute-start(s32[1,2048]{1,0:T(1,128)S(1)} %shard_map.50.refs_0_), channel_id=1, source_target_pairs={{0,4},{4,0},{1,5},{5,1},{2,6},{6,2},{3,7},{7,3},{8,12},{12,8},{9,1... | collective-permute-start | bytes 24584 | tf_op jit(solution)/shard_map/ppermute | solution.py:188
  4.3 7.6 %collective-permute-start.3 = (bf16[256,256]{1,0:T(8,128)(2,1)S(1)}, bf16[256,256]{1,0:T(8,128)(2,1)S(1)}, u32[]{:S(2)}, u32[]{:S(2)}) collective-permute-start(bf16[256,256]{1,0:T(8,128)(2,1)S(1)} %get-tuple-element.22.refs_4_), channel_id=1, source_target_pairs={{0,64},{64,0},{128,192},{192,128},{1,65},{65,1},{129,193},{193,129... | collective-permute-start | bytes 393224 | tf_op jit(solution)/shard_map/ppermute | solution.py:192
  6.6 6.8 %collective-permute-start.2 = (bf16[256,256]{1,0:T(8,128)(2,1)S(1)}, bf16[256,256]{1,0:T(8,128)(2,1)S(1)}, u32[]{:S(2)}, u32[]{:S(2)}) collective-permute-start(bf16[256,256]{1,0:T(8,128)(2,1)S(1)} %get-tuple-element.23.refs_5_), channel_id=1, source_target_pairs={{0,192},{192,0},{64,128},{128,64},{1,193},{193,1},{65,129},{129,65... | collective-permute-start | bytes 393224 | tf_op jit(solution)/shard_map/ppermute | solution.py:196
  8.5 8.1 %collective-permute-start.4 = (bf16[256,256]{1,0:T(8,128)(2,1)S(1)}, bf16[256,256]{1,0:T(8,128)(2,1)S(1)}, u32[]{:S(2)}, u32[]{:S(2)}) collective-permute-start(bf16[256,256]{1,0:T(8,128)(2,1)S(1)} %get-tuple-element.24.refs_4_), channel_id=1, source_target_pairs={{0,64},{64,0},{128,192},{192,128},{1,65},{65,1},{129,193},{193,129... | collective-permute-start | bytes 393224 | tf_op jit(solution)/shard_map/ppermute | solution.py:192
  9.9 6.7 %collective-permute-start.7 = (bf16[256,256]{1,0:T(8,128)(2,1)S(1)}, bf16[256,256]{1,0:T(8,128)(2,1)S(1)}, u32[]{:S(2)}, u32[]{:S(2)}) collective-permute-start(bf16[256,256]{1,0:T(8,128)(2,1)S(1)} %get-tuple-element.25.refs_5_), channel_id=1, source_target_pairs={{0,192},{192,0},{64,128},{128,64},{1,193},{193,1},{65,129},{129,65... | collective-permute-start | bytes 393224 | tf_op jit(solution)/shard_map/ppermute | solution.py:196
  11.9 5.8 %collective-permute-start.5 = (bf16[256,256]{1,0:T(8,128)(2,1)S(1)}, bf16[256,256]{1,0:T(8,128)(2,1)S(1)}, u32[]{:S(2)}, u32[]{:S(2)}) collective-permute-start(bf16[256,256]{1,0:T(8,128)(2,1)S(1)} %shard_map.56.refs_5_), channel_id=1, source_target_pairs={{0,192},{192,0},{64,128},{128,64},{1,193},{193,1},{65,129},{129,65... | collective-permute-start | bytes 393224 | tf_op jit(solution)/shard_map/ppermute | solution.py:196
  13.4 5.1 %collective-permute-start.6 = (bf16[256,256]{1,0:T(8,128)(2,1)S(1)}, bf16[256,256]{1,0:T(8,128)(2,1)S(1)}, u32[]{:S(2)}, u32[]{:S(2)}) collective-permute-start(bf16[256,256]{1,0:T(8,128)(2,1)S(1)} %shard_map.55.refs_4_), channel_id=1, source_target_pairs={{0,64},{64,0},{128,192},{192,128},{1,65},{65,1},{129,193},{193,129... | collective-permute-start | bytes 393224 | tf_op jit(solution)/shard_map/ppermute | solution.py:192
  50.2 6.0 %collective-permute-start.10 = (bf16[256,256]{1,0:T(8,128)(2,1)S(1)}, bf16[256,256]{1,0:T(8,128)(2,1)S(1)}, u32[]{:S(2)}, u32[]{:S(2)}) collective-permute-start(bf16[256,256]{1,0:T(8,128)(2,1)S(1)} %bitcast.16), channel_id=1, source_target_pairs={{0,192},{64,128},{128,64},{192,0},{4,68},{68,4},{132,196},{196,132... | collective-permute-start | bytes 393224 | tf_op jit(solution)/shard_map/ppermute | solution.py:201
  50.8 8.1 %collective-permute-start.8 = (bf16[256,256]{1,0:T(8,128)(2,1)S(1)}, bf16[256,256]{1,0:T(8,128)(2,1)S(1)}, u32[]{:S(2)}, u32[]{:S(2)}) collective-permute-start(bf16[256,256]{1,0:T(8,128)(2,1)S(1)} %bitcast.14), channel_id=1, source_target_pairs={{0,64},{64,0},{128,192},{192,128},{4,196},{68,132},{132,68},{196,4... | collective-permute-start | bytes 393224 | tf_op jit(solution)/shard_map/ppermute | solution.py:201
  53.3 5.8 %collective-permute-start.12 = (bf16[256,256]{1,0:T(8,128)(2,1)S(1)}, bf16[256,256]{1,0:T(8,128)(2,1)S(1)}, u32[]{:S(2)}, u32[]{:S(2)}) collective-permute-start(bf16[256,256]{1,0:T(8,128)(2,1)S(1)} %bitcast.17), channel_id=1, source_target_pairs={{0,64},{64,0},{128,192},{192,128},{4,196},{68,132},{132,68},{196,4... | collective-permute-start | bytes 393224 | tf_op jit(solution)/shard_map/ppermute | solution.py:201
  53.3 5.8 %collective-permute-start.13 = (bf16[256,256]{1,0:T(8,128)(2,1)S(1)}, bf16[256,256]{1,0:T(8,128)(2,1)S(1)}, u32[]{:S(2)}, u32[]{:S(2)}) collective-permute-start(bf16[256,256]{1,0:T(8,128)(2,1)S(1)} %bitcast.15), channel_id=1, source_target_pairs={{0,192},{64,128},{128,64},{192,0},{4,68},{68,4},{132,196},{196,132... | collective-permute-start | bytes 393224 | tf_op jit(solution)/shard_map/ppermute | solution.py:201
  56.2 6.6 %collective-permute-start.11 = (bf16[256,256]{1,0:T(8,128)(2,1)S(1)}, bf16[256,256]{1,0:T(8,128)(2,1)S(1)}, u32[]{:S(2)}, u32[]{:S(2)}) collective-permute-start(bf16[256,256]{1,0:T(8,128)(2,1)S(1)} %collective-permute-done.10.refs_8_), channel_id=1, source_target_pairs={{0,64},{64,0},{128,192},{192,128},{4,196},{68,132},{132,68},{196,4... | collective-permute-start | bytes 393224 | tf_op jit(solution)/shard_map/ppermute | solution.py:201
  58.8 5.0 %collective-permute-start.9 = (bf16[256,256]{1,0:T(8,128)(2,1)S(1)}, bf16[256,256]{1,0:T(8,128)(2,1)S(1)}, u32[]{:S(2)}, u32[]{:S(2)}) collective-permute-start(bf16[256,256]{1,0:T(8,128)(2,1)S(1)} %collective-permute-done.8.refs_5_), channel_id=1, source_target_pairs={{0,192},{64,128},{128,64},{192,0},{4,68},{68,4},{132,196},{196,132... | collective-permute-start | bytes 393224 | tf_op jit(solution)/shard_map/ppermute | solution.py:201
  64.3 1.6 %collective-permute-start.14 = (bf16[64,1152]{1,0:T(8,128)(2,1)S(1)}, bf16[64,1152]{1,0:T(8,128)(2,1)S(1)}, u32[]{:S(2)}, u32[]{:S(2)}) collective-permute-start(bf16[64,1152]{1,0:T(8,128)(2,1)S(1)} %shard_map.61.refs_5_.refs_1_), channel_id=1, source_target_pairs={{0,4},{4,0},{1,5},{5,1},{2,6},{6,2},{3,7},{7,3},{8,12},{12,8},{9,1... | collective-permute-start | bytes 442376 | tf_op jit(solution)/shard_map/ppermute | solution.py:188
  64.9 3.2 %collective-permute-start.17 = (bf16[64,1024]{1,0:T(8,128)(2,1)S(1)}, bf16[64,1024]{1,0:T(8,128)(2,1)S(1)}, u32[]{:S(2)}, u32[]{:S(2)}) collective-permute-start(bf16[64,1024]{1,0:T(8,128)(2,1)S(1)} %shard_map.62.refs_5_.refs_1_), channel_id=1, source_target_pairs={{0,4},{4,0},{1,5},{5,1},{2,6},{6,2},{3,7},{7,3},{8,12},{12,8},{9,1... | collective-permute-start | bytes 393224 | tf_op jit(solution)/shard_map/ppermute | solution.py:188
  66.0 5.9 %collective-permute-start.15 = (bf16[64,1152]{1,0:T(8,128)(2,1)S(1)}, bf16[64,1152]{1,0:T(8,128)(2,1)S(1)}, u32[]{:S(2)}, u32[]{:S(2)}) collective-permute-start(bf16[64,1152]{1,0:T(8,128)(2,1)S(1)} %shard_map.64.refs_0_.refs_5_), channel_id=1, source_target_pairs={{0,1},{1,0},{2,3},{3,2},{4,5},{5,4},{6,7},{7,6},{8,9},{9,8},{10,11... | collective-permute-start | bytes 442376 | tf_op jit(solution)/shard_map/ppermute | solution.py:192
  68.1 6.7 %collective-permute-start.18 = (bf16[64,1024]{1,0:T(8,128)(2,1)S(1)}, bf16[64,1024]{1,0:T(8,128)(2,1)S(1)}, u32[]{:S(2)}, u32[]{:S(2)}) collective-permute-start(bf16[64,1024]{1,0:T(8,128)(2,1)S(1)} %shard_map.68.refs_0_), channel_id=1, source_target_pairs={{0,3},{3,0},{1,2},{2,1},{4,7},{7,4},{5,6},{6,5},{8,11},{11,8},{9,1... | collective-permute-start | bytes 393224 | tf_op jit(solution)/shard_map/ppermute | solution.py:196
  72.0 6.4 %collective-permute-start.16 = (bf16[64,1152]{1,0:T(8,128)(2,1)S(1)}, bf16[64,1152]{1,0:T(8,128)(2,1)S(1)}, u32[]{:S(2)}, u32[]{:S(2)}) collective-permute-start(bf16[64,1152]{1,0:T(8,128)(2,1)S(1)} %shard_map.65.refs_1_), channel_id=1, source_target_pairs={{0,3},{3,0},{1,2},{2,1},{4,7},{7,4},{5,6},{6,5},{8,11},{11,8},{9,1... | collective-permute-start | bytes 442376 | tf_op jit(solution)/shard_map/ppermute | solution.py:196
  74.8 5.1 %collective-permute-start.19 = (bf16[64,1024]{1,0:T(8,128)(2,1)S(1)}, bf16[64,1024]{1,0:T(8,128)(2,1)S(1)}, u32[]{:S(2)}, u32[]{:S(2)}) collective-permute-start(bf16[64,1024]{1,0:T(8,128)(2,1)S(1)} %shard_map.69.refs_0_), channel_id=1, source_target_pairs={{0,1},{1,0},{2,3},{3,2},{4,5},{5,4},{6,7},{7,6},{8,9},{9,8},{10,11... | collective-permute-start | bytes 393224 | tf_op jit(solution)/shard_map/ppermute | solution.py:192

commit v5 on v4

--- a/solution.py
+++ b/solution.py
@@ -93,7 +93,7 @@
     y, core = lax.axis_index("y"), lax.axis_index("core")
     group_refs, refs = refs[: 2 * groups], refs[2 * groups :]
     block_refs, refs = refs[: len(blocks)], refs[len(blocks) :]
-    numbers = [(y ^ turned(k, core)) * 16 + 2 * z + core for k, z, _ in blocks]
+    numbers = [(y ^ turned(k, core)) * 16 + core for k in blocks]
     scores_in = squares_in = None
     if not first:
         scores_in, refs = refs[:groups], refs[groups:]
@@ -102,8 +102,8 @@
     if with_squares:
         lane = lax.broadcasted_iota(jnp.int32, (K, PARENTS), 1)
         squares = jnp.zeros((K, PARENTS), F32) if first else squares_in[...]
-        for number, block_ref, (_, _, count) in zip(numbers, block_refs, blocks):
-            for z in range(count):
+        for number, block_ref in zip(numbers, block_refs):
+            for z in range(NZ):
                 block = block_ref[z * K : (z + 1) * K, :].astype(F32)
                 square = jnp.sum(block * block, axis=1, keepdims=True)
                 squares = jnp.where(lane == number + 2 * z, square, squares)
@@ -117,11 +117,11 @@
             part = slice(start, start + BLOCK)
             rows, parent = rows_ref[part, :], codes[:, part] >> 6
             chosen = jnp.zeros((K, BLOCK), F32) if first else scores_in[group][:, part].astype(F32)
-            for number, block_ref, (_, _, count) in zip(numbers, block_refs, blocks):
+            for number, block_ref in zip(numbers, block_refs):
                 product = lax.dot_general(
                     block_ref[...], rows, (((1,), (1,)), ((), ())), preferred_element_type=F32
                 )
-                for z in range(count):
+                for z in range(NZ):
                     chosen = jnp.where(parent == number + 2 * z, product[z * K : (z + 1) * K, :], chosen)
             refs[group][:, start - span[0] : start - span[0] + BLOCK] = chosen.astype(BF16)
 
@@ -241,47 +241,48 @@
     )
     mine = lax.all_to_all(copies, "z", 0, 0, tiled=True)
 
-    low, high = mine[:HALF], mine[HALF:]
-    left_low, right_high = turn(low, 1), turn(high, 3)
-    left_high, right_low = turn(high, 1), turn(low, 3)
-    far_low, far_high = turn(left_low, 3), turn(right_high, 1)
+    far = turn(mine, 2)
+    near = [turn(mine, 1), turn(mine, 3)]
 
     plain = jax.ShapeDtypeStruct((K, ROWS), BF16)
     squared = jax.ShapeDtypeStruct((K, PARENTS), F32)
-    blocks = ((0, 0, NZ), (1, 0, 4), (1, 4, 4), (3, 0, 4), (3, 4, 4))
     state = call(
-        functools.partial(scores_kernel, 2, blocks, True, True, False, (0, ROWS)),
+        functools.partial(scores_kernel, 2, (0,), True, True, False, (0, ROWS)),
         (plain, plain, squared),
-        [*own, *other, mine, left_low, left_high, right_low, right_high],
-        flops=LONG,
-    )
-    blocks = ((2, 0, 4), (2, 4, 4))
+        [*own, *other, mine],
+    )
+    state = call(
+        functools.partial(scores_kernel, 2, (1, 3), False, True, False, (0, ROWS)),
+        (plain, plain, squared),
+        [*own, *other, *near, *state],
+    )
+    blocks = (2,)
     message = jax.ShapeDtypeStruct((K, SPLIT), BF16)
     long_message = jax.ShapeDtypeStruct((K, SPLIT + 2 * PARENTS), BF16)
     spans = ((0, SPLIT), (SPLIT, ROWS))
     (sent_a,) = call(
         functools.partial(scores_kernel, 1, blocks, False, True, True, spans[0]),
         (long_message,),
-        [*other, far_low, far_high, *state[1:]],
+        [*other, far, *state[1:]],
     )
     (sent_b,) = call(
         functools.partial(scores_kernel, 1, blocks, False, False, False, spans[1]),
         (message,),
-        [*other, far_low, far_high, state[1]],
+        [*other, far, state[1]],
         behind=[sent_a],
     )
     got_a, got_b = swap(sent_a), swap(sent_b)
     (kept_a,) = call(
         functools.partial(scores_kernel, 1, blocks, False, False, False, spans[0]),
         (message,),
-        [*own, far_low, far_high, state[0]],
+        [*own, far, state[0]],
         behind=[sent_b],
     )
     a = call(join_kernel, long_message, [kept_a, sent_a, got_a])
     (kept_b,) = call(
         functools.partial(scores_kernel, 1, blocks, False, False, False, spans[1]),
         (message,),
-        [*own, far_low, far_high, state[0]],
+        [*own, far, state[0]],
         behind=[a],
     )
     b = call(join_kernel, message, [kept_b, sent_b, got_b])

time: 81.1 us -> 81.2 us (level)
  waiting for transfers between devices: 9.92 us -> 13.7 us
  starting transfers between devices: 24.2 us -> 20.6 us
    ppermute x6 -> x3, waiting for transfers between devices: 2.37 us -> 6.17 us  [turn(): return lax.ppermute(x, ('y', 'core'), pairs)]
    ppermute x6 -> x3, starting transfers between devices: 7.55 us -> 3.96 us  [turn(): return lax.ppermute(x, ('y', 'core'), pairs)]
    pallas_call x21 -> x22, Pallas kernels: 12.6 us -> 12.8 us  [call(): pl.pallas_call(skipping, out_shape=out_shape, in_specs=[vmem] * (count +...]
  transfers between devices with their start and end apart: 20 -> 17, of which waited for: 8 -> 7; matrix products, arithmetic and copies ran while one was open for 1% -> 1% of each run, Pallas kernels for 13% -> 13%
where the time goes in v5:
time: 81.2 us; the launch traced here: 81 us
  blocking collectives  31.6 us (39%)
  starting transfers between devices  20.6 us (25%)
  waiting for transfers between devices  13.7 us (17%)
  Pallas kernels  12.8 us (16%)
  between operations  0.87 us (1%)
    all_to_all x1, blocking collectives, body(): parts = lax.all_to_all(merged, 'z', 0, 0, tiled=True)  18.7 us
    all_to_all x1, blocking collectives, body(): mine = lax.all_to_all(copies, 'z', 0, 0, tiled=True)  12.9 us
    pallas_call x22, Pallas kernels, call(): pl.pallas_call(skipping, out_shape=out_shape, in_specs=[vmem] * (count +...  12.8 us
    ppermute x5, starting transfers between devices, right(): return lax.ppermute(x, axis, [(0, 3), (3, 0), (1, 2), (2, 1)])  7.75 us
    ppermute x5, starting transfers between devices, left(): return lax.ppermute(x, axis, [(0, 1), (1, 0), (2, 3), (3, 2)])  7.56 us
    ppermute x3, waiting for transfers between devices, turn(): return lax.ppermute(x, ('y', 'core'), pairs)  6.17 us
    ppermute x5, waiting for transfers between devices, right(): return lax.ppermute(x, axis, [(0, 3), (3, 0), (1, 2), (2, 1)])  4.36 us
    ppermute x3, starting transfers between devices, turn(): return lax.ppermute(x, ('y', 'core'), pairs)  3.96 us
  transfers between devices with their start and end apart: 17, of which 7 were waited for; matrix products, arithmetic and copies ran while one was open for 1% of the time, Pallas kernels for 13%

profile of v5, /device:TPU:8, one launch (start us, length us, event | category | flops | bytes accessed | tf_op | source)
XLA Modules:
  0.0 81.0 jit_solution(13670463838539376945)
XLA Ops:
  0.7 0.7 broadcast_multiply_fusion
  1.5 0.6 collective-permute-start
  2.1 0.6 copy-done
  2.7 0.7 shard_map.51
  3.6 0.7 shard_map.52
  4.3 2.3 %collective-permute-start.3 = (bf16[256,256]{1,0:T(8,128)(2,1)S(1)}, bf16[256,256]{1,0:T(8,128)(2,1)S(1)}, u32[]{:S(2)}, u32[]{:S(2)}) collective-permute-start(bf16[256,256]{1,0:T(8,128)(2,1)S(1)} %get-tuple-element.25.refs_4_), channel_id=1, source_target_pairs={{0,64},{64,0},{128,192},{192,128},{1,65},{65,1},{129,193},{193,129... | collective-permute-start | bytes 393224 | tf_op jit(solution)/shard_map/ppermute | solution.py:192
  6.6 0.7 collective-permute-start.2
  7.3 1.2 %shard_map.53 = (bf16[256,256]{1,0:T(8,128)(2,1)S(1)}, bf16[256,256]{1,0:T(8,128)(2,1)S(1)}) custom-call(s32[1,2048]{1,0:T(1,128)S(1)} %shard_map.50.refs_0_, bf16[2048,256]{1,0:T(8,128)(2,1)S(1)} %copy-done, s32[1,2048]{1,0:T(1,128)S(1)} %collective-permute-done.refs_0_.refs_2_, bf16[2048,256]{1,0:T(8,128)(2,1)S(1)} %collective-permute-done.1.refs_1_.refs_3_, ...), custom_call_target="tpu_custom_call" | custom-call | flops 4294967296 | bytes 1000 | tf_op jit(solution)/shard_map/pallas_call | solution.py:35
  8.5 1.4 %collective-permute-start.4 = (bf16[256,256]{1,0:T(8,128)(2,1)S(1)}, bf16[256,256]{1,0:T(8,128)(2,1)S(1)}, u32[]{:S(2)}, u32[]{:S(2)}) collective-permute-start(bf16[256,256]{1,0:T(8,128)(2,1)S(1)} %get-tuple-element.27.refs_4_), channel_id=1, source_target_pairs={{0,64},{64,0},{128,192},{192,128},{1,65},{65,1},{129,193},{193,129... | collective-permute-start | bytes 393224 | tf_op jit(solution)/shard_map/ppermute | solution.py:192
  9.9 0.7 collective-permute-start.7
  10.6 1.2 %shard_map.54 = (f32[256,256]{1,0:T(8,128)S(1)}, f32[256,256]{1,0:T(8,128)S(1)}) custom-call(s32[1,2048]{1,0:T(1,128)S(1)} %shard_map.50.refs_0_, bf16[2048,256]{1,0:T(8,128)(2,1)S(1)} %copy-done, s32[1,2048]{1,0:T(1,128)S(1)} %collective-permute-done.refs_0_.refs_2_, bf16[2048,256]{1,0:T(8,128)(2,1)S(1)} %collective-permute-done.1.refs_1_.refs_3_, ...), custom_call_target="tpu_custom_call" | custom-call | flops 1000 | bytes 1000 | tf_op jit(solution)/shard_map/pallas_call | solution.py:35
  11.9 1.4 %collective-permute-start.5 = (bf16[256,256]{1,0:T(8,128)(2,1)S(1)}, bf16[256,256]{1,0:T(8,128)(2,1)S(1)}, u32[]{:S(2)}, u32[]{:S(2)}) collective-permute-start(bf16[256,256]{1,0:T(8,128)(2,1)S(1)} %shard_map.56.refs_5_), channel_id=1, source_target_pairs={{0,192},{192,0},{64,128},{128,64},{1,193},{193,1},{65,129},{129,65... | collective-permute-start | bytes 393224 | tf_op jit(solution)/shard_map/ppermute | solution.py:196
  13.4 2.0 %collective-permute-start.6 = (bf16[256,256]{1,0:T(8,128)(2,1)S(1)}, bf16[256,256]{1,0:T(8,128)(2,1)S(1)}, u32[]{:S(2)}, u32[]{:S(2)}) collective-permute-start(bf16[256,256]{1,0:T(8,128)(2,1)S(1)} %shard_map.55.refs_4_), channel_id=1, source_target_pairs={{0,64},{64,0},{128,192},{192,128},{1,65},{65,1},{129,193},{193,129... | collective-permute-start | bytes 393224 | tf_op jit(solution)/shard_map/ppermute | solution.py:192
  15.3 1.2 %shard_map.57 = (f32[256,256]{1,0:T(8,128)S(1)}, f32[256,256]{1,0:T(8,128)S(1)}) custom-call(s32[1,2048]{1,0:T(1,128)S(1)} %shard_map.50.refs_0_, bf16[2048,256]{1,0:T(8,128)(2,1)S(1)} %copy-done, s32[1,2048]{1,0:T(1,128)S(1)} %collective-permute-done.refs_0_.refs_2_, bf16[2048,256]{1,0:T(8,128)(2,1)S(1)} %collective-permute-done.1.refs_1_.refs_3_, ...), custom_call_target="tpu_custom_call" | custom-call | flops 1000 | bytes 1000 | tf_op jit(solution)/shard_map/pallas_call | solution.py:35
  16.6 1.1 %collective-permute-done.5.refs_3_ = bf16[256,256]{1,0:T(8,128)(2,1)S(1)} collective-permute-done((bf16[256,256]{1,0:T(8,128)(2,1)S(1)}, bf16[256,256]{1,0:T(8,128)(2,1)S(1)}, u32[]{:S(2)}, u32[]{:S(2)}) %collective-permute-start.5) | collective-permute-done | bytes 131104 | tf_op jit(solution)/shard_map/ppermute | solution.py:196
  17.7 0.7 collective-permute-done.6.refs_4_
  18.5 18.7 %all_to_all.22 = bf16[8,64,256]{2,1,0:T(8,128)(2,1)S(1)} all-to-all(bf16[8,64,256]{2,1,0:T(8,128)(2,1)S(1)} %bitcast.11), channel_id=1, replica_groups=mesh['y'=4,'z'=8,'core'=2,'feat'=4] {'z'}, dimensions={0} | all-to-all | bytes 524288 | tf_op jit(solution)/shard_map/all_to_all | solution.py:236
  37.3 12.9 %all_to_all.23 = bf16[8,64,256]{2,1,0:T(8,128)(2,1)S(1)} all-to-all(bf16[8,64,256]{2,1,0:T(8,128)(2,1)S(1)} %bitcast.13), channel_id=1, replica_groups=mesh['y'=4,'z'=8,'core'=2,'feat'=4] {'z'}, dimensions={0} | all-to-all | bytes 524288 | tf_op jit(solution)/shard_map/all_to_all | solution.py:242
  50.6 2.5 %collective-permute-start.9 = (bf16[512,256]{1,0:T(8,128)(2,1)S(1)}, bf16[512,256]{1,0:T(8,128)(2,1)S(1)}, u32[]{:S(2)}, u32[]{:S(2)}) collective-permute-start(bf16[512,256]{1,0:T(8,128)(2,1)S(1)} %bitcast.8), channel_id=1, source_target_pairs={{0,64},{64,0},{128,192},{192,128},{4,196},{68,132},{132,68},{196,4... | collective-permute-start | bytes 786440 | tf_op jit(solution)/shard_map/ppermute | solution.py:201
  53.2 1.0 %collective-permute-start.8 = (bf16[512,256]{1,0:T(8,128)(2,1)S(1)}, bf16[512,256]{1,0:T(8,128)(2,1)S(1)}, u32[]{:S(2)}, u32[]{:S(2)}) collective-permute-start(bf16[512,256]{1,0:T(8,128)(2,1)S(1)} %bitcast.9), channel_id=1, source_target_pairs={{0,128},{64,192},{128,0},{192,64},{4,132},{68,196},{132,4},{196,68... | collective-permute-start | bytes 786440 | tf_op jit(solution)/shard_map/ppermute | solution.py:201
  54.2 1.4 %shard_map.60 = (bf16[64,2048]{1,0:T(8,128)(2,1)S(1)}, bf16[64,2048]{1,0:T(8,128)(2,1)S(1)}, f32[64,64]{1,0:T(8,128)S(1)}) custom-call(s32[1,2048]{1,0:T(1,128)S(1)} %shard_map.50.refs_0_, bf16[2048,256]{1,0:T(8,128)(2,1)S(1)} %copy-done, s32[1,2048]{1,0:T(1,128)S(1)} %collective-permute-done.refs_0_.refs_2_, ...), custom_call_target="tpu_custom_call" | custom-call | flops 1000 | bytes 1000 | tf_op jit(solution)/shard_map/pallas_call | solution.py:35
  55.5 6.2 %collective-permute-done.10.refs_5_ = bf16[512,256]{1,0:T(8,128)(2,1)S(1)} collective-permute-done((bf16[512,256]{1,0:T(8,128)(2,1)S(1)}, bf16[512,256]{1,0:T(8,128)(2,1)S(1)}, u32[]{:S(2)}, u32[]{:S(2)}) %collective-permute-start.10) | collective-permute-done | bytes 262176 | tf_op jit(solution)/shard_map/ppermute | solution.py:201
  61.7 2.5 %shard_map.61 = (bf16[64,2048]{1,0:T(8,128)(2,1)S(1)}, bf16[64,2048]{1,0:T(8,128)(2,1)S(1)}, f32[64,64]{1,0:T(8,128)S(1)}) custom-call(s32[1,2048]{1,0:T(1,128)S(1)} %shard_map.50.refs_0_, bf16[2048,256]{1,0:T(8,128)(2,1)S(1)} %copy-done, s32[1,2048]{1,0:T(1,128)S(1)} %collective-permute-done.refs_0_.refs_2_, ...), custom_call_target="tpu_custom_call" | custom-call | flops 1000 | bytes 1000 | tf_op jit(solution)/shard_map/pallas_call | solution.py:35
  65.2 0.6 collective-permute-start.14
  66.3 1.6 %collective-permute-start.12 = (bf16[64,1152]{1,0:T(8,128)(2,1)S(1)}, bf16[64,1152]{1,0:T(8,128)(2,1)S(1)}, u32[]{:S(2)}, u32[]{:S(2)}) collective-permute-start(bf16[64,1152]{1,0:T(8,128)(2,1)S(1)} %shard_map.65.refs_0_.refs_4_), channel_id=1, source_target_pairs={{0,1},{1,0},{2,3},{3,2},{4,5},{5,4},{6,7},{7,6},{8,9},{9,8},{10,11... | collective-permute-start | bytes 442376 | tf_op jit(solution)/shard_map/ppermute | solution.py:192
  68.4 2.2 %collective-permute-start.15 = (bf16[64,1024]{1,0:T(8,128)(2,1)S(1)}, bf16[64,1024]{1,0:T(8,128)(2,1)S(1)}, u32[]{:S(2)}, u32[]{:S(2)}) collective-permute-start(bf16[64,1024]{1,0:T(8,128)(2,1)S(1)} %shard_map.69.refs_0_), channel_id=1, source_target_pairs={{0,3},{3,0},{1,2},{2,1},{4,7},{7,4},{5,6},{6,5},{8,11},{11,8},{9,1... | collective-permute-start | bytes 393224 | tf_op jit(solution)/shard_map/ppermute | solution.py:196
  70.6 1.6 %collective-permute-done.12.refs_1_ = bf16[64,1152]{1,0:T(8,128)(2,1)S(1)} collective-permute-done((bf16[64,1152]{1,0:T(8,128)(2,1)S(1)}, bf16[64,1152]{1,0:T(8,128)(2,1)S(1)}, u32[]{:S(2)}, u32[]{:S(2)}) %collective-permute-start.12) | collective-permute-done | bytes 147488 | tf_op jit(solution)/shard_map/ppermute | solution.py:192
  72.4 2.8 %collective-permute-start.13 = (bf16[64,1152]{1,0:T(8,128)(2,1)S(1)}, bf16[64,1152]{1,0:T(8,128)(2,1)S(1)}, u32[]{:S(2)}, u32[]{:S(2)}) collective-permute-start(bf16[64,1152]{1,0:T(8,128)(2,1)S(1)} %shard_map.66.refs_1_), channel_id=1, source_target_pairs={{0,3},{3,0},{1,2},{2,1},{4,7},{7,4},{5,6},{6,5},{8,11},{11,8},{9,1... | collective-permute-start | bytes 442376 | tf_op jit(solution)/shard_map/ppermute | solution.py:196
  75.5 3.2 %collective-permute-done.13.refs_2_ = bf16[64,1152]{1,0:T(8,128)(2,1)S(1)} collective-permute-done((bf16[64,1152]{1,0:T(8,128)(2,1)S(1)}, bf16[64,1152]{1,0:T(8,128)(2,1)S(1)}, u32[]{:S(2)}, u32[]{:S(2)}) %collective-permute-start.13) | collective-permute-done | bytes 147488 | tf_op jit(solution)/shard_map/ppermute | solution.py:196
  78.8 0.8 shard_map.67
  79.6 0.7 collective-permute-done.16.refs_1_
  80.3 0.7 shard_map.71
  (32 shorter events, 3.5 us)
Async XLA Ops:
  0.6 0.8 %copy-start.1 = (s32[2048]{0:T(1024)S(1)}, s32[2048]{0:T(1024)}, u32[]{:S(2)}) copy-start(s32[2048]{0:T(1024)} %param.5) | copy-start | bytes 24580
  0.6 3.0 %collective-permute-start.1 = (bf16[2048,256]{1,0:T(8,128)(2,1)}, bf16[2048,256]{1,0:T(8,128)(2,1)S(1)}, u32[]{:S(2)}, u32[]{:S(2)}) collective-permute-start(bf16[2048,256]{1,0:T(8,128)(2,1)} %refs_1_.15), channel_id=1, source_target_pairs={{0,4},{4,0},{1,5},{5,1},{2,6},{6,2},{3,7},{7,3},{8,12},{12,8},{9,1... | collective-permute-start | bytes 3145736 | tf_op jit(solution)/shard_map/ppermute | solution.py:188
  1.5 1.2 %copy-start = (bf16[2048,256]{1,0:T(8,128)(2,1)S(1)}, bf16[2048,256]{1,0:T(8,128)(2,1)}, u32[]{:S(2)}) copy-start(bf16[2048,256]{1,0:T(8,128)(2,1)} %refs_1_.15) | copy-start | bytes 3145732
  1.5 1.9 %collective-permute-start = (s32[1,2048]{1,0:T(1,128)S(1)}, s32[1,2048]{1,0:T(1,128)S(1)}, u32[]{:S(2)}, u32[]{:S(2)}) collective-permute-start(s32[1,2048]{1,0:T(1,128)S(1)} %shard_map.50.refs_0_), channel_id=1, source_target_pairs={{0,4},{4,0},{1,5},{5,1},{2,6},{6,2},{3,7},{7,3},{8,12},{12,8},{9,1... | collective-permute-start | bytes 24584 | tf_op jit(solution)/shard_map/ppermute | solution.py:188
  4.3 7.6 %collective-permute-start.3 = (bf16[256,256]{1,0:T(8,128)(2,1)S(1)}, bf16[256,256]{1,0:T(8,128)(2,1)S(1)}, u32[]{:S(2)}, u32[]{:S(2)}) collective-permute-start(bf16[256,256]{1,0:T(8,128)(2,1)S(1)} %get-tuple-element.25.refs_4_), channel_id=1, source_target_pairs={{0,64},{64,0},{128,192},{192,128},{1,65},{65,1},{129,193},{193,129... | collective-permute-start | bytes 393224 | tf_op jit(solution)/shard_map/ppermute | solution.py:192
  6.6 6.8 %collective-permute-start.2 = (bf16[256,256]{1,0:T(8,128)(2,1)S(1)}, bf16[256,256]{1,0:T(8,128)(2,1)S(1)}, u32[]{:S(2)}, u32[]{:S(2)}) collective-permute-start(bf16[256,256]{1,0:T(8,128)(2,1)S(1)} %get-tuple-element.26.refs_5_), channel_id=1, source_target_pairs={{0,192},{192,0},{64,128},{128,64},{1,193},{193,1},{65,129},{129,65... | collective-permute-start | bytes 393224 | tf_op jit(solution)/shard_map/ppermute | solution.py:196
  8.5 8.1 %collective-permute-start.4 = (bf16[256,256]{1,0:T(8,128)(2,1)S(1)}, bf16[256,256]{1,0:T(8,128)(2,1)S(1)}, u32[]{:S(2)}, u32[]{:S(2)}) collective-permute-start(bf16[256,256]{1,0:T(8,128)(2,1)S(1)} %get-tuple-element.27.refs_4_), channel_id=1, source_target_pairs={{0,64},{64,0},{128,192},{192,128},{1,65},{65,1},{129,193},{193,129... | collective-permute-start | bytes 393224 | tf_op jit(solution)/shard_map/ppermute | solution.py:192
  9.9 6.7 %collective-permute-start.7 = (bf16[256,256]{1,0:T(8,128)(2,1)S(1)}, bf16[256,256]{1,0:T(8,128)(2,1)S(1)}, u32[]{:S(2)}, u32[]{:S(2)}) collective-permute-start(bf16[256,256]{1,0:T(8,128)(2,1)S(1)} %get-tuple-element.28.refs_5_), channel_id=1, source_target_pairs={{0,192},{192,0},{64,128},{128,64},{1,193},{193,1},{65,129},{129,65... | collective-permute-start | bytes 393224 | tf_op jit(solution)/shard_map/ppermute | solution.py:196
  11.9 5.8 %collective-permute-start.5 = (bf16[256,256]{1,0:T(8,128)(2,1)S(1)}, bf16[256,256]{1,0:T(8,128)(2,1)S(1)}, u32[]{:S(2)}, u32[]{:S(2)}) collective-permute-start(bf16[256,256]{1,0:T(8,128)(2,1)S(1)} %shard_map.56.refs_5_), channel_id=1, source_target_pairs={{0,192},{192,0},{64,128},{128,64},{1,193},{193,1},{65,129},{129,65... | collective-permute-start | bytes 393224 | tf_op jit(solution)/shard_map/ppermute | solution.py:196
  13.4 5.1 %collective-permute-start.6 = (bf16[256,256]{1,0:T(8,128)(2,1)S(1)}, bf16[256,256]{1,0:T(8,128)(2,1)S(1)}, u32[]{:S(2)}, u32[]{:S(2)}) collective-permute-start(bf16[256,256]{1,0:T(8,128)(2,1)S(1)} %shard_map.55.refs_4_), channel_id=1, source_target_pairs={{0,64},{64,0},{128,192},{192,128},{1,65},{65,1},{129,193},{193,129... | collective-permute-start | bytes 393224 | tf_op jit(solution)/shard_map/ppermute | solution.py:192
  50.2 11.5 %collective-permute-start.10 = (bf16[512,256]{1,0:T(8,128)(2,1)S(1)}, bf16[512,256]{1,0:T(8,128)(2,1)S(1)}, u32[]{:S(2)}, u32[]{:S(2)}) collective-permute-start(bf16[512,256]{1,0:T(8,128)(2,1)S(1)} %bitcast.7), channel_id=1, source_target_pairs={{0,192},{64,128},{128,64},{192,0},{4,68},{68,4},{132,196},{196,132... | collective-permute-start | bytes 786440 | tf_op jit(solution)/shard_map/ppermute | solution.py:201
  50.6 11.0 %collective-permute-start.9 = (bf16[512,256]{1,0:T(8,128)(2,1)S(1)}, bf16[512,256]{1,0:T(8,128)(2,1)S(1)}, u32[]{:S(2)}, u32[]{:S(2)}) collective-permute-start(bf16[512,256]{1,0:T(8,128)(2,1)S(1)} %bitcast.8), channel_id=1, source_target_pairs={{0,64},{64,0},{128,192},{192,128},{4,196},{68,132},{132,68},{196,4... | collective-permute-start | bytes 786440 | tf_op jit(solution)/shard_map/ppermute | solution.py:201
  53.2 11.0 %collective-permute-start.8 = (bf16[512,256]{1,0:T(8,128)(2,1)S(1)}, bf16[512,256]{1,0:T(8,128)(2,1)S(1)}, u32[]{:S(2)}, u32[]{:S(2)}) collective-permute-start(bf16[512,256]{1,0:T(8,128)(2,1)S(1)} %bitcast.9), channel_id=1, source_target_pairs={{0,128},{64,192},{128,0},{192,64},{4,132},{68,196},{132,4},{196,68... | collective-permute-start | bytes 786440 | tf_op jit(solution)/shard_map/ppermute | solution.py:201
  64.7 1.6 %collective-permute-start.11 = (bf16[64,1152]{1,0:T(8,128)(2,1)S(1)}, bf16[64,1152]{1,0:T(8,128)(2,1)S(1)}, u32[]{:S(2)}, u32[]{:S(2)}) collective-permute-start(bf16[64,1152]{1,0:T(8,128)(2,1)S(1)} %shard_map.62.refs_4_.refs_1_), channel_id=1, source_target_pairs={{0,4},{4,0},{1,5},{5,1},{2,6},{6,2},{3,7},{7,3},{8,12},{12,8},{9,1... | collective-permute-start | bytes 442376 | tf_op jit(solution)/shard_map/ppermute | solution.py:188
  65.2 3.1 %collective-permute-start.14 = (bf16[64,1024]{1,0:T(8,128)(2,1)S(1)}, bf16[64,1024]{1,0:T(8,128)(2,1)S(1)}, u32[]{:S(2)}, u32[]{:S(2)}) collective-permute-start(bf16[64,1024]{1,0:T(8,128)(2,1)S(1)} %shard_map.63.refs_4_.refs_1_), channel_id=1, source_target_pairs={{0,4},{4,0},{1,5},{5,1},{2,6},{6,2},{3,7},{7,3},{8,12},{12,8},{9,1... | collective-permute-start | bytes 393224 | tf_op jit(solution)/shard_map/ppermute | solution.py:188
  66.3 5.9 %collective-permute-start.12 = (bf16[64,1152]{1,0:T(8,128)(2,1)S(1)}, bf16[64,1152]{1,0:T(8,128)(2,1)S(1)}, u32[]{:S(2)}, u32[]{:S(2)}) collective-permute-start(bf16[64,1152]{1,0:T(8,128)(2,1)S(1)} %shard_map.65.refs_0_.refs_4_), channel_id=1, source_target_pairs={{0,1},{1,0},{2,3},{3,2},{4,5},{5,4},{6,7},{7,6},{8,9},{9,8},{10,11... | collective-permute-start | bytes 442376 | tf_op jit(solution)/shard_map/ppermute | solution.py:192
  68.4 6.8 %collective-permute-start.15 = (bf16[64,1024]{1,0:T(8,128)(2,1)S(1)}, bf16[64,1024]{1,0:T(8,128)(2,1)S(1)}, u32[]{:S(2)}, u32[]{:S(2)}) collective-permute-start(bf16[64,1024]{1,0:T(8,128)(2,1)S(1)} %shard_map.69.refs_0_), channel_id=1, source_target_pairs={{0,3},{3,0},{1,2},{2,1},{4,7},{7,4},{5,6},{6,5},{8,11},{11,8},{9,1... | collective-permute-start | bytes 393224 | tf_op jit(solution)/shard_map/ppermute | solution.py:196
  72.4 6.4 %collective-permute-start.13 = (bf16[64,1152]{1,0:T(8,128)(2,1)S(1)}, bf16[64,1152]{1,0:T(8,128)(2,1)S(1)}, u32[]{:S(2)}, u32[]{:S(2)}) collective-permute-start(bf16[64,1152]{1,0:T(8,128)(2,1)S(1)} %shard_map.66.refs_1_), channel_id=1, source_target_pairs={{0,3},{3,0},{1,2},{2,1},{4,7},{7,4},{5,6},{6,5},{8,11},{11,8},{9,1... | collective-permute-start | bytes 442376 | tf_op jit(solution)/shard_map/ppermute | solution.py:196
  75.2 5.1 %collective-permute-start.16 = (bf16[64,1024]{1,0:T(8,128)(2,1)S(1)}, bf16[64,1024]{1,0:T(8,128)(2,1)S(1)}, u32[]{:S(2)}, u32[]{:S(2)}) collective-permute-start(bf16[64,1024]{1,0:T(8,128)(2,1)S(1)} %shard_map.70.refs_0_), channel_id=1, source_target_pairs={{0,1},{1,0},{2,3},{3,2},{4,5},{5,4},{6,7},{7,6},{8,9},{9,8},{10,11... | collective-permute-start | bytes 393224 | tf_op jit(solution)/shard_map/ppermute | solution.py:192

commit v6 on v5

--- a/solution.py
+++ b/solution.py
@@ -85,15 +85,11 @@
         copies_ref[z * K : (z + 1) * K, :] = rounded
 
 
-def turned(k, core):
-    return k ^ (2 * core) if k & 1 else k
-
-
 def scores_kernel(groups, blocks, first, with_squares, packed, span, *refs):
     y, core = lax.axis_index("y"), lax.axis_index("core")
     group_refs, refs = refs[: 2 * groups], refs[2 * groups :]
     block_refs, refs = refs[: len(blocks)], refs[len(blocks) :]
-    numbers = [(y ^ turned(k, core)) * 16 + core for k in blocks]
+    numbers = [(y ^ k) * 16 + core for k in blocks]
     scores_in = squares_in = None
     if not first:
         scores_in, refs = refs[:groups], refs[groups:]
@@ -196,9 +192,8 @@
     return lax.ppermute(x, axis, [(0, 3), (3, 0), (1, 2), (2, 1)])
 
 
-def turn(x, k):
-    pairs = [(2 * i + core, 2 * (i ^ turned(k, core)) + core) for core in range(NC) for i in range(NY)]
-    return lax.ppermute(x, ("y", "core"), pairs)
+def across(x):
+    return lax.ppermute(x, "y", [(i, i ^ 2) for i in range(NY)])
 
 
 def body(embeddings, parent_ids, child_assignment):
@@ -241,8 +236,8 @@
     )
     mine = lax.all_to_all(copies, "z", 0, 0, tiled=True)
 
-    far = turn(mine, 2)
-    near = [turn(mine, 1), turn(mine, 3)]
+    far = across(mine)
+    near = [left(mine, "y"), right(mine, "y")]
 
     plain = jax.ShapeDtypeStruct((K, ROWS), BF16)
     squared = jax.ShapeDtypeStruct((K, PARENTS), F32)

time: 81.2 us -> 80.2 us (0.988); the launches traced: 81 us -> 78.8 us
  waiting for transfers between devices: 13.7 us -> 11.6 us
    ppermute x3 -> x1, waiting for transfers between devices: 6.17 us -> 0.36 us  [across(): return lax.ppermute(x, 'y', [(i, i ^ 2) for i in range(NY)])]
    ppermute x5 -> x6, waiting for transfers between devices: 4.36 us -> 8.04 us  [right(): return lax.ppermute(x, axis, [(0, 3), (3, 0), (1, 2), (2, 1)])]
    ppermute x3 -> x1, starting transfers between devices: 3.96 us -> 0.98 us  [across(): return lax.ppermute(x, 'y', [(i, i ^ 2) for i in range(NY)])]
    ppermute x5 -> x6, starting transfers between devices: 7.56 us -> 10.1 us  [left(): return lax.ppermute(x, axis, [(0, 1), (1, 0), (2, 3), (3, 2)])]
    ppermute x5 -> x6, starting transfers between devices: 7.75 us -> 8.21 us  [right(): return lax.ppermute(x, axis, [(0, 3), (3, 0), (1, 2), (2, 1)])]
    ppermute x5 -> x6, waiting for transfers between devices: 3.01 us -> 3.01 us  [left(): return lax.ppermute(x, axis, [(0, 1), (1, 0), (2, 3), (3, 2)])]
  transfers between devices with their start and end apart: 17 -> 17, of which waited for: 7 -> 8; matrix products, arithmetic and copies ran while one was open for 1% -> 1% of each run, Pallas kernels for 13% -> 14%
where the time goes in v6:
time: 80.2 us; the launch traced here: 78.8 us
  blocking collectives  31.6 us (39%)
  starting transfers between devices  20.6 us (26%)
  Pallas kernels  12.8 us (16%)
  waiting for transfers between devices  11.6 us (14%)
  between operations  0.86 us (1%)
    all_to_all x1, blocking collectives, body(): parts = lax.all_to_all(merged, 'z', 0, 0, tiled=True)  18.7 us
    all_to_all x1, blocking collectives, body(): mine = lax.all_to_all(copies, 'z', 0, 0, tiled=True)  12.9 us
    pallas_call x22, Pallas kernels, call(): pl.pallas_call(skipping, out_shape=out_shape, in_specs=[vmem] * (count +...  12.8 us
    ppermute x6, starting transfers between devices, left(): return lax.ppermute(x, axis, [(0, 1), (1, 0), (2, 3), (3, 2)])  10.1 us
    ppermute x6, starting transfers between devices, right(): return lax.ppermute(x, axis, [(0, 3), (3, 0), (1, 2), (2, 1)])  8.21 us
    ppermute x6, waiting for transfers between devices, right(): return lax.ppermute(x, axis, [(0, 3), (3, 0), (1, 2), (2, 1)])  8.04 us
    ppermute x6, waiting for transfers between devices, left(): return lax.ppermute(x, axis, [(0, 1), (1, 0), (2, 3), (3, 2)])  3.01 us
  transfers between devices with their start and end apart: 17, of which 8 were waited for; matrix products, arithmetic and copies ran while one was open for 1% of the time, Pallas kernels for 14%

profile of v6, /device:TPU:8, one launch (start us, length us, event | category | flops | bytes accessed | tf_op | source)
XLA Modules:
  0.0 78.8 jit_solution(2760343082424818352)
XLA Ops:
  0.7 0.7 broadcast_multiply_fusion
  1.5 0.6 collective-permute-start
  2.1 0.6 copy-done
  2.7 0.7 shard_map.51
  3.6 0.7 shard_map.52
  4.3 2.3 %collective-permute-start.3 = (bf16[256,256]{1,0:T(8,128)(2,1)S(1)}, bf16[256,256]{1,0:T(8,128)(2,1)S(1)}, u32[]{:S(2)}, u32[]{:S(2)}) collective-permute-start(bf16[256,256]{1,0:T(8,128)(2,1)S(1)} %get-tuple-element.25.refs_4_), channel_id=1, source_target_pairs={{0,64},{64,0},{128,192},{192,128},{1,65},{65,1},{129,193},{193,129... | collective-permute-start | bytes 393224 | tf_op jit(solution)/shard_map/ppermute | solution.py:188
  6.6 0.7 collective-permute-start.2
  7.3 1.2 %shard_map.53 = (bf16[256,256]{1,0:T(8,128)(2,1)S(1)}, bf16[256,256]{1,0:T(8,128)(2,1)S(1)}) custom-call(s32[1,2048]{1,0:T(1,128)S(1)} %shard_map.50.refs_0_, bf16[2048,256]{1,0:T(8,128)(2,1)S(1)} %copy-done, s32[1,2048]{1,0:T(1,128)S(1)} %collective-permute-done.refs_0_.refs_2_, bf16[2048,256]{1,0:T(8,128)(2,1)S(1)} %collective-permute-done.1.refs_1_.refs_3_, ...), custom_call_target="tpu_custom_call" | custom-call | flops 4294967296 | bytes 1000 | tf_op jit(solution)/shard_map/pallas_call | solution.py:35
  8.5 1.4 %collective-permute-start.4 = (bf16[256,256]{1,0:T(8,128)(2,1)S(1)}, bf16[256,256]{1,0:T(8,128)(2,1)S(1)}, u32[]{:S(2)}, u32[]{:S(2)}) collective-permute-start(bf16[256,256]{1,0:T(8,128)(2,1)S(1)} %get-tuple-element.27.refs_4_), channel_id=1, source_target_pairs={{0,64},{64,0},{128,192},{192,128},{1,65},{65,1},{129,193},{193,129... | collective-permute-start | bytes 393224 | tf_op jit(solution)/shard_map/ppermute | solution.py:188
  9.9 0.7 collective-permute-start.7
  10.6 1.2 %shard_map.54 = (f32[256,256]{1,0:T(8,128)S(1)}, f32[256,256]{1,0:T(8,128)S(1)}) custom-call(s32[1,2048]{1,0:T(1,128)S(1)} %shard_map.50.refs_0_, bf16[2048,256]{1,0:T(8,128)(2,1)S(1)} %copy-done, s32[1,2048]{1,0:T(1,128)S(1)} %collective-permute-done.refs_0_.refs_2_, bf16[2048,256]{1,0:T(8,128)(2,1)S(1)} %collective-permute-done.1.refs_1_.refs_3_, ...), custom_call_target="tpu_custom_call" | custom-call | flops 1000 | bytes 1000 | tf_op jit(solution)/shard_map/pallas_call | solution.py:35
  11.9 1.4 %collective-permute-start.5 = (bf16[256,256]{1,0:T(8,128)(2,1)S(1)}, bf16[256,256]{1,0:T(8,128)(2,1)S(1)}, u32[]{:S(2)}, u32[]{:S(2)}) collective-permute-start(bf16[256,256]{1,0:T(8,128)(2,1)S(1)} %shard_map.56.refs_5_), channel_id=1, source_target_pairs={{0,192},{192,0},{64,128},{128,64},{1,193},{193,1},{65,129},{129,65... | collective-permute-start | bytes 393224 | tf_op jit(solution)/shard_map/ppermute | solution.py:192
  13.4 2.0 %collective-permute-start.6 = (bf16[256,256]{1,0:T(8,128)(2,1)S(1)}, bf16[256,256]{1,0:T(8,128)(2,1)S(1)}, u32[]{:S(2)}, u32[]{:S(2)}) collective-permute-start(bf16[256,256]{1,0:T(8,128)(2,1)S(1)} %shard_map.55.refs_4_), channel_id=1, source_target_pairs={{0,64},{64,0},{128,192},{192,128},{1,65},{65,1},{129,193},{193,129... | collective-permute-start | bytes 393224 | tf_op jit(solution)/shard_map/ppermute | solution.py:188
  15.3 1.2 %shard_map.57 = (f32[256,256]{1,0:T(8,128)S(1)}, f32[256,256]{1,0:T(8,128)S(1)}) custom-call(s32[1,2048]{1,0:T(1,128)S(1)} %shard_map.50.refs_0_, bf16[2048,256]{1,0:T(8,128)(2,1)S(1)} %copy-done, s32[1,2048]{1,0:T(1,128)S(1)} %collective-permute-done.refs_0_.refs_2_, bf16[2048,256]{1,0:T(8,128)(2,1)S(1)} %collective-permute-done.1.refs_1_.refs_3_, ...), custom_call_target="tpu_custom_call" | custom-call | flops 1000 | bytes 1000 | tf_op jit(solution)/shard_map/pallas_call | solution.py:35
  16.6 1.1 %collective-permute-done.5.refs_3_ = bf16[256,256]{1,0:T(8,128)(2,1)S(1)} collective-permute-done((bf16[256,256]{1,0:T(8,128)(2,1)S(1)}, bf16[256,256]{1,0:T(8,128)(2,1)S(1)}, u32[]{:S(2)}, u32[]{:S(2)}) %collective-permute-start.5) | collective-permute-done | bytes 131104 | tf_op jit(solution)/shard_map/ppermute | solution.py:192
  17.7 0.7 collective-permute-done.6.refs_4_
  18.5 18.7 %all_to_all.22 = bf16[8,64,256]{2,1,0:T(8,128)(2,1)S(1)} all-to-all(bf16[8,64,256]{2,1,0:T(8,128)(2,1)S(1)} %bitcast.11), channel_id=1, replica_groups=mesh['y'=4,'z'=8,'core'=2,'feat'=4] {'z'}, dimensions={0} | all-to-all | bytes 524288 | tf_op jit(solution)/shard_map/all_to_all | solution.py:231
  37.3 12.9 %all_to_all.23 = bf16[8,64,256]{2,1,0:T(8,128)(2,1)S(1)} all-to-all(bf16[8,64,256]{2,1,0:T(8,128)(2,1)S(1)} %bitcast.13), channel_id=1, replica_groups=mesh['y'=4,'z'=8,'core'=2,'feat'=4] {'z'}, dimensions={0} | all-to-all | bytes 524288 | tf_op jit(solution)/shard_map/all_to_all | solution.py:237
  50.6 2.5 %collective-permute-start.9 = (bf16[512,256]{1,0:T(8,128)(2,1)S(1)}, bf16[512,256]{1,0:T(8,128)(2,1)S(1)}, u32[]{:S(2)}, u32[]{:S(2)}) collective-permute-start(bf16[512,256]{1,0:T(8,128)(2,1)S(1)} %bitcast.8), channel_id=1, source_target_pairs={{0,64},{64,0},{128,192},{192,128},{1,65},{65,1},{129,193},{193,129... | collective-permute-start | bytes 786440 | tf_op jit(solution)/shard_map/ppermute | solution.py:188
  53.2 1.0 %collective-permute-start.8 = (bf16[512,256]{1,0:T(8,128)(2,1)S(1)}, bf16[512,256]{1,0:T(8,128)(2,1)S(1)}, u32[]{:S(2)}, u32[]{:S(2)}) collective-permute-start(bf16[512,256]{1,0:T(8,128)(2,1)S(1)} %bitcast.9), channel_id=1, source_target_pairs={{0,128},{64,192},{128,0},{192,64},{1,129},{65,193},{129,1},{193,65... | collective-permute-start | bytes 786440 | tf_op jit(solution)/shard_map/ppermute | solution.py:196
  54.2 1.4 %shard_map.60 = (bf16[64,2048]{1,0:T(8,128)(2,1)S(1)}, bf16[64,2048]{1,0:T(8,128)(2,1)S(1)}, f32[64,64]{1,0:T(8,128)S(1)}) custom-call(s32[1,2048]{1,0:T(1,128)S(1)} %shard_map.50.refs_0_, bf16[2048,256]{1,0:T(8,128)(2,1)S(1)} %copy-done, s32[1,2048]{1,0:T(1,128)S(1)} %collective-permute-done.refs_0_.refs_2_, ...), custom_call_target="tpu_custom_call" | custom-call | flops 1000 | bytes 1000 | tf_op jit(solution)/shard_map/pallas_call | solution.py:35
  55.5 3.7 %collective-permute-done.10.refs_5_ = bf16[512,256]{1,0:T(8,128)(2,1)S(1)} collective-permute-done((bf16[512,256]{1,0:T(8,128)(2,1)S(1)}, bf16[512,256]{1,0:T(8,128)(2,1)S(1)}, u32[]{:S(2)}, u32[]{:S(2)}) %collective-permute-start.10) | collective-permute-done | bytes 262176 | tf_op jit(solution)/shard_map/ppermute | solution.py:192
  59.2 2.5 %shard_map.61 = (bf16[64,2048]{1,0:T(8,128)(2,1)S(1)}, bf16[64,2048]{1,0:T(8,128)(2,1)S(1)}, f32[64,64]{1,0:T(8,128)S(1)}) custom-call(s32[1,2048]{1,0:T(1,128)S(1)} %shard_map.50.refs_0_, bf16[2048,256]{1,0:T(8,128)(2,1)S(1)} %copy-done, s32[1,2048]{1,0:T(1,128)S(1)} %collective-permute-done.refs_0_.refs_2_, ...), custom_call_target="tpu_custom_call" | custom-call | flops 1000 | bytes 1000 | tf_op jit(solution)/shard_map/pallas_call | solution.py:35
  63.1 0.6 collective-permute-start.14
  64.2 1.6 %collective-permute-start.12 = (bf16[64,1152]{1,0:T(8,128)(2,1)S(1)}, bf16[64,1152]{1,0:T(8,128)(2,1)S(1)}, u32[]{:S(2)}, u32[]{:S(2)}) collective-permute-start(bf16[64,1152]{1,0:T(8,128)(2,1)S(1)} %shard_map.65.refs_0_.refs_4_), channel_id=1, source_target_pairs={{0,1},{1,0},{2,3},{3,2},{4,5},{5,4},{6,7},{7,6},{8,9},{9,8},{10,11... | collective-permute-start | bytes 442376 | tf_op jit(solution)/shard_map/ppermute | solution.py:188
  66.3 2.2 %collective-permute-start.15 = (bf16[64,1024]{1,0:T(8,128)(2,1)S(1)}, bf16[64,1024]{1,0:T(8,128)(2,1)S(1)}, u32[]{:S(2)}, u32[]{:S(2)}) collective-permute-start(bf16[64,1024]{1,0:T(8,128)(2,1)S(1)} %shard_map.69.refs_0_), channel_id=1, source_target_pairs={{0,3},{3,0},{1,2},{2,1},{4,7},{7,4},{5,6},{6,5},{8,11},{11,8},{9,1... | collective-permute-start | bytes 393224 | tf_op jit(solution)/shard_map/ppermute | solution.py:192
  68.5 1.6 %collective-permute-done.12.refs_1_ = bf16[64,1152]{1,0:T(8,128)(2,1)S(1)} collective-permute-done((bf16[64,1152]{1,0:T(8,128)(2,1)S(1)}, bf16[64,1152]{1,0:T(8,128)(2,1)S(1)}, u32[]{:S(2)}, u32[]{:S(2)}) %collective-permute-start.12) | collective-permute-done | bytes 147488 | tf_op jit(solution)/shard_map/ppermute | solution.py:188
  70.2 2.8 %collective-permute-start.13 = (bf16[64,1152]{1,0:T(8,128)(2,1)S(1)}, bf16[64,1152]{1,0:T(8,128)(2,1)S(1)}, u32[]{:S(2)}, u32[]{:S(2)}) collective-permute-start(bf16[64,1152]{1,0:T(8,128)(2,1)S(1)} %shard_map.66.refs_1_), channel_id=1, source_target_pairs={{0,3},{3,0},{1,2},{2,1},{4,7},{7,4},{5,6},{6,5},{8,11},{11,8},{9,1... | collective-permute-start | bytes 442376 | tf_op jit(solution)/shard_map/ppermute | solution.py:192
  73.4 3.2 %collective-permute-done.13.refs_2_ = bf16[64,1152]{1,0:T(8,128)(2,1)S(1)} collective-permute-done((bf16[64,1152]{1,0:T(8,128)(2,1)S(1)}, bf16[64,1152]{1,0:T(8,128)(2,1)S(1)}, u32[]{:S(2)}, u32[]{:S(2)}) %collective-permute-start.13) | collective-permute-done | bytes 147488 | tf_op jit(solution)/shard_map/ppermute | solution.py:192
  76.6 0.8 %shard_map.67 = (f32[64,1024]{1,0:T(8,128)S(1)}, bf16[64,256]{1,0:T(8,128)(2,1)}, f32[1,1024]{1,0:T(1,128)S(1)}) custom-call(s32[1,2048]{1,0:T(1,128)S(1)} %shard_map.50.refs_0_, bf16[64,1152]{1,0:T(8,128)(2,1)S(1)} %shard_map.66.refs_1_, bf16[64,1152]{1,0:T(8,128)(2,1)S(1)} %collective-permute-done.13.refs_2_, f32[64,256]{1,0:T(8,128)S(1)} %get-tuple-element.40.refs_3_), custom_call_target="tpu_custom_call" | custom-call | flops 1000 | bytes 1000 | tf_op jit(solution)/shard_map/pallas_call | solution.py:35
  77.4 0.7 collective-permute-done.16.refs_1_
  78.1 0.7 shard_map.71
  (32 shorter events, 3.8 us)
Async XLA Ops:
  0.6 0.8 %copy-start.1 = (s32[2048]{0:T(1024)S(1)}, s32[2048]{0:T(1024)}, u32[]{:S(2)}) copy-start(s32[2048]{0:T(1024)} %param.5) | copy-start | bytes 24580
  0.6 3.0 %collective-permute-start.1 = (bf16[2048,256]{1,0:T(8,128)(2,1)}, bf16[2048,256]{1,0:T(8,128)(2,1)S(1)}, u32[]{:S(2)}, u32[]{:S(2)}) collective-permute-start(bf16[2048,256]{1,0:T(8,128)(2,1)} %refs_1_.15), channel_id=1, source_target_pairs={{0,4},{4,0},{1,5},{5,1},{2,6},{6,2},{3,7},{7,3},{8,12},{12,8},{9,1... | collective-permute-start | bytes 3145736 | tf_op jit(solution)/shard_map/ppermute | solution.py:184
  1.5 1.2 %copy-start = (bf16[2048,256]{1,0:T(8,128)(2,1)S(1)}, bf16[2048,256]{1,0:T(8,128)(2,1)}, u32[]{:S(2)}) copy-start(bf16[2048,256]{1,0:T(8,128)(2,1)} %refs_1_.15) | copy-start | bytes 3145732
  1.5 1.9 %collective-permute-start = (s32[1,2048]{1,0:T(1,128)S(1)}, s32[1,2048]{1,0:T(1,128)S(1)}, u32[]{:S(2)}, u32[]{:S(2)}) collective-permute-start(s32[1,2048]{1,0:T(1,128)S(1)} %shard_map.50.refs_0_), channel_id=1, source_target_pairs={{0,4},{4,0},{1,5},{5,1},{2,6},{6,2},{3,7},{7,3},{8,12},{12,8},{9,1... | collective-permute-start | bytes 24584 | tf_op jit(solution)/shard_map/ppermute | solution.py:184
  4.3 7.6 %collective-permute-start.3 = (bf16[256,256]{1,0:T(8,128)(2,1)S(1)}, bf16[256,256]{1,0:T(8,128)(2,1)S(1)}, u32[]{:S(2)}, u32[]{:S(2)}) collective-permute-start(bf16[256,256]{1,0:T(8,128)(2,1)S(1)} %get-tuple-element.25.refs_4_), channel_id=1, source_target_pairs={{0,64},{64,0},{128,192},{192,128},{1,65},{65,1},{129,193},{193,129... | collective-permute-start | bytes 393224 | tf_op jit(solution)/shard_map/ppermute | solution.py:188
  6.6 6.8 %collective-permute-start.2 = (bf16[256,256]{1,0:T(8,128)(2,1)S(1)}, bf16[256,256]{1,0:T(8,128)(2,1)S(1)}, u32[]{:S(2)}, u32[]{:S(2)}) collective-permute-start(bf16[256,256]{1,0:T(8,128)(2,1)S(1)} %get-tuple-element.26.refs_5_), channel_id=1, source_target_pairs={{0,192},{192,0},{64,128},{128,64},{1,193},{193,1},{65,129},{129,65... | collective-permute-start | bytes 393224 | tf_op jit(solution)/shard_map/ppermute | solution.py:192
  8.5 8.1 %collective-permute-start.4 = (bf16[256,256]{1,0:T(8,128)(2,1)S(1)}, bf16[256,256]{1,0:T(8,128)(2,1)S(1)}, u32[]{:S(2)}, u32[]{:S(2)}) collective-permute-start(bf16[256,256]{1,0:T(8,128)(2,1)S(1)} %get-tuple-element.27.refs_4_), channel_id=1, source_target_pairs={{0,64},{64,0},{128,192},{192,128},{1,65},{65,1},{129,193},{193,129... | collective-permute-start | bytes 393224 | tf_op jit(solution)/shard_map/ppermute | solution.py:188
  9.9 6.7 %collective-permute-start.7 = (bf16[256,256]{1,0:T(8,128)(2,1)S(1)}, bf16[256,256]{1,0:T(8,128)(2,1)S(1)}, u32[]{:S(2)}, u32[]{:S(2)}) collective-permute-start(bf16[256,256]{1,0:T(8,128)(2,1)S(1)} %get-tuple-element.28.refs_5_), channel_id=1, source_target_pairs={{0,192},{192,0},{64,128},{128,64},{1,193},{193,1},{65,129},{129,65... | collective-permute-start | bytes 393224 | tf_op jit(solution)/shard_map/ppermute | solution.py:192
  11.9 5.8 %collective-permute-start.5 = (bf16[256,256]{1,0:T(8,128)(2,1)S(1)}, bf16[256,256]{1,0:T(8,128)(2,1)S(1)}, u32[]{:S(2)}, u32[]{:S(2)}) collective-permute-start(bf16[256,256]{1,0:T(8,128)(2,1)S(1)} %shard_map.56.refs_5_), channel_id=1, source_target_pairs={{0,192},{192,0},{64,128},{128,64},{1,193},{193,1},{65,129},{129,65... | collective-permute-start | bytes 393224 | tf_op jit(solution)/shard_map/ppermute | solution.py:192
  13.4 5.1 %collective-permute-start.6 = (bf16[256,256]{1,0:T(8,128)(2,1)S(1)}, bf16[256,256]{1,0:T(8,128)(2,1)S(1)}, u32[]{:S(2)}, u32[]{:S(2)}) collective-permute-start(bf16[256,256]{1,0:T(8,128)(2,1)S(1)} %shard_map.55.refs_4_), channel_id=1, source_target_pairs={{0,64},{64,0},{128,192},{192,128},{1,65},{65,1},{129,193},{193,129... | collective-permute-start | bytes 393224 | tf_op jit(solution)/shard_map/ppermute | solution.py:188
  50.2 9.0 %collective-permute-start.10 = (bf16[512,256]{1,0:T(8,128)(2,1)S(1)}, bf16[512,256]{1,0:T(8,128)(2,1)S(1)}, u32[]{:S(2)}, u32[]{:S(2)}) collective-permute-start(bf16[512,256]{1,0:T(8,128)(2,1)S(1)} %bitcast.7), channel_id=1, source_target_pairs={{0,192},{192,0},{64,128},{128,64},{1,193},{193,1},{65,129},{129,65... | collective-permute-start | bytes 786440 | tf_op jit(solution)/shard_map/ppermute | solution.py:192
  50.6 8.6 %collective-permute-start.9 = (bf16[512,256]{1,0:T(8,128)(2,1)S(1)}, bf16[512,256]{1,0:T(8,128)(2,1)S(1)}, u32[]{:S(2)}, u32[]{:S(2)}) collective-permute-start(bf16[512,256]{1,0:T(8,128)(2,1)S(1)} %bitcast.8), channel_id=1, source_target_pairs={{0,64},{64,0},{128,192},{192,128},{1,65},{65,1},{129,193},{193,129... | collective-permute-start | bytes 786440 | tf_op jit(solution)/shard_map/ppermute | solution.py:188
  53.2 8.9 %collective-permute-start.8 = (bf16[512,256]{1,0:T(8,128)(2,1)S(1)}, bf16[512,256]{1,0:T(8,128)(2,1)S(1)}, u32[]{:S(2)}, u32[]{:S(2)}) collective-permute-start(bf16[512,256]{1,0:T(8,128)(2,1)S(1)} %bitcast.9), channel_id=1, source_target_pairs={{0,128},{64,192},{128,0},{192,64},{1,129},{65,193},{129,1},{193,65... | collective-permute-start | bytes 786440 | tf_op jit(solution)/shard_map/ppermute | solution.py:196
  62.5 1.6 %collective-permute-start.11 = (bf16[64,1152]{1,0:T(8,128)(2,1)S(1)}, bf16[64,1152]{1,0:T(8,128)(2,1)S(1)}, u32[]{:S(2)}, u32[]{:S(2)}) collective-permute-start(bf16[64,1152]{1,0:T(8,128)(2,1)S(1)} %shard_map.62.refs_4_.refs_1_), channel_id=1, source_target_pairs={{0,4},{4,0},{1,5},{5,1},{2,6},{6,2},{3,7},{7,3},{8,12},{12,8},{9,1... | collective-permute-start | bytes 442376 | tf_op jit(solution)/shard_map/ppermute | solution.py:184
  63.1 3.1 %collective-permute-start.14 = (bf16[64,1024]{1,0:T(8,128)(2,1)S(1)}, bf16[64,1024]{1,0:T(8,128)(2,1)S(1)}, u32[]{:S(2)}, u32[]{:S(2)}) collective-permute-start(bf16[64,1024]{1,0:T(8,128)(2,1)S(1)} %shard_map.63.refs_4_.refs_1_), channel_id=1, source_target_pairs={{0,4},{4,0},{1,5},{5,1},{2,6},{6,2},{3,7},{7,3},{8,12},{12,8},{9,1... | collective-permute-start | bytes 393224 | tf_op jit(solution)/shard_map/ppermute | solution.py:184
  64.2 5.9 %collective-permute-start.12 = (bf16[64,1152]{1,0:T(8,128)(2,1)S(1)}, bf16[64,1152]{1,0:T(8,128)(2,1)S(1)}, u32[]{:S(2)}, u32[]{:S(2)}) collective-permute-start(bf16[64,1152]{1,0:T(8,128)(2,1)S(1)} %shard_map.65.refs_0_.refs_4_), channel_id=1, source_target_pairs={{0,1},{1,0},{2,3},{3,2},{4,5},{5,4},{6,7},{7,6},{8,9},{9,8},{10,11... | collective-permute-start | bytes 442376 | tf_op jit(solution)/shard_map/ppermute | solution.py:188
  66.3 6.8 %collective-permute-start.15 = (bf16[64,1024]{1,0:T(8,128)(2,1)S(1)}, bf16[64,1024]{1,0:T(8,128)(2,1)S(1)}, u32[]{:S(2)}, u32[]{:S(2)}) collective-permute-start(bf16[64,1024]{1,0:T(8,128)(2,1)S(1)} %shard_map.69.refs_0_), channel_id=1, source_target_pairs={{0,3},{3,0},{1,2},{2,1},{4,7},{7,4},{5,6},{6,5},{8,11},{11,8},{9,1... | collective-permute-start | bytes 393224 | tf_op jit(solution)/shard_map/ppermute | solution.py:192
  70.2 6.4 %collective-permute-start.13 = (bf16[64,1152]{1,0:T(8,128)(2,1)S(1)}, bf16[64,1152]{1,0:T(8,128)(2,1)S(1)}, u32[]{:S(2)}, u32[]{:S(2)}) collective-permute-start(bf16[64,1152]{1,0:T(8,128)(2,1)S(1)} %shard_map.66.refs_1_), channel_id=1, source_target_pairs={{0,3},{3,0},{1,2},{2,1},{4,7},{7,4},{5,6},{6,5},{8,11},{11,8},{9,1... | collective-permute-start | bytes 442376 | tf_op jit(solution)/shard_map/ppermute | solution.py:192
  73.1 5.1 %collective-permute-start.16 = (bf16[64,1024]{1,0:T(8,128)(2,1)S(1)}, bf16[64,1024]{1,0:T(8,128)(2,1)S(1)}, u32[]{:S(2)}, u32[]{:S(2)}) collective-permute-start(bf16[64,1024]{1,0:T(8,128)(2,1)S(1)} %shard_map.70.refs_0_), channel_id=1, source_target_pairs={{0,1},{1,0},{2,3},{3,2},{4,5},{5,4},{6,7},{7,6},{8,9},{9,8},{10,11... | collective-permute-start | bytes 393224 | tf_op jit(solution)/shard_map/ppermute | solution.py:188

commit v7 on v6

--- a/solution.py
+++ b/solution.py
@@ -216,17 +216,17 @@
 
     halves = ((2, 0), (2, 1))
     far_low, far_high = sums(halves, BF16, [other], sums(halves, F32, [own]))
-    got_low, got_high = left(far_low, "y"), right(far_high, "y")
-    left_low, right_high = sums(((1, 0), (3, 1)), BF16, [own, other], behind=[far_low, far_high], flops=LONG)
-    own_high, own_low = sums(((1, 1), (3, 0)), F32, [own, other], behind=[left_low, right_high])
+    got_low, got_high = right(far_low, "y"), left(far_high, "y")
+    right_low, left_high = sums(((3, 0), (1, 1)), BF16, [own, other], behind=[far_low, far_high], flops=LONG)
+    own_high, own_low = sums(((3, 1), (1, 0)), F32, [own, other], behind=[right_low, left_high])
     half = jax.ShapeDtypeStruct((HALF, WIDTH), BF16)
-    right_low = call(hand_on_kernel, half, [own_low, got_low])
-    left_high = call(hand_on_kernel, half, [own_high, got_high])
-    kept = sums(((0, 0), (0, 1)), F32, [own, other], behind=[left_high, right_low])
+    left_low = call(hand_on_kernel, half, [own_low, got_low])
+    right_high = call(hand_on_kernel, half, [own_high, got_high])
+    kept = sums(((0, 0), (0, 1)), F32, [own, other], behind=[right_high, left_low])
     merged = call(
         merge_kernel,
         jax.ShapeDtypeStruct((PIECE, WIDTH), BF16),
-        [*kept, left(left_low, "y"), right(right_low, "y"), left(left_high, "y"), right(right_high, "y")],
+        [*kept, right(right_low, "y"), left(left_low, "y"), right(right_high, "y"), left(left_high, "y")],
     )
     parts = lax.all_to_all(merged, "z", 0, 0, tiled=True)
     totals, copies = call(

time: 80.2 us -> 79.9 us (level)
  blocking collectives: 31.6 us -> 30.5 us
  waiting for transfers between devices: 11.6 us -> 12.7 us
    ppermute x6, starting transfers between devices: 8.21 us -> 10.7 us  [right(): return lax.ppermute(x, axis, [(0, 3), (3, 0), (1, 2), (2, 1)])]
    ppermute x6, starting transfers between devices: 10.1 us -> 8.24 us  [left(): return lax.ppermute(x, axis, [(0, 1), (1, 0), (2, 3), (3, 2)])]
    ppermute x6, waiting for transfers between devices: 3.01 us -> 4.62 us  [left(): return lax.ppermute(x, axis, [(0, 1), (1, 0), (2, 3), (3, 2)])]
    all_to_all x1, blocking collectives: 18.7 us -> 17.6 us  [body(): parts = lax.all_to_all(merged, 'z', 0, 0, tiled=True)]
    ppermute x6, waiting for transfers between devices: 8.04 us -> 7.05 us  [right(): return lax.ppermute(x, axis, [(0, 3), (3, 0), (1, 2), (2, 1)])]
  transfers between devices with their start and end apart: 17 -> 17, of which waited for: 8 -> 9; matrix products, arithmetic and copies ran while one was open for 1% -> 1% of each run, Pallas kernels for 14% -> 14%
where the time goes in v7:
time: 79.9 us; the launch traced here: 78.7 us
  blocking collectives  30.5 us (38%)
  starting transfers between devices  20.6 us (26%)
  Pallas kernels  12.8 us (16%)
  waiting for transfers between devices  12.7 us (16%)
  between operations  0.85 us (1%)
    all_to_all x1, blocking collectives, body(): parts = lax.all_to_all(merged, 'z', 0, 0, tiled=True)  17.6 us
    all_to_all x1, blocking collectives, body(): mine = lax.all_to_all(copies, 'z', 0, 0, tiled=True)  12.9 us
    pallas_call x22, Pallas kernels, call(): pl.pallas_call(skipping, out_shape=out_shape, in_specs=[vmem] * (count +...  12.8 us
    ppermute x6, starting transfers between devices, right(): return lax.ppermute(x, axis, [(0, 3), (3, 0), (1, 2), (2, 1)])  10.7 us
    ppermute x6, starting transfers between devices, left(): return lax.ppermute(x, axis, [(0, 1), (1, 0), (2, 3), (3, 2)])  8.24 us
    ppermute x6, waiting for transfers between devices, right(): return lax.ppermute(x, axis, [(0, 3), (3, 0), (1, 2), (2, 1)])  7.05 us
    ppermute x6, waiting for transfers between devices, left(): return lax.ppermute(x, axis, [(0, 1), (1, 0), (2, 3), (3, 2)])  4.62 us
  transfers between devices with their start and end apart: 17, of which 9 were waited for; matrix products, arithmetic and copies ran while one was open for 1% of the time, Pallas kernels for 14%

profile of v7, /device:TPU:8, one launch (start us, length us, event | category | flops | bytes accessed | tf_op | source)
XLA Modules:
  0.0 78.7 jit_solution(16791363208057350740)
XLA Ops:
  0.7 0.7 broadcast_multiply_fusion
  2.1 0.6 copy-done
  2.7 0.7 shard_map.51
  3.6 0.7 shard_map.52
  4.3 1.7 %collective-permute-start.3 = (bf16[256,256]{1,0:T(8,128)(2,1)S(1)}, bf16[256,256]{1,0:T(8,128)(2,1)S(1)}, u32[]{:S(2)}, u32[]{:S(2)}) collective-permute-start(bf16[256,256]{1,0:T(8,128)(2,1)S(1)} %get-tuple-element.25.refs_4_), channel_id=1, source_target_pairs={{0,192},{192,0},{64,128},{128,64},{1,193},{193,1},{65,129},{129,65... | collective-permute-start | bytes 393224 | tf_op jit(solution)/shard_map/ppermute | solution.py:192
  6.0 1.9 %collective-permute-start.2 = (bf16[256,256]{1,0:T(8,128)(2,1)S(1)}, bf16[256,256]{1,0:T(8,128)(2,1)S(1)}, u32[]{:S(2)}, u32[]{:S(2)}) collective-permute-start(bf16[256,256]{1,0:T(8,128)(2,1)S(1)} %get-tuple-element.26.refs_5_), channel_id=1, source_target_pairs={{0,64},{64,0},{128,192},{192,128},{1,65},{65,1},{129,193},{193,129... | collective-permute-start | bytes 393224 | tf_op jit(solution)/shard_map/ppermute | solution.py:188
  7.9 1.2 %shard_map.53 = (bf16[256,256]{1,0:T(8,128)(2,1)S(1)}, bf16[256,256]{1,0:T(8,128)(2,1)S(1)}) custom-call(s32[1,2048]{1,0:T(1,128)S(1)} %shard_map.50.refs_0_, bf16[2048,256]{1,0:T(8,128)(2,1)S(1)} %copy-done, s32[1,2048]{1,0:T(1,128)S(1)} %collective-permute-done.refs_0_.refs_2_, bf16[2048,256]{1,0:T(8,128)(2,1)S(1)} %collective-permute-done.1.refs_1_.refs_3_, ...), custom_call_target="tpu_custom_call" | custom-call | flops 4294967296 | bytes 1000 | tf_op jit(solution)/shard_map/pallas_call | solution.py:35
  9.1 1.4 %collective-permute-start.4 = (bf16[256,256]{1,0:T(8,128)(2,1)S(1)}, bf16[256,256]{1,0:T(8,128)(2,1)S(1)}, u32[]{:S(2)}, u32[]{:S(2)}) collective-permute-start(bf16[256,256]{1,0:T(8,128)(2,1)S(1)} %get-tuple-element.27.refs_4_), channel_id=1, source_target_pairs={{0,192},{192,0},{64,128},{128,64},{1,193},{193,1},{65,129},{129,65... | collective-permute-start | bytes 393224 | tf_op jit(solution)/shard_map/ppermute | solution.py:192
  10.5 0.6 collective-permute-start.7
  11.2 1.2 %shard_map.54 = (f32[256,256]{1,0:T(8,128)S(1)}, f32[256,256]{1,0:T(8,128)S(1)}) custom-call(s32[1,2048]{1,0:T(1,128)S(1)} %shard_map.50.refs_0_, bf16[2048,256]{1,0:T(8,128)(2,1)S(1)} %copy-done, s32[1,2048]{1,0:T(1,128)S(1)} %collective-permute-done.refs_0_.refs_2_, bf16[2048,256]{1,0:T(8,128)(2,1)S(1)} %collective-permute-done.1.refs_1_.refs_3_, ...), custom_call_target="tpu_custom_call" | custom-call | flops 1000 | bytes 1000 | tf_op jit(solution)/shard_map/pallas_call | solution.py:35
  12.4 1.6 %collective-permute-start.5 = (bf16[256,256]{1,0:T(8,128)(2,1)S(1)}, bf16[256,256]{1,0:T(8,128)(2,1)S(1)}, u32[]{:S(2)}, u32[]{:S(2)}) collective-permute-start(bf16[256,256]{1,0:T(8,128)(2,1)S(1)} %shard_map.56.refs_5_), channel_id=1, source_target_pairs={{0,64},{64,0},{128,192},{192,128},{1,65},{65,1},{129,193},{193,129... | collective-permute-start | bytes 393224 | tf_op jit(solution)/shard_map/ppermute | solution.py:188
  14.1 0.7 collective-permute-start.6
  14.7 1.2 %shard_map.57 = (f32[256,256]{1,0:T(8,128)S(1)}, f32[256,256]{1,0:T(8,128)S(1)}) custom-call(s32[1,2048]{1,0:T(1,128)S(1)} %shard_map.50.refs_0_, bf16[2048,256]{1,0:T(8,128)(2,1)S(1)} %copy-done, s32[1,2048]{1,0:T(1,128)S(1)} %collective-permute-done.refs_0_.refs_2_, bf16[2048,256]{1,0:T(8,128)(2,1)S(1)} %collective-permute-done.1.refs_1_.refs_3_, ...), custom_call_target="tpu_custom_call" | custom-call | flops 1000 | bytes 1000 | tf_op jit(solution)/shard_map/pallas_call | solution.py:35
  16.5 1.8 %collective-permute-done.5.refs_3_ = bf16[256,256]{1,0:T(8,128)(2,1)S(1)} collective-permute-done((bf16[256,256]{1,0:T(8,128)(2,1)S(1)}, bf16[256,256]{1,0:T(8,128)(2,1)S(1)}, u32[]{:S(2)}, u32[]{:S(2)}) %collective-permute-start.5) | collective-permute-done | bytes 131104 | tf_op jit(solution)/shard_map/ppermute | solution.py:188
  18.3 0.8 %collective-permute-done.6.refs_4_ = bf16[256,256]{1,0:T(8,128)(2,1)S(1)} collective-permute-done((bf16[256,256]{1,0:T(8,128)(2,1)S(1)}, bf16[256,256]{1,0:T(8,128)(2,1)S(1)}, u32[]{:S(2)}, u32[]{:S(2)}) %collective-permute-start.6) | collective-permute-done | bytes 131104 | tf_op jit(solution)/shard_map/ppermute | solution.py:192
  19.2 17.6 %all_to_all.22 = bf16[8,64,256]{2,1,0:T(8,128)(2,1)S(1)} all-to-all(bf16[8,64,256]{2,1,0:T(8,128)(2,1)S(1)} %bitcast.11), channel_id=1, replica_groups=mesh['y'=4,'z'=8,'core'=2,'feat'=4] {'z'}, dimensions={0} | all-to-all | bytes 524288 | tf_op jit(solution)/shard_map/all_to_all | solution.py:231
  36.9 12.9 %all_to_all.23 = bf16[8,64,256]{2,1,0:T(8,128)(2,1)S(1)} all-to-all(bf16[8,64,256]{2,1,0:T(8,128)(2,1)S(1)} %bitcast.13), channel_id=1, replica_groups=mesh['y'=4,'z'=8,'core'=2,'feat'=4] {'z'}, dimensions={0} | all-to-all | bytes 524288 | tf_op jit(solution)/shard_map/all_to_all | solution.py:237
  49.8 2.0 %collective-permute-start.10 = (bf16[512,256]{1,0:T(8,128)(2,1)S(1)}, bf16[512,256]{1,0:T(8,128)(2,1)S(1)}, u32[]{:S(2)}, u32[]{:S(2)}) collective-permute-start(bf16[512,256]{1,0:T(8,128)(2,1)S(1)} %bitcast.7), channel_id=1, source_target_pairs={{0,192},{192,0},{64,128},{128,64},{1,193},{193,1},{65,129},{129,65... | collective-permute-start | bytes 786440 | tf_op jit(solution)/shard_map/ppermute | solution.py:192
  51.7 2.3 %collective-permute-start.9 = (bf16[512,256]{1,0:T(8,128)(2,1)S(1)}, bf16[512,256]{1,0:T(8,128)(2,1)S(1)}, u32[]{:S(2)}, u32[]{:S(2)}) collective-permute-start(bf16[512,256]{1,0:T(8,128)(2,1)S(1)} %bitcast.8), channel_id=1, source_target_pairs={{0,64},{64,0},{128,192},{192,128},{1,65},{65,1},{129,193},{193,129... | collective-permute-start | bytes 786440 | tf_op jit(solution)/shard_map/ppermute | solution.py:188
  54.3 1.4 %shard_map.60 = (bf16[64,2048]{1,0:T(8,128)(2,1)S(1)}, bf16[64,2048]{1,0:T(8,128)(2,1)S(1)}, f32[64,64]{1,0:T(8,128)S(1)}) custom-call(s32[1,2048]{1,0:T(1,128)S(1)} %shard_map.50.refs_0_, bf16[2048,256]{1,0:T(8,128)(2,1)S(1)} %copy-done, s32[1,2048]{1,0:T(1,128)S(1)} %collective-permute-done.refs_0_.refs_2_, ...), custom_call_target="tpu_custom_call" | custom-call | flops 1000 | bytes 1000 | tf_op jit(solution)/shard_map/pallas_call | solution.py:35
  55.6 3.0 %collective-permute-done.10.refs_5_ = bf16[512,256]{1,0:T(8,128)(2,1)S(1)} collective-permute-done((bf16[512,256]{1,0:T(8,128)(2,1)S(1)}, bf16[512,256]{1,0:T(8,128)(2,1)S(1)}, u32[]{:S(2)}, u32[]{:S(2)}) %collective-permute-start.10) | collective-permute-done | bytes 262176 | tf_op jit(solution)/shard_map/ppermute | solution.py:192
  58.6 2.5 %shard_map.61 = (bf16[64,2048]{1,0:T(8,128)(2,1)S(1)}, bf16[64,2048]{1,0:T(8,128)(2,1)S(1)}, f32[64,64]{1,0:T(8,128)S(1)}) custom-call(s32[1,2048]{1,0:T(1,128)S(1)} %shard_map.50.refs_0_, bf16[2048,256]{1,0:T(8,128)(2,1)S(1)} %copy-done, s32[1,2048]{1,0:T(1,128)S(1)} %collective-permute-done.refs_0_.refs_2_, ...), custom_call_target="tpu_custom_call" | custom-call | flops 1000 | bytes 1000 | tf_op jit(solution)/shard_map/pallas_call | solution.py:35
  61.1 0.8 %collective-permute-done.8.refs_2_ = bf16[512,256]{1,0:T(8,128)(2,1)S(1)} collective-permute-done((bf16[512,256]{1,0:T(8,128)(2,1)S(1)}, bf16[512,256]{1,0:T(8,128)(2,1)S(1)}, u32[]{:S(2)}, u32[]{:S(2)}) %collective-permute-start.8) | collective-permute-done | bytes 262176 | tf_op jit(solution)/shard_map/ppermute | solution.py:196
  63.0 0.6 collective-permute-start.14
  64.1 1.6 %collective-permute-start.12 = (bf16[64,1152]{1,0:T(8,128)(2,1)S(1)}, bf16[64,1152]{1,0:T(8,128)(2,1)S(1)}, u32[]{:S(2)}, u32[]{:S(2)}) collective-permute-start(bf16[64,1152]{1,0:T(8,128)(2,1)S(1)} %shard_map.65.refs_0_.refs_4_), channel_id=1, source_target_pairs={{0,1},{1,0},{2,3},{3,2},{4,5},{5,4},{6,7},{7,6},{8,9},{9,8},{10,11... | collective-permute-start | bytes 442376 | tf_op jit(solution)/shard_map/ppermute | solution.py:188
  66.1 2.2 %collective-permute-start.15 = (bf16[64,1024]{1,0:T(8,128)(2,1)S(1)}, bf16[64,1024]{1,0:T(8,128)(2,1)S(1)}, u32[]{:S(2)}, u32[]{:S(2)}) collective-permute-start(bf16[64,1024]{1,0:T(8,128)(2,1)S(1)} %shard_map.69.refs_0_), channel_id=1, source_target_pairs={{0,3},{3,0},{1,2},{2,1},{4,7},{7,4},{5,6},{6,5},{8,11},{11,8},{9,1... | collective-permute-start | bytes 393224 | tf_op jit(solution)/shard_map/ppermute | solution.py:192
  68.3 1.6 %collective-permute-done.12.refs_1_ = bf16[64,1152]{1,0:T(8,128)(2,1)S(1)} collective-permute-done((bf16[64,1152]{1,0:T(8,128)(2,1)S(1)}, bf16[64,1152]{1,0:T(8,128)(2,1)S(1)}, u32[]{:S(2)}, u32[]{:S(2)}) %collective-permute-start.12) | collective-permute-done | bytes 147488 | tf_op jit(solution)/shard_map/ppermute | solution.py:188
  70.1 2.8 %collective-permute-start.13 = (bf16[64,1152]{1,0:T(8,128)(2,1)S(1)}, bf16[64,1152]{1,0:T(8,128)(2,1)S(1)}, u32[]{:S(2)}, u32[]{:S(2)}) collective-permute-start(bf16[64,1152]{1,0:T(8,128)(2,1)S(1)} %shard_map.66.refs_1_), channel_id=1, source_target_pairs={{0,3},{3,0},{1,2},{2,1},{4,7},{7,4},{5,6},{6,5},{8,11},{11,8},{9,1... | collective-permute-start | bytes 442376 | tf_op jit(solution)/shard_map/ppermute | solution.py:192
  73.2 3.2 %collective-permute-done.13.refs_2_ = bf16[64,1152]{1,0:T(8,128)(2,1)S(1)} collective-permute-done((bf16[64,1152]{1,0:T(8,128)(2,1)S(1)}, bf16[64,1152]{1,0:T(8,128)(2,1)S(1)}, u32[]{:S(2)}, u32[]{:S(2)}) %collective-permute-start.13) | collective-permute-done | bytes 147488 | tf_op jit(solution)/shard_map/ppermute | solution.py:192
  76.5 0.8 %shard_map.67 = (f32[64,1024]{1,0:T(8,128)S(1)}, bf16[64,256]{1,0:T(8,128)(2,1)}, f32[1,1024]{1,0:T(1,128)S(1)}) custom-call(s32[1,2048]{1,0:T(1,128)S(1)} %shard_map.50.refs_0_, bf16[64,1152]{1,0:T(8,128)(2,1)S(1)} %shard_map.66.refs_1_, bf16[64,1152]{1,0:T(8,128)(2,1)S(1)} %collective-permute-done.13.refs_2_, f32[64,256]{1,0:T(8,128)S(1)} %get-tuple-element.40.refs_3_), custom_call_target="tpu_custom_call" | custom-call | flops 1000 | bytes 1000 | tf_op jit(solution)/shard_map/pallas_call | solution.py:35
  77.3 0.7 collective-permute-done.16.refs_1_
  78.0 0.7 shard_map.71
  (32 shorter events, 4.3 us)
Async XLA Ops:
  0.6 0.8 %copy-start.1 = (s32[2048]{0:T(1024)S(1)}, s32[2048]{0:T(1024)}, u32[]{:S(2)}) copy-start(s32[2048]{0:T(1024)} %param.5) | copy-start | bytes 24580
  0.6 3.0 %collective-permute-start.1 = (bf16[2048,256]{1,0:T(8,128)(2,1)}, bf16[2048,256]{1,0:T(8,128)(2,1)S(1)}, u32[]{:S(2)}, u32[]{:S(2)}) collective-permute-start(bf16[2048,256]{1,0:T(8,128)(2,1)} %refs_1_.15), channel_id=1, source_target_pairs={{0,4},{4,0},{1,5},{5,1},{2,6},{6,2},{3,7},{7,3},{8,12},{12,8},{9,1... | collective-permute-start | bytes 3145736 | tf_op jit(solution)/shard_map/ppermute | solution.py:184
  1.5 1.2 %copy-start = (bf16[2048,256]{1,0:T(8,128)(2,1)S(1)}, bf16[2048,256]{1,0:T(8,128)(2,1)}, u32[]{:S(2)}) copy-start(bf16[2048,256]{1,0:T(8,128)(2,1)} %refs_1_.15) | copy-start | bytes 3145732
  1.5 1.9 %collective-permute-start = (s32[1,2048]{1,0:T(1,128)S(1)}, s32[1,2048]{1,0:T(1,128)S(1)}, u32[]{:S(2)}, u32[]{:S(2)}) collective-permute-start(s32[1,2048]{1,0:T(1,128)S(1)} %shard_map.50.refs_0_), channel_id=1, source_target_pairs={{0,4},{4,0},{1,5},{5,1},{2,6},{6,2},{3,7},{7,3},{8,12},{12,8},{9,1... | collective-permute-start | bytes 24584 | tf_op jit(solution)/shard_map/ppermute | solution.py:184
  4.3 8.1 %collective-permute-start.3 = (bf16[256,256]{1,0:T(8,128)(2,1)S(1)}, bf16[256,256]{1,0:T(8,128)(2,1)S(1)}, u32[]{:S(2)}, u32[]{:S(2)}) collective-permute-start(bf16[256,256]{1,0:T(8,128)(2,1)S(1)} %get-tuple-element.25.refs_4_), channel_id=1, source_target_pairs={{0,192},{192,0},{64,128},{128,64},{1,193},{193,1},{65,129},{129,65... | collective-permute-start | bytes 393224 | tf_op jit(solution)/shard_map/ppermute | solution.py:192
  6.0 8.1 %collective-permute-start.2 = (bf16[256,256]{1,0:T(8,128)(2,1)S(1)}, bf16[256,256]{1,0:T(8,128)(2,1)S(1)}, u32[]{:S(2)}, u32[]{:S(2)}) collective-permute-start(bf16[256,256]{1,0:T(8,128)(2,1)S(1)} %get-tuple-element.26.refs_5_), channel_id=1, source_target_pairs={{0,64},{64,0},{128,192},{192,128},{1,65},{65,1},{129,193},{193,129... | collective-permute-start | bytes 393224 | tf_op jit(solution)/shard_map/ppermute | solution.py:188
  9.1 6.9 %collective-permute-start.4 = (bf16[256,256]{1,0:T(8,128)(2,1)S(1)}, bf16[256,256]{1,0:T(8,128)(2,1)S(1)}, u32[]{:S(2)}, u32[]{:S(2)}) collective-permute-start(bf16[256,256]{1,0:T(8,128)(2,1)S(1)} %get-tuple-element.27.refs_4_), channel_id=1, source_target_pairs={{0,192},{192,0},{64,128},{128,64},{1,193},{193,1},{65,129},{129,65... | collective-permute-start | bytes 393224 | tf_op jit(solution)/shard_map/ppermute | solution.py:192
  10.5 6.0 %collective-permute-start.7 = (bf16[256,256]{1,0:T(8,128)(2,1)S(1)}, bf16[256,256]{1,0:T(8,128)(2,1)S(1)}, u32[]{:S(2)}, u32[]{:S(2)}) collective-permute-start(bf16[256,256]{1,0:T(8,128)(2,1)S(1)} %get-tuple-element.28.refs_5_), channel_id=1, source_target_pairs={{0,64},{64,0},{128,192},{192,128},{1,65},{65,1},{129,193},{193,129... | collective-permute-start | bytes 393224 | tf_op jit(solution)/shard_map/ppermute | solution.py:188
  12.4 5.9 %collective-permute-start.5 = (bf16[256,256]{1,0:T(8,128)(2,1)S(1)}, bf16[256,256]{1,0:T(8,128)(2,1)S(1)}, u32[]{:S(2)}, u32[]{:S(2)}) collective-permute-start(bf16[256,256]{1,0:T(8,128)(2,1)S(1)} %shard_map.56.refs_5_), channel_id=1, source_target_pairs={{0,64},{64,0},{128,192},{192,128},{1,65},{65,1},{129,193},{193,129... | collective-permute-start | bytes 393224 | tf_op jit(solution)/shard_map/ppermute | solution.py:188
  14.1 5.1 %collective-permute-start.6 = (bf16[256,256]{1,0:T(8,128)(2,1)S(1)}, bf16[256,256]{1,0:T(8,128)(2,1)S(1)}, u32[]{:S(2)}, u32[]{:S(2)}) collective-permute-start(bf16[256,256]{1,0:T(8,128)(2,1)S(1)} %shard_map.55.refs_4_), channel_id=1, source_target_pairs={{0,192},{192,0},{64,128},{128,64},{1,193},{193,1},{65,129},{129,65... | collective-permute-start | bytes 393224 | tf_op jit(solution)/shard_map/ppermute | solution.py:192
  49.8 8.9 %collective-permute-start.10 = (bf16[512,256]{1,0:T(8,128)(2,1)S(1)}, bf16[512,256]{1,0:T(8,128)(2,1)S(1)}, u32[]{:S(2)}, u32[]{:S(2)}) collective-permute-start(bf16[512,256]{1,0:T(8,128)(2,1)S(1)} %bitcast.7), channel_id=1, source_target_pairs={{0,192},{192,0},{64,128},{128,64},{1,193},{193,1},{65,129},{129,65... | collective-permute-start | bytes 786440 | tf_op jit(solution)/shard_map/ppermute | solution.py:192
  51.7 6.9 %collective-permute-start.9 = (bf16[512,256]{1,0:T(8,128)(2,1)S(1)}, bf16[512,256]{1,0:T(8,128)(2,1)S(1)}, u32[]{:S(2)}, u32[]{:S(2)}) collective-permute-start(bf16[512,256]{1,0:T(8,128)(2,1)S(1)} %bitcast.8), channel_id=1, source_target_pairs={{0,64},{64,0},{128,192},{192,128},{1,65},{65,1},{129,193},{193,129... | collective-permute-start | bytes 786440 | tf_op jit(solution)/shard_map/ppermute | solution.py:188
  54.0 7.9 %collective-permute-start.8 = (bf16[512,256]{1,0:T(8,128)(2,1)S(1)}, bf16[512,256]{1,0:T(8,128)(2,1)S(1)}, u32[]{:S(2)}, u32[]{:S(2)}) collective-permute-start(bf16[512,256]{1,0:T(8,128)(2,1)S(1)} %bitcast.9), channel_id=1, source_target_pairs={{0,128},{64,192},{128,0},{192,64},{1,129},{65,193},{129,1},{193,65... | collective-permute-start | bytes 786440 | tf_op jit(solution)/shard_map/ppermute | solution.py:196
  62.4 1.6 %collective-permute-start.11 = (bf16[64,1152]{1,0:T(8,128)(2,1)S(1)}, bf16[64,1152]{1,0:T(8,128)(2,1)S(1)}, u32[]{:S(2)}, u32[]{:S(2)}) collective-permute-start(bf16[64,1152]{1,0:T(8,128)(2,1)S(1)} %shard_map.62.refs_4_.refs_1_), channel_id=1, source_target_pairs={{0,4},{4,0},{1,5},{5,1},{2,6},{6,2},{3,7},{7,3},{8,12},{12,8},{9,1... | collective-permute-start | bytes 442376 | tf_op jit(solution)/shard_map/ppermute | solution.py:184
  63.0 3.1 %collective-permute-start.14 = (bf16[64,1024]{1,0:T(8,128)(2,1)S(1)}, bf16[64,1024]{1,0:T(8,128)(2,1)S(1)}, u32[]{:S(2)}, u32[]{:S(2)}) collective-permute-start(bf16[64,1024]{1,0:T(8,128)(2,1)S(1)} %shard_map.63.refs_4_.refs_1_), channel_id=1, source_target_pairs={{0,4},{4,0},{1,5},{5,1},{2,6},{6,2},{3,7},{7,3},{8,12},{12,8},{9,1... | collective-permute-start | bytes 393224 | tf_op jit(solution)/shard_map/ppermute | solution.py:184
  64.1 5.9 %collective-permute-start.12 = (bf16[64,1152]{1,0:T(8,128)(2,1)S(1)}, bf16[64,1152]{1,0:T(8,128)(2,1)S(1)}, u32[]{:S(2)}, u32[]{:S(2)}) collective-permute-start(bf16[64,1152]{1,0:T(8,128)(2,1)S(1)} %shard_map.65.refs_0_.refs_4_), channel_id=1, source_target_pairs={{0,1},{1,0},{2,3},{3,2},{4,5},{5,4},{6,7},{7,6},{8,9},{9,8},{10,11... | collective-permute-start | bytes 442376 | tf_op jit(solution)/shard_map/ppermute | solution.py:188
  66.1 6.8 %collective-permute-start.15 = (bf16[64,1024]{1,0:T(8,128)(2,1)S(1)}, bf16[64,1024]{1,0:T(8,128)(2,1)S(1)}, u32[]{:S(2)}, u32[]{:S(2)}) collective-permute-start(bf16[64,1024]{1,0:T(8,128)(2,1)S(1)} %shard_map.69.refs_0_), channel_id=1, source_target_pairs={{0,3},{3,0},{1,2},{2,1},{4,7},{7,4},{5,6},{6,5},{8,11},{11,8},{9,1... | collective-permute-start | bytes 393224 | tf_op jit(solution)/shard_map/ppermute | solution.py:192
  70.1 6.4 %collective-permute-start.13 = (bf16[64,1152]{1,0:T(8,128)(2,1)S(1)}, bf16[64,1152]{1,0:T(8,128)(2,1)S(1)}, u32[]{:S(2)}, u32[]{:S(2)}) collective-permute-start(bf16[64,1152]{1,0:T(8,128)(2,1)S(1)} %shard_map.66.refs_1_), channel_id=1, source_target_pairs={{0,3},{3,0},{1,2},{2,1},{4,7},{7,4},{5,6},{6,5},{8,11},{11,8},{9,1... | collective-permute-start | bytes 442376 | tf_op jit(solution)/shard_map/ppermute | solution.py:192
  72.9 5.1 %collective-permute-start.16 = (bf16[64,1024]{1,0:T(8,128)(2,1)S(1)}, bf16[64,1024]{1,0:T(8,128)(2,1)S(1)}, u32[]{:S(2)}, u32[]{:S(2)}) collective-permute-start(bf16[64,1024]{1,0:T(8,128)(2,1)S(1)} %shard_map.70.refs_0_), channel_id=1, source_target_pairs={{0,1},{1,0},{2,3},{3,2},{4,5},{5,4},{6,7},{7,6},{8,9},{9,8},{10,11... | collective-permute-start | bytes 393224 | tf_op jit(solution)/shard_map/ppermute | solution.py:188
